TPU v7x, 128 devices: a whole 4x4x4 slice. The times are simulated.
128 devices in a mesh: src: 16 (over z_hi, y, core), rcv: 8 (over z_lo, x).
Axes of the slice: x: 4, y: 4, z: 4 (z_hi: 2, z_lo: 2; z = z_hi * 2 + z_lo), core: 2. Of those that a mesh axis runs over, the one named last changes fastest.
Arguments:
- spectra: bfloat16 [2048, 2, 10, 400], P(('src', 'rcv')), may hold values from -6 to 6
- offsets: int32 [2048, 10], P(('src', 'rcv')), may hold values from 0 to 399
- channel_mask: int32 [2048], P(('src', 'rcv')), may hold values 0 or 1
Outputs:
- correlations: bfloat16 [101, 2048, 2048], P(None, 'src', 'rcv')
All inputs are finite; a program needn't handle non-finite values. No bound on the sum of `channel_mask` on one device may be relied on, other than what follows from the above.
Results may differ from a plain program's by a relative error of at most 0.0058.
Values may be sent and summed in bfloat16 or wider, within the bound.
No kernel may reach another device: no remote copies, remote signals or barrier semaphores. Data moves between devices by JAX's collectives and lax.ppermute only.
A program may use at most 128 MiB of HBM per device.

v0:
```python
import math

import jax
import jax.numpy as jnp
from jax import lax
from jax.sharding import PartitionSpec as P

W = 10
F = 400
KLO = 6
NT = 12000
HALF = 50


def from_root(shard, axis, root):
    mine = lax.axis_index(axis) == root
    return lax.psum(jnp.where(mine, shard, jnp.zeros_like(shard)), axis)


def block_width(total):
    width = 1
    for trial in range(1, 41):
        if total % trial == 0:
            width = trial
    return width


def prepare(spectra, offsets, channel_mask):
    values = spectra.astype(jnp.float32)
    real_part = values[:, 0]
    imag_part = values[:, 1]
    power = jnp.mean(real_part * real_part + imag_part * imag_part, axis=-1, keepdims=True)
    scale = lax.rsqrt(power + 1e-06) * channel_mask.astype(jnp.float32)[:, None, None]
    freq = KLO + jnp.arange(F, dtype=jnp.int32)
    turns = offsets[:, :, None] * freq[None, None, :] % NT
    angle = 2.0 * math.pi / NT * turns.astype(jnp.float32)
    cosine = jnp.cos(angle)
    sine = jnp.sin(angle)
    rot_real = (real_part * cosine + imag_part * sine) * scale
    rot_imag = (imag_part * cosine - real_part * sine) * scale
    return jnp.stack([rot_real, rot_imag], 1).astype(jnp.bfloat16)


def lag_table():
    freq = KLO + jnp.arange(F, dtype=jnp.int32)
    shifts = jnp.arange(2 * HALF + 1, dtype=jnp.int32) - HALF
    turns = shifts[:, None] * freq[None, :] % NT
    angle = 2.0 * math.pi / NT * turns.astype(jnp.float32)
    return jnp.stack([jnp.cos(angle), -jnp.sin(angle)], -1).astype(jnp.bfloat16)


def correlate(rows, cols):
    row_count = rows.shape[0]
    col_count = cols.shape[0]
    lag_count = 2 * HALF + 1
    width = block_width(F)
    table = lag_table()
    flipped = jnp.stack([cols, jnp.stack([-cols[:, 1], cols[:, 0]], 1)], 1)

    def advance(total, block_index):
        start = block_index * width
        left = lax.dynamic_slice_in_dim(rows, start, width, 3)
        right = lax.dynamic_slice_in_dim(flipped, start, width, 4)
        weights = lax.dynamic_slice_in_dim(table, start, width, 1)
        cross = jnp.einsum(
            "icwf,jkcwf->fkij", left, right, preferred_element_type=jnp.float32
        ).astype(jnp.bfloat16)
        total = total + jnp.dot(
            weights.reshape(lag_count, width * 2),
            cross.reshape(width * 2, row_count * col_count),
            preferred_element_type=jnp.float32,
        )
        return (total, None)

    start_total = jnp.zeros((lag_count, row_count * col_count), jnp.float32)
    total = lax.scan(advance, start_total, jnp.arange(F // width, dtype=jnp.int32))[0]
    total = total * (1.0 / math.sqrt(W * F))
    return total.reshape(lag_count, row_count, col_count).astype(jnp.bfloat16)


def body(spectra, offsets, channel_mask):
    white = prepare(spectra, offsets, channel_mask)
    rows = lax.all_gather(white, "rcv", axis=0, tiled=True)
    ratio = lax.axis_size("src") // lax.axis_size("rcv")
    column = lax.axis_index("rcv")
    panel_rows = rows.shape[0]
    columns = jnp.zeros((ratio * panel_rows,) + rows.shape[1:], jnp.bfloat16)
    for turn in range(ratio):
        slot = column * 0 + turn
        piece = from_root(rows, "src", column * ratio + slot)
        columns = lax.dynamic_update_slice_in_dim(columns, piece, slot * panel_rows, 0)
    return correlate(rows, columns)


def solution(mesh):
    in_specs = (P(("src", "rcv"), None, None, None), P(("src", "rcv"), None), P(("src", "rcv")))
    out_specs = P(None, "src", "rcv")
    return jax.shard_map(body, mesh=mesh, in_specs=in_specs, out_specs=out_specs, check_vma=False)
```

profile of v0, /device:TPU:1, one launch (start us, length us, event | category | flops | bytes accessed | tf_op | source)
XLA Modules:
  0.0 601.6 jit_solution(11725296294001790456)
XLA Ops:
  8.0 1.1 copy_convert_fusion
  9.2 1.6 multiply_convert_fusion.2
  10.9 1.1 copy.20
  12.0 42.4 %all-gather.2.cloned.1.call-done = bf16[128,2,10,400]{3,1,2,0:T(2,128)(2,1)} async-done(((bf16[16,2,10,400]{3,1,2,0:T(2,128)(2,1)}), bf16[128,2,10,400]{3,1,2,0:T(2,128)(2,1)}) %all-gather.2.cloned.1.call-update) | async-done | bytes 2048016 | tf_op jit(solution)/shard_map/all_gather | solution.py:83
  54.4 8.1 %broadcast_select_fusion = (bf16[128,2,10,400]{3,1,2,0:T(2,128)(2,1)}, bf16[128,2,10,400]{3,1,2,0:T(2,128)(2,1)}) fusion(bf16[128,2,10,400]{3,1,2,0:T(2,128)(2,1)} %all-gather.2.cloned.1.call-done, pred[]{:T(512)S(6)} %eq.11, pred[]{:T(512)S(6)} %eq.10), kind=kLoop, calls=%fused_computation.12 | loop fusion | flops 2048000 | bytes 6144002 | tf_op jit(solution)/shard_map/jit(_where)/select_n | solution.py:17
  62.6 1.2 cosine_convert_fusion
  63.9 8.2 %copy.23 = bf16[128,2,10,400]{0,2,1,3:T(8,128)(2,1)} copy(bf16[128,2,10,400]{3,1,2,0:T(2,128)(2,1)S(1)} %copy-done) | data formatting | bytes 4096000
  72.1 146.6 %all-reduce.3.cloned.1.call-done = (bf16[128,2,10,400]{3,1,2,0:T(2,128)(2,1)}, bf16[128,2,10,400]{3,1,2,0:T(2,128)(2,1)}) async-done(((bf16[128,2,10,400]{3,1,2,0:T(2,128)(2,1)}, bf16[128,2,10,400]{3,1,2,0:T(2,128)(2,1)}), (bf16[128,2,10,400]{3,1,2,0:T(2,128)(2,1)}, bf16[128,2,10,400]{3,1,2,0:T(2,128)(2,1)})) %all-reduce.3.cloned.1.call-update) | async-done | bytes 4096016 | tf_op jit(solution)/shard_map/psum | solution.py:17
  218.7 3.7 constant_dynamic-update-slice_fusion.1
  222.4 2.0 constant_dynamic-update-slice_fusion
  224.4 11.7 %slice_negate_fusion = (bf16[256,1,10,400]{3,1,2,0:T(2,128)(2,1)S(1)}, bf16[256,1,10,400]{3,1,2,0:T(2,128)(2,1)S(1)}) fusion(bf16[256,2,10,400]{3,1,2,0:T(2,128)(2,1)S(1)} %constant_dynamic-update-slice_fusion), kind=kLoop, calls=%fused_computation.10 | loop fusion | flops 1024000 | bytes 8192000 | tf_op jit(solution)/shard_map/neg | solution.py:58
  236.1 12.6 %maximum_bitcast_fusion = bf16[256,1,2,10,400]{4,2,3,0,1:T(2,128)(2,1)S(1)} fusion(bf16[256,1,10,400]{3,1,2,0:T(2,128)(2,1)S(1)} %get-tuple-element.98, bf16[256,1,10,400]{3,1,2,0:T(2,128)(2,1)S(1)} %get-tuple-element.97), kind=kLoop, calls=%fused_computation.11 | loop fusion | flops 8192000 | bytes 8192000 | tf_op jit(solution)/shard_map/stack | solution.py:58
  248.7 17.0 %pad_maximum_fusion = bf16[256,2,2,10,400]{4,2,3,0,1:T(2,128)(2,1)} fusion(bf16[256,1,2,10,400]{4,2,3,0,1:T(2,128)(2,1)S(1)} %maximum_bitcast_fusion, bf16[256,1,2,10,400]{4,2,3,0,1:T(2,128)(2,1)S(1)} %bitcast.46), kind=kLoop, calls=%fused_computation.9 | loop fusion | flops 4096000 | bytes 16384000 | tf_op jit(solution)/shard_map/stack | solution.py:58
  265.7 30.3 %copy.22 = bf16[256,2,2,10,400]{0,3,2,1,4:T(8,128)(2,1)} copy(bf16[256,2,2,10,400]{4,2,3,0,1:T(2,128)(2,1)} %pad_maximum_fusion) | data formatting | bytes 16384000
  296.0 281.4 %while.11 = (s32[]{:T(128)}, f32[101,32768]{1,0:T(8,128)}, s32[10]{0:T(128)S(1)}, bf16[101,400,2]{0,1,2:T(8,128)(2,1)S(1)}, bf16[256,2,2,10,400]{0,3,2,1,4:T(8,1...) while((s32[]{:T(128)}, f32[101,32768]{1,0:T(8,128)}, ...), condition=%wide.region_4.5_spmd.clone, body=%wide.region_3.4_spmd.clone.sunk | while | flops 643629056 | bytes 49168468 | solution.py:76
  297.3 5.3 fusion.28
  302.6 8.6 %copy.34 = bf16[10,8,128,256]{3,1,2,0:T(8,128)(2,1)} copy(bf16[10,8,128,256]{2,3,1,0:T(8,128)(2,1)} %bitcast.45) | data formatting | bytes 10485760 | tf_op jit(solution)/shard_map/while
  311.2 9.3 %convolution_add_fusion.2 = f32[101,32768]{1,0:T(8,128)} fusion(bf16[101,80]{0,1:T(8,128)(2,1)S(1)} %bitcast.49, bf16[80,32768]{1,0:T(8,128)(2,1)} %bitcast.44, f32[101,32768]{1,0:T(8,128)} %get-tuple-element.153, pred[]{:T(512)S(6)} %compare.3), kind=kOutput, calls=%fused_computation.clone.1 | convolution fusion | flops 536150016 | bytes 31735584 | tf_op jit(solution)/shard_map/while/body/eval_jaxpr/dot_general | solution.py:68
  321.9 5.3 fusion.28
  327.2 8.6 %copy.34 = bf16[10,8,128,256]{3,1,2,0:T(8,128)(2,1)} copy(bf16[10,8,128,256]{2,3,1,0:T(8,128)(2,1)} %bitcast.45) | data formatting | bytes 10485760 | tf_op jit(solution)/shard_map/while
  335.8 13.3 %convolution_add_fusion.2 = f32[101,32768]{1,0:T(8,128)} fusion(bf16[101,80]{0,1:T(8,128)(2,1)S(1)} %bitcast.49, bf16[80,32768]{1,0:T(8,128)(2,1)} %bitcast.44, f32[101,32768]{1,0:T(8,128)} %get-tuple-element.153, pred[]{:T(512)S(6)} %compare.3), kind=kOutput, calls=%fused_computation.clone.1 | convolution fusion | flops 536150016 | bytes 31735584 | tf_op jit(solution)/shard_map/while/body/eval_jaxpr/dot_general | solution.py:68
  350.4 5.3 fusion.28
  355.7 8.6 %copy.34 = bf16[10,8,128,256]{3,1,2,0:T(8,128)(2,1)} copy(bf16[10,8,128,256]{2,3,1,0:T(8,128)(2,1)} %bitcast.45) | data formatting | bytes 10485760 | tf_op jit(solution)/shard_map/while
  364.4 13.3 %convolution_add_fusion.2 = f32[101,32768]{1,0:T(8,128)} fusion(bf16[101,80]{0,1:T(8,128)(2,1)S(1)} %bitcast.49, bf16[80,32768]{1,0:T(8,128)(2,1)} %bitcast.44, f32[101,32768]{1,0:T(8,128)} %get-tuple-element.153, pred[]{:T(512)S(6)} %compare.3), kind=kOutput, calls=%fused_computation.clone.1 | convolution fusion | flops 536150016 | bytes 31735584 | tf_op jit(solution)/shard_map/while/body/eval_jaxpr/dot_general | solution.py:68
  378.9 5.3 fusion.28
  384.3 8.6 %copy.34 = bf16[10,8,128,256]{3,1,2,0:T(8,128)(2,1)} copy(bf16[10,8,128,256]{2,3,1,0:T(8,128)(2,1)} %bitcast.45) | data formatting | bytes 10485760 | tf_op jit(solution)/shard_map/while
  392.9 13.3 %convolution_add_fusion.2 = f32[101,32768]{1,0:T(8,128)} fusion(bf16[101,80]{0,1:T(8,128)(2,1)S(1)} %bitcast.49, bf16[80,32768]{1,0:T(8,128)(2,1)} %bitcast.44, f32[101,32768]{1,0:T(8,128)} %get-tuple-element.153, pred[]{:T(512)S(6)} %compare.3), kind=kOutput, calls=%fused_computation.clone.1 | convolution fusion | flops 536150016 | bytes 31735584 | tf_op jit(solution)/shard_map/while/body/eval_jaxpr/dot_general | solution.py:68
  407.5 5.3 fusion.28
  412.8 8.6 %copy.34 = bf16[10,8,128,256]{3,1,2,0:T(8,128)(2,1)} copy(bf16[10,8,128,256]{2,3,1,0:T(8,128)(2,1)} %bitcast.45) | data formatting | bytes 10485760 | tf_op jit(solution)/shard_map/while
  421.4 13.3 %convolution_add_fusion.2 = f32[101,32768]{1,0:T(8,128)} fusion(bf16[101,80]{0,1:T(8,128)(2,1)S(1)} %bitcast.49, bf16[80,32768]{1,0:T(8,128)(2,1)} %bitcast.44, f32[101,32768]{1,0:T(8,128)} %get-tuple-element.153, pred[]{:T(512)S(6)} %compare.3), kind=kOutput, calls=%fused_computation.clone.1 | convolution fusion | flops 536150016 | bytes 31735584 | tf_op jit(solution)/shard_map/while/body/eval_jaxpr/dot_general | solution.py:68
  436.0 5.3 fusion.28
  441.3 8.6 %copy.34 = bf16[10,8,128,256]{3,1,2,0:T(8,128)(2,1)} copy(bf16[10,8,128,256]{2,3,1,0:T(8,128)(2,1)} %bitcast.45) | data formatting | bytes 10485760 | tf_op jit(solution)/shard_map/while
  450.0 13.3 %convolution_add_fusion.2 = f32[101,32768]{1,0:T(8,128)} fusion(bf16[101,80]{0,1:T(8,128)(2,1)S(1)} %bitcast.49, bf16[80,32768]{1,0:T(8,128)(2,1)} %bitcast.44, f32[101,32768]{1,0:T(8,128)} %get-tuple-element.153, pred[]{:T(512)S(6)} %compare.3), kind=kOutput, calls=%fused_computation.clone.1 | convolution fusion | flops 536150016 | bytes 31735584 | tf_op jit(solution)/shard_map/while/body/eval_jaxpr/dot_general | solution.py:68
  464.5 5.3 fusion.28
  469.9 8.6 %copy.34 = bf16[10,8,128,256]{3,1,2,0:T(8,128)(2,1)} copy(bf16[10,8,128,256]{2,3,1,0:T(8,128)(2,1)} %bitcast.45) | data formatting | bytes 10485760 | tf_op jit(solution)/shard_map/while
  478.5 13.3 %convolution_add_fusion.2 = f32[101,32768]{1,0:T(8,128)} fusion(bf16[101,80]{0,1:T(8,128)(2,1)S(1)} %bitcast.49, bf16[80,32768]{1,0:T(8,128)(2,1)} %bitcast.44, f32[101,32768]{1,0:T(8,128)} %get-tuple-element.153, pred[]{:T(512)S(6)} %compare.3), kind=kOutput, calls=%fused_computation.clone.1 | convolution fusion | flops 536150016 | bytes 31735584 | tf_op jit(solution)/shard_map/while/body/eval_jaxpr/dot_general | solution.py:68
  493.1 5.3 fusion.28
  498.4 8.6 %copy.34 = bf16[10,8,128,256]{3,1,2,0:T(8,128)(2,1)} copy(bf16[10,8,128,256]{2,3,1,0:T(8,128)(2,1)} %bitcast.45) | data formatting | bytes 10485760 | tf_op jit(solution)/shard_map/while
  507.0 13.3 %convolution_add_fusion.2 = f32[101,32768]{1,0:T(8,128)} fusion(bf16[101,80]{0,1:T(8,128)(2,1)S(1)} %bitcast.49, bf16[80,32768]{1,0:T(8,128)(2,1)} %bitcast.44, f32[101,32768]{1,0:T(8,128)} %get-tuple-element.153, pred[]{:T(512)S(6)} %compare.3), kind=kOutput, calls=%fused_computation.clone.1 | convolution fusion | flops 536150016 | bytes 31735584 | tf_op jit(solution)/shard_map/while/body/eval_jaxpr/dot_general | solution.py:68
  521.6 5.3 fusion.28
  527.0 8.6 %copy.34 = bf16[10,8,128,256]{3,1,2,0:T(8,128)(2,1)} copy(bf16[10,8,128,256]{2,3,1,0:T(8,128)(2,1)} %bitcast.45) | data formatting | bytes 10485760 | tf_op jit(solution)/shard_map/while
  535.6 13.3 %convolution_add_fusion.2 = f32[101,32768]{1,0:T(8,128)} fusion(bf16[101,80]{0,1:T(8,128)(2,1)S(1)} %bitcast.49, bf16[80,32768]{1,0:T(8,128)(2,1)} %bitcast.44, f32[101,32768]{1,0:T(8,128)} %get-tuple-element.153, pred[]{:T(512)S(6)} %compare.3), kind=kOutput, calls=%fused_computation.clone.1 | convolution fusion | flops 536150016 | bytes 31735584 | tf_op jit(solution)/shard_map/while/body/eval_jaxpr/dot_general | solution.py:68
  550.1 5.3 fusion.28
  555.5 8.6 %copy.34 = bf16[10,8,128,256]{3,1,2,0:T(8,128)(2,1)} copy(bf16[10,8,128,256]{2,3,1,0:T(8,128)(2,1)} %bitcast.45) | data formatting | bytes 10485760 | tf_op jit(solution)/shard_map/while
  564.1 13.3 %convolution_add_fusion.2 = f32[101,32768]{1,0:T(8,128)} fusion(bf16[101,80]{0,1:T(8,128)(2,1)S(1)} %bitcast.49, bf16[80,32768]{1,0:T(8,128)(2,1)} %bitcast.44, f32[101,32768]{1,0:T(8,128)} %get-tuple-element.153, pred[]{:T(512)S(6)} %compare.3), kind=kOutput, calls=%fused_computation.clone.1 | convolution fusion | flops 536150016 | bytes 31735584 | tf_op jit(solution)/shard_map/while/body/eval_jaxpr/dot_general | solution.py:68
  577.4 8.7 %multiply_convert_fusion = bf16[101,32768]{1,0:T(8,128)(2,1)} fusion(f32[101,32768]{1,0:T(8,128)} %get-tuple-element.37), kind=kLoop, calls=%fused_computation.8 | loop fusion | flops 6619136 | bytes 19857408 | tf_op jit(solution)/shard_map/convert_element_type | solution.py:78
  586.2 5.0 copy.28
  591.1 3.6 slice.20
  (48 shorter events, 7.8 us)
Async XLA Ops:
  6.5 47.9 %all-gather.2.cloned.1.call-start = ((), (), s32[]{:S(2)}) async-start(), calls=%async_computation | async-start | bytes 2949120 | tf_op jit(solution)/shard_map/all_gather | solution.py:83
  12.0 206.8 %all-reduce.3.cloned.1.call-start = ((), (), s32[]{:S(2)}) async-start(), calls=%async_computation.1 | async-start | bytes 10485760 | tf_op jit(solution)/shard_map/psum | solution.py:17
  54.4 9.5 %copy-start = (bf16[128,2,10,400]{3,1,2,0:T(2,128)(2,1)S(1)}, bf16[128,2,10,400]{3,1,2,0:T(2,128)(2,1)}, u32[]{:S(2)}) copy-start(bf16[128,2,10,400]{3,1,2,0:T(2,128)(2,1)} %all-gather.2.cloned.1.call-done) | copy-start | bytes 6144004
  218.7 3.7 copy-start.1
Sparse Core Ops, SparseCore 0:
  12.1 42.3 all-gather.1
  62.7 155.9 all-reduce.2
where the time goes:
time: 605 us; the launch traced here: 602 us
  waiting for transfers between devices  189 us (31%)
  matrix products  182 us (30%)
  local copies, waits for them, and re-layouts  147 us (24%)
  other arithmetic  63 us (10%)
  between operations  13.5 us (2%)
  loops' own time  6.75 us (1%)
    psum x1, waiting for transfers between devices, from_root(): return lax.psum(jnp.where(mine, shard, jnp.zeros_like(shard)), axis)  147 us
    dot_general x10, matrix products, advance(): jnp.dot(weights.reshape(lag_count, width * 2), cross.reshape(width * 2, r...  129 us
    while x10, local copies, waits for them, and re-layouts  86.2 us
    dot_general x10, matrix products, advance(): jnp.einsum('icwf,jkcwf->fkij', left, right, preferred_element_type=jnp.fl...  53.3 us
    unnamed x9, local copies, waits for them, and re-layouts  48 us
    all_gather x1, waiting for transfers between devices, body(): rows = lax.all_gather(white, 'rcv', axis=0, tiled=True)  42.4 us
    another operation x2, other arithmetic, correlate(): flipped = jnp.stack([cols, jnp.stack([-cols[:, 1], cols[:, 0]], 1)], 1)  29.6 us
  transfers between devices with their start and end apart: 2, of which 2 were waited for; matrix products, arithmetic and copies ran while one was open for 2% of the time, Pallas kernels for 0%

commit v1 on v0

v1 whole, which is shorter than its diff:
```python
import functools
import math

import jax
import jax.numpy as jnp
import numpy as np
from jax import lax
from jax.experimental import pallas as pl
from jax.experimental.pallas import tpu as pltpu
from jax.sharding import PartitionSpec as P

W = 10
F = 400
KLO = 6
NT = 12000
HALF = 50
LAGS = 2 * HALF + 1
LAG_ROWS = 104
FB = 8
NB = F // FB
OWN = 16
MAIN = 16
TILES = NB + -(-NB // 4)
LANES = TILES * 128
GROUP = 32


def unit_circle(turns):
    turns = turns - NT * jnp.floor(turns * (1.0 / NT))
    quarter = jnp.floor(turns * (4.0 / NT) + 0.5)
    a = (turns - (NT // 4) * quarter) * (2.0 * math.pi / NT)
    s = a * a
    sin = a + a * s * (-1 / 6 + s * (1 / 120 + s * (-1 / 5040 + s * (1 / 362880))))
    cos = 1.0 + s * (-0.5 + s * (1 / 24 + s * (-1 / 720 + s * (1 / 40320 + s * (-1 / 3628800)))))
    swap = (quarter == 1.0) | (quarter == 3.0)
    c = jnp.where(swap, sin, cos)
    s = jnp.where(swap, cos, sin)
    c = jnp.where((quarter == 1.0) | (quarter == 2.0), -c, c)
    s = jnp.where((quarter == 2.0) | (quarter == 3.0), -s, s)
    return c, s


def whiten_kernel(mask_ref, spectra_ref, offsets_ref, white_ref, parts):
    freq = (KLO + lax.broadcasted_iota(jnp.int32, (W, F), 1)).astype(jnp.float32)
    eye = lax.broadcasted_iota(jnp.int32, (W, W), 0) == lax.broadcasted_iota(jnp.int32, (W, W), 1)
    parts[3] = jnp.zeros((OWN * 32, 128), jnp.float32)
    for ch in range(OWN):
        re = spectra_ref[ch, 0].astype(jnp.float32)
        im = spectra_ref[ch, 1].astype(jnp.float32)
        power = jnp.sum(re * re + im * im, axis=1, keepdims=True) * (1.0 / F)
        scale = lax.rsqrt(power + 1e-06) * mask_ref[ch].astype(jnp.float32)
        row = jnp.broadcast_to(offsets_ref[ch : ch + 1].astype(jnp.float32), (W, W))
        offset = jnp.sum(jnp.where(eye, row, 0.0), axis=1, keepdims=True)
        c, s = unit_circle(offset * freq)
        out = ((re * c + im * s) * scale, (im * c - re * s) * scale)
        for part in range(2):
            for t in range(4):
                n = min(128, F - 128 * t)
                parts[t, ch * 32 + part * 16 : ch * 32 + part * 16 + W, :n] = out[part][:, 128 * t : 128 * t + n]

    chunk = lax.broadcasted_iota(jnp.int32, (OWN, 128), 1) // 8
    for t in range(4):
        pairs = [parts[t, pl.ds(16 * (m % 2) + m // 2, OWN, stride=32), :] for m in range(2 * W)]
        main, rest = pairs[:MAIN], pairs[MAIN:]
        for values, low, bits in ((main, 0, 4), (rest, 2, 2)):
            for bit in range(bits):
                shift = 8 << (low + bit)
                upper = (chunk >> (low + bit)) % 2 == 1
                for m in range(len(values)):
                    if not m >> bit & 1:
                        a, b = values[m], values[m | 1 << bit]
                        values[m] = jnp.where(upper, pltpu.roll(b, shift, 1), a)
                        values[m | 1 << bit] = jnp.where(upper, b, pltpu.roll(a, 128 - shift, 1))
        for k in range(16):
            if 16 * t + k < NB:
                white_ref[:, (16 * t + k) * 128 : (16 * t + k + 1) * 128] = main[k].astype(jnp.bfloat16)
        for k in range(4):
            tile = NB + 4 * t + k
            if tile < TILES:
                white_ref[:, tile * 128 : (tile + 1) * 128] = rest[k].astype(jnp.bfloat16)


def whiten(spectra, offsets, channel_mask):
    return pl.pallas_call(
        whiten_kernel,
        in_specs=[
            pl.BlockSpec(memory_space=pltpu.SMEM),
            pl.BlockSpec(memory_space=pltpu.VMEM),
            pl.BlockSpec(memory_space=pltpu.VMEM),
        ],
        out_specs=pl.BlockSpec(memory_space=pltpu.VMEM),
        out_shape=jax.ShapeDtypeStruct((OWN, LANES), jnp.bfloat16),
        scratch_shapes=[pltpu.VMEM((4, OWN * 32, 128), jnp.float32)],
    )(channel_mask, spectra, offsets)


def lag_table():
    freq = KLO + np.arange(F)
    shifts = np.arange(LAGS) - HALF
    angle = 2.0 * math.pi / NT * ((shifts[:, None] * freq[None, :]) % NT)
    table = np.stack([np.cos(angle), -np.sin(angle)], 1).reshape(LAGS, 2, NB, FB)
    table = table.transpose(0, 2, 1, 3).reshape(LAGS, 2 * F)
    return np.pad(table, ((0, LAG_ROWS - LAGS), (0, 0)))


def correlate_kernel(n_rows, n_cols, place_ref, *refs):
    row_refs, refs = refs[:n_rows], refs[n_rows:]
    col_refs, refs = refs[:n_cols], refs[n_cols:]
    table_ref, out_ref, cols, cols_t, rows, turned, cross, lagged = refs
    step = pl.program_id(0)
    lane = lax.broadcasted_iota(jnp.int32, (8, 128), 1)
    same_bin = (lane % 8) == lax.broadcasted_iota(jnp.int32, (8, 128), 0)

    @pl.when(step == 0)
    def _():
        for k, ref in enumerate(col_refs):
            cols[pl.ds(pl.multiple_of(place_ref[n_rows + k] * OWN, OWN), OWN), :] = ref[...]

        def turn(values, shift):
            odd = (lax.broadcasted_iota(jnp.int32, values.shape, 1) // shift) % 2 == 1
            return jnp.where(odd, -pltpu.roll(values, shift, 1), pltpu.roll(values, 128 - shift, 1))

        for k, ref in enumerate(row_refs):
            at = pl.ds(pl.multiple_of(place_ref[k] * OWN, OWN), OWN)

            @pl.loop(0, NB)
            def _(t):
                o = pl.ds(pl.multiple_of(t * 128, 128), 128)
                r = ref[:, o].astype(jnp.float32)
                rows[at, o] = r
                turned[at, o] = turn(r, 8)

            @pl.loop(NB, TILES)
            def _(t):
                o = pl.ds(pl.multiple_of(t * 128, 128), 128)
                r = ref[:, o].astype(jnp.float32)
                rows[at, o] = r
                turned[at, o] = turn(r, 32)

        @pl.loop(0, TILES)
        def _(t):
            o = pl.ds(pl.multiple_of(t * 128, 128), 128)
            cols_t[o, :] = cols[:, o].T

    base = pl.multiple_of(step * GROUP, GROUP)

    @pl.loop(0, NB)
    def _(b):
        mo = pl.ds(pl.multiple_of(b * 128, 128), 128)
        ro = pl.ds(pl.multiple_of((NB + b // 4) * 128, 128), 128)
        right = jnp.concatenate([cols_t[mo, :], cols_t[ro, :]], 0)
        same_rest = same_bin & ((lane // 8) % 4 == b % 4)
        for g in range(GROUP // 8):
            at = pl.ds(pl.multiple_of(base + g * 8, 8), 8)
            loaded = [rows[at, mo], turned[at, mo], rows[at, ro], turned[at, ro]]
            left = []
            for u in range(8):
                v = [jnp.broadcast_to(x[u : u + 1], (8, 128)) for x in loaded]
                m = jnp.concatenate([jnp.where(same_bin, v[0], 0.0), jnp.where(same_bin, v[1], 0.0)], 0)
                r = jnp.concatenate([jnp.where(same_rest, v[2], 0.0), jnp.where(same_rest, v[3], 0.0)], 0)
                left.append(jnp.concatenate([m.astype(jnp.bfloat16), r.astype(jnp.bfloat16)], 1))
            product = jnp.dot(jnp.concatenate(left, 0), right, preferred_element_type=jnp.float32)
            product = product.astype(jnp.bfloat16)
            for u in range(8):
                cross[g * 8 + u, pl.ds(pl.multiple_of(b * 16, 16), 16), :] = product[u * 16 : u * 16 + 16]

    @pl.loop(0, GROUP // 16)
    def _(g):
        for u in range(16):
            z = jnp.dot(table_ref[...], cross[g * 16 + u], preferred_element_type=jnp.float32)
            for h in range(2):
                lagged[h, u * LAG_ROWS : (u + 1) * LAG_ROWS, :] = z[:, h * 128 : (h + 1) * 128]
        at = pl.ds(pl.multiple_of(g * 16, 16), 16)
        for lag in range(LAGS):
            for h in range(2):
                v = lagged[h, pl.ds(lag, 16, stride=LAG_ROWS), :] * (1.0 / math.sqrt(W * F))
                out_ref[lag, at, h * 128 : (h + 1) * 128] = v.astype(jnp.bfloat16)


def correlate(places, row_blocks, col_blocks):
    n, m = OWN * len(row_blocks), OWN * len(col_blocks)
    whole = pl.BlockSpec((OWN, LANES), lambda s: (0, 0))
    return pl.pallas_call(
        functools.partial(correlate_kernel, len(row_blocks), len(col_blocks)),
        grid=(n // GROUP,),
        in_specs=[pl.BlockSpec(memory_space=pltpu.SMEM)]
        + [whole] * (len(row_blocks) + len(col_blocks))
        + [pl.BlockSpec((LAG_ROWS, 2 * F), lambda s: (0, 0))],
        out_specs=pl.BlockSpec((LAGS, GROUP, m), lambda s: (0, s, 0)),
        out_shape=jax.ShapeDtypeStruct((LAGS, n, m), jnp.bfloat16),
        scratch_shapes=[
            pltpu.VMEM((m, LANES), jnp.bfloat16),
            pltpu.VMEM((LANES, m), jnp.bfloat16),
            pltpu.VMEM((n, LANES), jnp.float32),
            pltpu.VMEM((n, LANES), jnp.float32),
            pltpu.VMEM((GROUP, 2 * F, m), jnp.bfloat16),
            pltpu.VMEM((2, 16 * LAG_ROWS, 128), jnp.float32),
        ],
        compiler_params=pltpu.CompilerParams(vmem_limit_bytes=60 * 1024 * 1024),
    )(places, *row_blocks, *col_blocks, jnp.asarray(lag_table(), jnp.bfloat16))


def gather8(block, move):
    side = move(block, 0, 1)
    found = {(0, 0): block, (0, 1): side}
    found[-1, 0] = move(block, 1, 0)
    found[1, 0] = move(block, -1, 0)
    found[2, 0] = move(found[-1, 0], 1, 0)
    found[-1, 1] = move(side, 1, 0)
    found[1, 1] = move(side, -1, 0)
    found[2, 1] = move(found[2, 0], 0, 1)
    return found


def body(spectra, offsets, channel_mask):
    white = whiten(spectra, offsets, channel_mask)
    p, src = lax.axis_index("rcv"), lax.axis_index("src")
    q, core = src // 2, src % 2

    def step(index, ring, side):
        return (index ^ (4 * side)) & 4 | (index + ring) & 3

    def over_rcv(value, ring, side):
        return lax.ppermute(value, "rcv", [(i, step(i, ring, side)) for i in range(8)])

    def over_src(value, ring, side):
        return lax.ppermute(value, "src", [(i, 2 * step(i // 2, ring, side) + i % 2) for i in range(16)])

    def other_core(value):
        return lax.ppermute(value, "src", [(i, i ^ 1) for i in range(16)])

    flip = [((i * 2 + k) * 8 + j, (j * 2 + k) * 8 + i) for i in range(8) for k in range(2) for j in range(8)]
    turned = lax.ppermute(white, ("src", "rcv"), flip)
    rows = gather8(white, over_rcv)
    cols = gather8(turned, over_src)
    swapped = {key: other_core(value) for key, value in cols.items()}
    places = [step(p, *key) for key in rows]
    places += [core * 8 + step(q, *key) for key in cols]
    places += [(1 - core) * 8 + step(q, *key) for key in swapped]
    places = jnp.stack(places).astype(jnp.int32)
    return correlate(places, list(rows.values()), list(cols.values()) + list(swapped.values()))


def solution(mesh):
    in_specs = (P(("src", "rcv"), None, None, None), P(("src", "rcv"), None), P(("src", "rcv")))
    out_specs = P(None, "src", "rcv")
    return jax.shard_map(body, mesh=mesh, in_specs=in_specs, out_specs=out_specs, check_vma=False)
```

time: 605 us -> 171 us (0.28)
  matrix products: 182 us -> 0 us
  waiting for transfers between devices: 189 us -> 8.26 us
  local copies, waits for them, and re-layouts: 147 us -> 2.58 us
  Pallas kernels: 0 us -> 110 us
  other arithmetic: 63 us -> 0 us
  starting transfers between devices: 0.04 us -> 49.9 us
  between operations: 13.5 us -> 0.18 us
  loops' own time: 6.75 us -> 0 us
    dot_general x20 -> x0, matrix products: 182 us -> none  [the longest x10 129 us: advance(): jnp.dot(weights.reshape(lag_count, width * 2), cross.reshape(width * 2, r...]
    psum x1 -> x0, waiting for transfers between devices: 147 us -> none  [from_root(): return lax.psum(jnp.where(mine, shard, jnp.zeros_like(shard)), axis)]
    pallas_call x0 -> x2, Pallas kernels: none -> 110 us  [the longest x1 107 us: correlate(): pl.pallas_call(functools.partial(correlate_kernel, len(row_blocks), len(c...]
    while x10 -> x0, local copies, waits for them, and re-layouts: 86.2 us -> none
    ppermute x0 -> x23, starting transfers between devices: none -> 49.9 us  [the longest x7 19.4 us: over_src(): lax.ppermute(value, 'src', [(i, 2 * step(i // 2, ring, side) + i % 2) for...]
    unnamed x9 -> x31, local copies, waits for them, and re-layouts: 48 us -> 1.9 us
    all_gather x1 -> x0, waiting for transfers between devices: 42.4 us -> none  [body(): rows = lax.all_gather(white, 'rcv', axis=0, tiled=True)]
    another operation x6 -> x0, other arithmetic: 32.6 us -> none  [the longest x2 29.6 us: correlate(): flipped = jnp.stack([cols, jnp.stack([-cols[:, 1], cols[:, 0]], 1)], 1)]
  transfers between devices with their start and end apart: 2 -> 23, of which waited for: 2 -> 7; matrix products, arithmetic and copies ran while one was open for 2% -> 0% of each run, Pallas kernels for 0% -> 0%
where the time goes in v1:
time: 171 us
  Pallas kernels  110 us (64%)
  starting transfers between devices  49.9 us (29%)
  waiting for transfers between devices  8.26 us (5%)
  local copies, waits for them, and re-layouts  2.58 us (2%)
    pallas_call x1, Pallas kernels, correlate(): pl.pallas_call(functools.partial(correlate_kernel, len(row_blocks), len(c...  107 us
    ppermute x7, starting transfers between devices, over_src(): lax.ppermute(value, 'src', [(i, 2 * step(i // 2, ring, side) + i % 2) for...  19.4 us
    ppermute x8, starting transfers between devices, other_core(): return lax.ppermute(value, 'src', [(i, i ^ 1) for i in range(16)])  16.9 us
    ppermute x7, starting transfers between devices, over_rcv(): lax.ppermute(value, 'rcv', [(i, step(i, ring, side)) for i in range(8)])  12 us
    ppermute x7, waiting for transfers between devices, over_rcv(): lax.ppermute(value, 'rcv', [(i, step(i, ring, side)) for i in range(8)])  5.21 us
  transfers between devices with their start and end apart: 23, of which 7 were waited for; matrix products, arithmetic and copies ran while one was open for 0% of the time, Pallas kernels for 0%

profile of v1, /device:TPU:1, one launch (start us, length us, event | category | flops | bytes accessed | tf_op | source)
XLA Modules:
  0.0 170.8 jit_solution(16321856373877825654)
XLA Ops:
  0.0 1.8 %copy.5.spectra_ref = bf16[16,2,10,400]{3,2,1,0:T(8,128)(2,1)} copy(bf16[16,2,10,400]{3,1,2,0:T(2,128)(2,1)} %param.4) | data formatting | bytes 512000 | tf_op args[0]
  1.8 3.4 %shard_map.46.refs_0_ = bf16[16,8064]{1,0:T(8,128)(2,1)} custom-call(s32[16]{0:T(128)} %mask_ref.1, bf16[16,2,10,400]{3,2,1,0:T(8,128)(2,1)} %copy.5.spectra_ref, s32[16,10]{1,0:T(8,128)} %offsets_ref.1), custom_call_target="tpu_custom_call" | custom-call | tf_op jit(solution)/shard_map/pallas_call | solution.py:84
  5.2 1.6 collective-permute-start.7
  6.8 6.3 %collective-permute-start.2 = (bf16[16,8064]{1,0:T(8,128)(2,1)}, bf16[16,8064]{1,0:T(8,128)(2,1)S(1)}, u32[]{:S(2)}, u32[]{:S(2)}) collective-permute-start(bf16[16,8064]{1,0:T(8,128)(2,1)} %shard_map.46.refs_0_), channel_id=1, source_target_pairs={{0,3},{1,0},{2,1},{3,2},{4,7},{5,4},{6,5},{7,6},{8,11},{9,8},{10,9... | collective-permute-start | bytes 774152 | tf_op jit(solution)/shard_map/ppermute | solution.py:224
  13.2 0.0 collective-permute-start.1
  13.2 3.0 %collective-permute-start = (bf16[16,8064]{1,0:T(8,128)(2,1)}, bf16[16,8064]{1,0:T(8,128)(2,1)S(1)}, u32[]{:S(2)}, u32[]{:S(2)}) collective-permute-start(bf16[16,8064]{1,0:T(8,128)(2,1)} %shard_map.46.refs_0_), channel_id=1, source_target_pairs={{0,4},{1,5},{2,6},{3,7},{4,0},{5,1},{6,2},{7,3},{8,12},{9,13},{10,... | collective-permute-start | bytes 774152 | tf_op jit(solution)/shard_map/ppermute | solution.py:224
  16.2 0.0 collective-permute-done.7.refs_8_
  16.2 1.5 collective-permute-start.15
  17.7 11.3 %collective-permute-start.10 = (bf16[16,8064]{1,0:T(8,128)(2,1)S(1)}, bf16[16,8064]{1,0:T(8,128)(2,1)S(1)}, u32[]{:S(2)}, u32[]{:S(2)}) collective-permute-start(bf16[16,8064]{1,0:T(8,128)(2,1)S(1)} %collective-permute-done.7.refs_8_), channel_id=1, source_target_pairs={{0,48},{8,56},{16,0},{24,8},{32,16},{40,24},{48,32},{56,40},{64,11... | collective-permute-start | bytes 774152 | tf_op jit(solution)/shard_map/ppermute | solution.py:227
  29.0 0.0 collective-permute-done.2.refs_3_
  29.0 0.0 collective-permute-start.9
  29.0 1.5 collective-permute-done.1.refs_2_
  30.5 3.1 %collective-permute-start.8 = (bf16[16,8064]{1,0:T(8,128)(2,1)S(1)}, bf16[16,8064]{1,0:T(8,128)(2,1)S(1)}, u32[]{:S(2)}, u32[]{:S(2)}) collective-permute-start(bf16[16,8064]{1,0:T(8,128)(2,1)S(1)} %collective-permute-done.7.refs_8_), channel_id=1, source_target_pairs={{0,64},{8,72},{16,80},{24,88},{32,96},{40,104},{48,112},{56,120},{... | collective-permute-start | bytes 774152 | tf_op jit(solution)/shard_map/ppermute | solution.py:227
  33.7 0.0 collective-permute-done.refs_1_
  33.7 0.0 collective-permute-start.3
  33.7 0.0 collective-permute-done.15.refs_16_
  33.7 2.7 %collective-permute-start.5 = (bf16[16,8064]{1,0:T(8,128)(2,1)S(1)}, bf16[16,8064]{1,0:T(8,128)(2,1)S(1)}, u32[]{:S(2)}, u32[]{:S(2)}) collective-permute-start(bf16[16,8064]{1,0:T(8,128)(2,1)S(1)} %collective-permute-done.refs_1_), channel_id=1, source_target_pairs={{0,3},{1,0},{2,1},{3,2},{4,7},{5,4},{6,5},{7,6},{8,11},{9,8},{10,9... | collective-permute-start | bytes 774152 | tf_op jit(solution)/shard_map/ppermute | solution.py:224
  36.4 0.0 collective-permute-done.10.refs_11_
  36.4 0.0 collective-permute-start.4
  36.4 1.3 collective-permute-done.9.refs_10_
  37.7 1.1 collective-permute-start.18
  38.8 0.3 collective-permute-done.8.refs_9_
  39.1 0.0 collective-permute-start.11
  39.1 2.2 %collective-permute-done.3.refs_4_ = bf16[16,8064]{1,0:T(8,128)(2,1)S(1)} collective-permute-done((bf16[16,8064]{1,0:T(8,128)(2,1)S(1)}, bf16[16,8064]{1,0:T(8,128)(2,1)S(1)}, u32[]{:S(2)}, u32[]{:S(2)}) %collective-permute-start.3) | collective-permute-done | bytes 258080 | tf_op jit(solution)/shard_map/ppermute | solution.py:224
  41.3 4.0 %collective-permute-start.17 = (bf16[16,8064]{1,0:T(8,128)(2,1)S(1)}, bf16[16,8064]{1,0:T(8,128)(2,1)S(1)}, u32[]{:S(2)}, u32[]{:S(2)}) collective-permute-start(bf16[16,8064]{1,0:T(8,128)(2,1)S(1)} %collective-permute-done.9.refs_10_), channel_id=1, source_target_pairs={{0,8},{8,0},{16,24},{24,16},{32,40},{40,32},{48,56},{56,48},{64,72... | collective-permute-start | bytes 774152 | tf_op jit(solution)/shard_map/ppermute | solution.py:230
  45.3 0.0 collective-permute-done.5.refs_6_
  45.3 0.1 collective-permute-start.16
  45.4 1.5 collective-permute-done.4.refs_5_
  46.9 2.9 %collective-permute-start.13 = (bf16[16,8064]{1,0:T(8,128)(2,1)S(1)}, bf16[16,8064]{1,0:T(8,128)(2,1)}, u32[]{:S(2)}, u32[]{:S(2)}) collective-permute-start(bf16[16,8064]{1,0:T(8,128)(2,1)S(1)} %collective-permute-done.8.refs_9_), channel_id=1, source_target_pairs={{0,48},{8,56},{16,0},{24,8},{32,16},{40,24},{48,32},{56,40},{64,11... | collective-permute-start | bytes 774152 | tf_op jit(solution)/shard_map/ppermute | solution.py:227
  49.8 0.0 collective-permute-done.18.refs_19_
  49.8 0.0 collective-permute-start.12
  49.8 0.0 collective-permute-done.11.refs_12_
  49.8 2.0 %collective-permute-start.14 = (bf16[16,8064]{1,0:T(8,128)(2,1)S(1)}, bf16[16,8064]{1,0:T(8,128)(2,1)}, u32[]{:S(2)}, u32[]{:S(2)}) collective-permute-start(bf16[16,8064]{1,0:T(8,128)(2,1)S(1)} %collective-permute-done.11.refs_12_), channel_id=1, source_target_pairs={{0,64},{8,72},{16,80},{24,88},{32,96},{40,104},{48,112},{56,120},{... | collective-permute-start | bytes 774152 | tf_op jit(solution)/shard_map/ppermute | solution.py:227
  51.8 0.0 collective-permute-done.17.refs_18_
  51.8 0.0 collective-permute-start.6
  51.8 0.0 collective-permute-done.16.refs_17_
  51.9 2.6 %collective-permute-start.19 = (bf16[16,8064]{1,0:T(8,128)(2,1)S(1)}, bf16[16,8064]{1,0:T(8,128)(2,1)}, u32[]{:S(2)}, u32[]{:S(2)}) collective-permute-start(bf16[16,8064]{1,0:T(8,128)(2,1)S(1)} %collective-permute-done.11.refs_12_), channel_id=1, source_target_pairs={{0,8},{8,0},{16,24},{24,16},{32,40},{40,32},{48,56},{56,48},{64,72... | collective-permute-start | bytes 774152 | tf_op jit(solution)/shard_map/ppermute | solution.py:230
  54.5 0.0 collective-permute-done.13.refs_14_
  54.5 1.7 %collective-permute-start.21 = (bf16[16,8064]{1,0:T(8,128)(2,1)}, bf16[16,8064]{1,0:T(8,128)(2,1)}, u32[]{:S(2)}, u32[]{:S(2)}) collective-permute-start(bf16[16,8064]{1,0:T(8,128)(2,1)} %collective-permute-done.13.refs_14_), channel_id=1, source_target_pairs={{0,8},{8,0},{16,24},{24,16},{32,40},{40,32},{48,56},{56,48},{64,72... | collective-permute-start | bytes 774152 | tf_op jit(solution)/shard_map/ppermute | solution.py:230
  56.2 0.6 collective-permute-done.12.refs_13_
  56.8 2.9 %collective-permute-start.20 = (bf16[16,8064]{1,0:T(8,128)(2,1)}, bf16[16,8064]{1,0:T(8,128)(2,1)}, u32[]{:S(2)}, u32[]{:S(2)}) collective-permute-start(bf16[16,8064]{1,0:T(8,128)(2,1)} %collective-permute-done.12.refs_13_), channel_id=1, source_target_pairs={{0,8},{8,0},{16,24},{24,16},{32,40},{40,32},{48,56},{56,48},{64,72... | collective-permute-start | bytes 774152 | tf_op jit(solution)/shard_map/ppermute | solution.py:230
  59.7 0.0 collective-permute-done.14.refs_15_
  59.8 2.9 %collective-permute-start.22 = (bf16[16,8064]{1,0:T(8,128)(2,1)}, bf16[16,8064]{1,0:T(8,128)(2,1)}, u32[]{:S(2)}, u32[]{:S(2)}) collective-permute-start(bf16[16,8064]{1,0:T(8,128)(2,1)} %collective-permute-done.14.refs_15_), channel_id=1, source_target_pairs={{0,8},{8,0},{16,24},{24,16},{32,40},{40,32},{48,56},{56,48},{64,72... | collective-permute-start | bytes 774152 | tf_op jit(solution)/shard_map/ppermute | solution.py:230
  62.7 0.7 stack.99.place_ref
  63.4 0.0 collective-permute-done.6.refs_7_
  63.4 0.0 collective-permute-done.20.refs_21_
  63.4 0.8 collective-permute-done.22.refs_23_
  64.3 106.5 %shard_map.47 = bf16[101,128,256]{2,1,0:T(8,128)(2,1)} custom-call(s32[24]{0:T(128)} %stack.99.place_ref, bf16[16,8064]{1,0:T(8,128)(2,1)} %shard_map.46.refs_0_, bf16[16,8064]{1,0:T(8,128)(2,1)} %copy-done.3, bf16[16,8064]{1,0:T(8,128)(2,1)} %copy-done.2, bf16[16,8064]{1,0:T(8,128)(2,1)} %copy-done.1, bf16[16,8064]{1,0:T(8,128)(2,1)} %copy-done.8, ...), custom_call_target="tpu_custom_call" | custom-call | tf_op jit(solution)/shard_map/pallas_call | solution.py:183
  (32 shorter events, 0.1 us)
Async XLA Ops:
  5.2 10.9 %collective-permute-start.7 = (bf16[16,8064]{1,0:T(8,128)(2,1)}, bf16[16,8064]{1,0:T(8,128)(2,1)S(1)}, u32[]{:S(2)}, u32[]{:S(2)}) collective-permute-start(bf16[16,8064]{1,0:T(8,128)(2,1)} %shard_map.46.refs_0_), channel_id=1, source_target_pairs={{0,0},{1,16},{2,32},{3,48},{4,64},{5,80},{6,96},{7,112},{8,8},{9,2... | collective-permute-start | bytes 774152 | tf_op jit(solution)/shard_map/ppermute | solution.py:233
  6.8 22.1 %collective-permute-start.2 = (bf16[16,8064]{1,0:T(8,128)(2,1)}, bf16[16,8064]{1,0:T(8,128)(2,1)S(1)}, u32[]{:S(2)}, u32[]{:S(2)}) collective-permute-start(bf16[16,8064]{1,0:T(8,128)(2,1)} %shard_map.46.refs_0_), channel_id=1, source_target_pairs={{0,3},{1,0},{2,1},{3,2},{4,7},{5,4},{6,5},{7,6},{8,11},{9,8},{10,9... | collective-permute-start | bytes 774152 | tf_op jit(solution)/shard_map/ppermute | solution.py:224
  13.2 17.4 %collective-permute-start.1 = (bf16[16,8064]{1,0:T(8,128)(2,1)}, bf16[16,8064]{1,0:T(8,128)(2,1)S(1)}, u32[]{:S(2)}, u32[]{:S(2)}) collective-permute-start(bf16[16,8064]{1,0:T(8,128)(2,1)} %shard_map.46.refs_0_), channel_id=1, source_target_pairs={{0,1},{1,2},{2,3},{3,0},{4,5},{5,6},{6,7},{7,4},{8,9},{9,10},{10,1... | collective-permute-start | bytes 774152 | tf_op jit(solution)/shard_map/ppermute | solution.py:224
  13.2 20.5 %collective-permute-start = (bf16[16,8064]{1,0:T(8,128)(2,1)}, bf16[16,8064]{1,0:T(8,128)(2,1)S(1)}, u32[]{:S(2)}, u32[]{:S(2)}) collective-permute-start(bf16[16,8064]{1,0:T(8,128)(2,1)} %shard_map.46.refs_0_), channel_id=1, source_target_pairs={{0,4},{1,5},{2,6},{3,7},{4,0},{5,1},{6,2},{7,3},{8,12},{9,13},{10,... | collective-permute-start | bytes 774152 | tf_op jit(solution)/shard_map/ppermute | solution.py:224
  16.2 48.0 %copy-start = (bf16[16,8064]{1,0:T(8,128)(2,1)}, bf16[16,8064]{1,0:T(8,128)(2,1)S(1)}, u32[]{:S(2)}) copy-start(bf16[16,8064]{1,0:T(8,128)(2,1)S(1)} %collective-permute-done.7.refs_8_) | copy-start | bytes 774148
  16.2 17.5 %collective-permute-start.15 = (bf16[16,8064]{1,0:T(8,128)(2,1)S(1)}, bf16[16,8064]{1,0:T(8,128)(2,1)S(1)}, u32[]{:S(2)}, u32[]{:S(2)}) collective-permute-start(bf16[16,8064]{1,0:T(8,128)(2,1)S(1)} %collective-permute-done.7.refs_8_), channel_id=1, source_target_pairs={{0,8},{8,0},{16,24},{24,16},{32,40},{40,32},{48,56},{56,48},{64,72... | collective-permute-start | bytes 774152 | tf_op jit(solution)/shard_map/ppermute | solution.py:230
  17.7 18.7 %collective-permute-start.10 = (bf16[16,8064]{1,0:T(8,128)(2,1)S(1)}, bf16[16,8064]{1,0:T(8,128)(2,1)S(1)}, u32[]{:S(2)}, u32[]{:S(2)}) collective-permute-start(bf16[16,8064]{1,0:T(8,128)(2,1)S(1)} %collective-permute-done.7.refs_8_), channel_id=1, source_target_pairs={{0,48},{8,56},{16,0},{24,8},{32,16},{40,24},{48,32},{56,40},{64,11... | collective-permute-start | bytes 774152 | tf_op jit(solution)/shard_map/ppermute | solution.py:227
  29.0 35.2 %copy-start.1 = (bf16[16,8064]{1,0:T(8,128)(2,1)}, bf16[16,8064]{1,0:T(8,128)(2,1)S(1)}, u32[]{:S(2)}) copy-start(bf16[16,8064]{1,0:T(8,128)(2,1)S(1)} %collective-permute-done.2.refs_3_) | copy-start | bytes 774148
  29.0 8.7 %collective-permute-start.9 = (bf16[16,8064]{1,0:T(8,128)(2,1)S(1)}, bf16[16,8064]{1,0:T(8,128)(2,1)S(1)}, u32[]{:S(2)}, u32[]{:S(2)}) collective-permute-start(bf16[16,8064]{1,0:T(8,128)(2,1)S(1)} %collective-permute-done.7.refs_8_), channel_id=1, source_target_pairs={{0,16},{8,24},{16,32},{24,40},{32,48},{40,56},{48,0},{56,8},{64,80... | collective-permute-start | bytes 774152 | tf_op jit(solution)/shard_map/ppermute | solution.py:227
  30.5 33.7 %copy-start.2 = (bf16[16,8064]{1,0:T(8,128)(2,1)}, bf16[16,8064]{1,0:T(8,128)(2,1)S(1)}, u32[]{:S(2)}) copy-start(bf16[16,8064]{1,0:T(8,128)(2,1)S(1)} %collective-permute-done.1.refs_2_) | copy-start | bytes 774148
  30.5 8.6 %collective-permute-start.8 = (bf16[16,8064]{1,0:T(8,128)(2,1)S(1)}, bf16[16,8064]{1,0:T(8,128)(2,1)S(1)}, u32[]{:S(2)}, u32[]{:S(2)}) collective-permute-start(bf16[16,8064]{1,0:T(8,128)(2,1)S(1)} %collective-permute-done.7.refs_8_), channel_id=1, source_target_pairs={{0,64},{8,72},{16,80},{24,88},{32,96},{40,104},{48,112},{56,120},{... | collective-permute-start | bytes 774152 | tf_op jit(solution)/shard_map/ppermute | solution.py:227
  33.7 30.5 %copy-start.3 = (bf16[16,8064]{1,0:T(8,128)(2,1)}, bf16[16,8064]{1,0:T(8,128)(2,1)S(1)}, u32[]{:S(2)}) copy-start(bf16[16,8064]{1,0:T(8,128)(2,1)S(1)} %collective-permute-done.refs_1_) | copy-start | bytes 774148
  33.7 7.7 %collective-permute-start.3 = (bf16[16,8064]{1,0:T(8,128)(2,1)S(1)}, bf16[16,8064]{1,0:T(8,128)(2,1)S(1)}, u32[]{:S(2)}, u32[]{:S(2)}) collective-permute-start(bf16[16,8064]{1,0:T(8,128)(2,1)S(1)} %collective-permute-done.1.refs_2_), channel_id=1, source_target_pairs={{0,1},{1,2},{2,3},{3,0},{4,5},{5,6},{6,7},{7,4},{8,9},{9,10},{10,1... | collective-permute-start | bytes 774152 | tf_op jit(solution)/shard_map/ppermute | solution.py:224
  33.7 30.5 %copy-start.4 = (bf16[16,8064]{1,0:T(8,128)(2,1)}, bf16[16,8064]{1,0:T(8,128)(2,1)S(1)}, u32[]{:S(2)}) copy-start(bf16[16,8064]{1,0:T(8,128)(2,1)S(1)} %collective-permute-done.15.refs_16_) | copy-start | bytes 774148
  33.7 11.6 %collective-permute-start.5 = (bf16[16,8064]{1,0:T(8,128)(2,1)S(1)}, bf16[16,8064]{1,0:T(8,128)(2,1)S(1)}, u32[]{:S(2)}, u32[]{:S(2)}) collective-permute-start(bf16[16,8064]{1,0:T(8,128)(2,1)S(1)} %collective-permute-done.refs_1_), channel_id=1, source_target_pairs={{0,3},{1,0},{2,1},{3,2},{4,7},{5,4},{6,5},{7,6},{8,11},{9,8},{10,9... | collective-permute-start | bytes 774152 | tf_op jit(solution)/shard_map/ppermute | solution.py:224
  36.4 27.9 %copy-start.5 = (bf16[16,8064]{1,0:T(8,128)(2,1)}, bf16[16,8064]{1,0:T(8,128)(2,1)S(1)}, u32[]{:S(2)}) copy-start(bf16[16,8064]{1,0:T(8,128)(2,1)S(1)} %collective-permute-done.10.refs_11_) | copy-start | bytes 774148
  36.4 10.5 %collective-permute-start.4 = (bf16[16,8064]{1,0:T(8,128)(2,1)S(1)}, bf16[16,8064]{1,0:T(8,128)(2,1)S(1)}, u32[]{:S(2)}, u32[]{:S(2)}) collective-permute-start(bf16[16,8064]{1,0:T(8,128)(2,1)S(1)} %collective-permute-done.refs_1_), channel_id=1, source_target_pairs={{0,1},{1,2},{2,3},{3,0},{4,5},{5,6},{6,7},{7,4},{8,9},{9,10},{10,1... | collective-permute-start | bytes 774152 | tf_op jit(solution)/shard_map/ppermute | solution.py:224
  37.7 26.5 %copy-start.6 = (bf16[16,8064]{1,0:T(8,128)(2,1)}, bf16[16,8064]{1,0:T(8,128)(2,1)S(1)}, u32[]{:S(2)}) copy-start(bf16[16,8064]{1,0:T(8,128)(2,1)S(1)} %collective-permute-done.9.refs_10_) | copy-start | bytes 774148
  37.7 12.1 %collective-permute-start.18 = (bf16[16,8064]{1,0:T(8,128)(2,1)S(1)}, bf16[16,8064]{1,0:T(8,128)(2,1)S(1)}, u32[]{:S(2)}, u32[]{:S(2)}) collective-permute-start(bf16[16,8064]{1,0:T(8,128)(2,1)S(1)} %collective-permute-done.10.refs_11_), channel_id=1, source_target_pairs={{0,8},{8,0},{16,24},{24,16},{32,40},{40,32},{48,56},{56,48},{64,72... | collective-permute-start | bytes 774152 | tf_op jit(solution)/shard_map/ppermute | solution.py:230
  39.1 25.1 %copy-start.7 = (bf16[16,8064]{1,0:T(8,128)(2,1)}, bf16[16,8064]{1,0:T(8,128)(2,1)S(1)}, u32[]{:S(2)}) copy-start(bf16[16,8064]{1,0:T(8,128)(2,1)S(1)} %collective-permute-done.8.refs_9_) | copy-start | bytes 774148
  39.1 10.7 %collective-permute-start.11 = (bf16[16,8064]{1,0:T(8,128)(2,1)S(1)}, bf16[16,8064]{1,0:T(8,128)(2,1)S(1)}, u32[]{:S(2)}, u32[]{:S(2)}) collective-permute-start(bf16[16,8064]{1,0:T(8,128)(2,1)S(1)} %collective-permute-done.9.refs_10_), channel_id=1, source_target_pairs={{0,16},{8,24},{16,32},{24,40},{32,48},{40,56},{48,0},{56,8},{64,80... | collective-permute-start | bytes 774152 | tf_op jit(solution)/shard_map/ppermute | solution.py:227
  41.3 22.9 %copy-start.8 = (bf16[16,8064]{1,0:T(8,128)(2,1)}, bf16[16,8064]{1,0:T(8,128)(2,1)S(1)}, u32[]{:S(2)}) copy-start(bf16[16,8064]{1,0:T(8,128)(2,1)S(1)} %collective-permute-done.3.refs_4_) | copy-start | bytes 774148
  41.3 10.5 %collective-permute-start.17 = (bf16[16,8064]{1,0:T(8,128)(2,1)S(1)}, bf16[16,8064]{1,0:T(8,128)(2,1)S(1)}, u32[]{:S(2)}, u32[]{:S(2)}) collective-permute-start(bf16[16,8064]{1,0:T(8,128)(2,1)S(1)} %collective-permute-done.9.refs_10_), channel_id=1, source_target_pairs={{0,8},{8,0},{16,24},{24,16},{32,40},{40,32},{48,56},{56,48},{64,72... | collective-permute-start | bytes 774152 | tf_op jit(solution)/shard_map/ppermute | solution.py:230
  45.3 18.9 %copy-start.9 = (bf16[16,8064]{1,0:T(8,128)(2,1)}, bf16[16,8064]{1,0:T(8,128)(2,1)S(1)}, u32[]{:S(2)}) copy-start(bf16[16,8064]{1,0:T(8,128)(2,1)S(1)} %collective-permute-done.5.refs_6_) | copy-start | bytes 774148
  45.3 6.5 %collective-permute-start.16 = (bf16[16,8064]{1,0:T(8,128)(2,1)S(1)}, bf16[16,8064]{1,0:T(8,128)(2,1)S(1)}, u32[]{:S(2)}, u32[]{:S(2)}) collective-permute-start(bf16[16,8064]{1,0:T(8,128)(2,1)S(1)} %collective-permute-done.8.refs_9_), channel_id=1, source_target_pairs={{0,8},{8,0},{16,24},{24,16},{32,40},{40,32},{48,56},{56,48},{64,72... | collective-permute-start | bytes 774152 | tf_op jit(solution)/shard_map/ppermute | solution.py:230
  46.9 17.4 %copy-start.10 = (bf16[16,8064]{1,0:T(8,128)(2,1)}, bf16[16,8064]{1,0:T(8,128)(2,1)S(1)}, u32[]{:S(2)}) copy-start(bf16[16,8064]{1,0:T(8,128)(2,1)S(1)} %collective-permute-done.4.refs_5_) | copy-start | bytes 774148
  46.9 7.6 %collective-permute-start.13 = (bf16[16,8064]{1,0:T(8,128)(2,1)S(1)}, bf16[16,8064]{1,0:T(8,128)(2,1)}, u32[]{:S(2)}, u32[]{:S(2)}) collective-permute-start(bf16[16,8064]{1,0:T(8,128)(2,1)S(1)} %collective-permute-done.8.refs_9_), channel_id=1, source_target_pairs={{0,48},{8,56},{16,0},{24,8},{32,16},{40,24},{48,32},{56,40},{64,11... | collective-permute-start | bytes 774152 | tf_op jit(solution)/shard_map/ppermute | solution.py:227
  49.8 14.5 %copy-start.11 = (bf16[16,8064]{1,0:T(8,128)(2,1)}, bf16[16,8064]{1,0:T(8,128)(2,1)S(1)}, u32[]{:S(2)}) copy-start(bf16[16,8064]{1,0:T(8,128)(2,1)S(1)} %collective-permute-done.18.refs_19_) | copy-start | bytes 774148
  49.8 7.0 %collective-permute-start.12 = (bf16[16,8064]{1,0:T(8,128)(2,1)S(1)}, bf16[16,8064]{1,0:T(8,128)(2,1)}, u32[]{:S(2)}, u32[]{:S(2)}) collective-permute-start(bf16[16,8064]{1,0:T(8,128)(2,1)S(1)} %collective-permute-done.8.refs_9_), channel_id=1, source_target_pairs={{0,16},{8,24},{16,32},{24,40},{32,48},{40,56},{48,0},{56,8},{64,80... | collective-permute-start | bytes 774152 | tf_op jit(solution)/shard_map/ppermute | solution.py:227
  49.8 14.5 %copy-start.12 = (bf16[16,8064]{1,0:T(8,128)(2,1)}, bf16[16,8064]{1,0:T(8,128)(2,1)S(1)}, u32[]{:S(2)}) copy-start(bf16[16,8064]{1,0:T(8,128)(2,1)S(1)} %collective-permute-done.11.refs_12_) | copy-start | bytes 774148
  49.8 9.9 %collective-permute-start.14 = (bf16[16,8064]{1,0:T(8,128)(2,1)S(1)}, bf16[16,8064]{1,0:T(8,128)(2,1)}, u32[]{:S(2)}, u32[]{:S(2)}) collective-permute-start(bf16[16,8064]{1,0:T(8,128)(2,1)S(1)} %collective-permute-done.11.refs_12_), channel_id=1, source_target_pairs={{0,64},{8,72},{16,80},{24,88},{32,96},{40,104},{48,112},{56,120},{... | collective-permute-start | bytes 774152 | tf_op jit(solution)/shard_map/ppermute | solution.py:227
  51.8 7.9 %copy-start.13 = (bf16[16,8064]{1,0:T(8,128)(2,1)}, bf16[16,8064]{1,0:T(8,128)(2,1)S(1)}, u32[]{:S(2)}) copy-start(bf16[16,8064]{1,0:T(8,128)(2,1)S(1)} %collective-permute-done.17.refs_18_) | copy-start | bytes 774148
  51.8 11.5 %collective-permute-start.6 = (bf16[16,8064]{1,0:T(8,128)(2,1)S(1)}, bf16[16,8064]{1,0:T(8,128)(2,1)}, u32[]{:S(2)}, u32[]{:S(2)}) collective-permute-start(bf16[16,8064]{1,0:T(8,128)(2,1)S(1)} %collective-permute-done.3.refs_4_), channel_id=1, source_target_pairs={{0,4},{1,5},{2,6},{3,7},{4,0},{5,1},{6,2},{7,3},{8,12},{9,13},{10,... | collective-permute-start | bytes 774152 | tf_op jit(solution)/shard_map/ppermute | solution.py:224
  51.8 10.8 %copy-start.14 = (bf16[16,8064]{1,0:T(8,128)(2,1)}, bf16[16,8064]{1,0:T(8,128)(2,1)S(1)}, u32[]{:S(2)}) copy-start(bf16[16,8064]{1,0:T(8,128)(2,1)S(1)} %collective-permute-done.16.refs_17_) | copy-start | bytes 774148
  51.9 11.5 %collective-permute-start.19 = (bf16[16,8064]{1,0:T(8,128)(2,1)S(1)}, bf16[16,8064]{1,0:T(8,128)(2,1)}, u32[]{:S(2)}, u32[]{:S(2)}) collective-permute-start(bf16[16,8064]{1,0:T(8,128)(2,1)S(1)} %collective-permute-done.11.refs_12_), channel_id=1, source_target_pairs={{0,8},{8,0},{16,24},{24,16},{32,40},{40,32},{48,56},{56,48},{64,72... | collective-permute-start | bytes 774152 | tf_op jit(solution)/shard_map/ppermute | solution.py:230
  54.5 8.9 %collective-permute-start.21 = (bf16[16,8064]{1,0:T(8,128)(2,1)}, bf16[16,8064]{1,0:T(8,128)(2,1)}, u32[]{:S(2)}, u32[]{:S(2)}) collective-permute-start(bf16[16,8064]{1,0:T(8,128)(2,1)} %collective-permute-done.13.refs_14_), channel_id=1, source_target_pairs={{0,8},{8,0},{16,24},{24,16},{32,40},{40,32},{48,56},{56,48},{64,72... | collective-permute-start | bytes 774152 | tf_op jit(solution)/shard_map/ppermute | solution.py:230
  56.8 6.6 %collective-permute-start.20 = (bf16[16,8064]{1,0:T(8,128)(2,1)}, bf16[16,8064]{1,0:T(8,128)(2,1)}, u32[]{:S(2)}, u32[]{:S(2)}) collective-permute-start(bf16[16,8064]{1,0:T(8,128)(2,1)} %collective-permute-done.12.refs_13_), channel_id=1, source_target_pairs={{0,8},{8,0},{16,24},{24,16},{32,40},{40,32},{48,56},{56,48},{64,72... | collective-permute-start | bytes 774152 | tf_op jit(solution)/shard_map/ppermute | solution.py:230
  59.8 4.4 %collective-permute-start.22 = (bf16[16,8064]{1,0:T(8,128)(2,1)}, bf16[16,8064]{1,0:T(8,128)(2,1)}, u32[]{:S(2)}, u32[]{:S(2)}) collective-permute-start(bf16[16,8064]{1,0:T(8,128)(2,1)} %collective-permute-done.14.refs_15_), channel_id=1, source_target_pairs={{0,8},{8,0},{16,24},{24,16},{32,40},{40,32},{48,56},{56,48},{64,72... | collective-permute-start | bytes 774152 | tf_op jit(solution)/shard_map/ppermute | solution.py:230

commit v2 on v1

--- a/solution.py
+++ b/solution.py
@@ -16,13 +16,16 @@
 HALF = 50
 LAGS = 2 * HALF + 1
 LAG_ROWS = 104
+LAG_TILE = 112
 FB = 8
 NB = F // FB
 OWN = 16
 MAIN = 16
 TILES = NB + -(-NB // 4)
 LANES = TILES * 128
-GROUP = 32
+HALF_ROWS = 64
+DEPTH = 4
+LAG = 6
 
 
 def unit_circle(turns):
@@ -94,110 +97,159 @@
     )(channel_mask, spectra, offsets)
 
 
-def lag_table():
+def lag_tables(offsets):
     freq = KLO + np.arange(F)
     shifts = np.arange(LAGS) - HALF
     angle = 2.0 * math.pi / NT * ((shifts[:, None] * freq[None, :]) % NT)
     table = np.stack([np.cos(angle), -np.sin(angle)], 1).reshape(LAGS, 2, NB, FB)
     table = table.transpose(0, 2, 1, 3).reshape(LAGS, 2 * F)
-    return np.pad(table, ((0, LAG_ROWS - LAGS), (0, 0)))
+    table = np.pad(table, ((0, LAG_TILE - LAGS), (0, 0)))
+    tiles, done = [], 0
+    for at in offsets:
+        tile = table[:, at : at + 256].copy()
+        tile[:, : done - at] = 0
+        tiles.append(tile)
+        done = at + 256
+    return np.stack(tiles)
+
+
+def tile_offsets(rows):
+    return [min(at, rows - 256) for at in range(0, rows, 256)]
 
 
 def correlate_kernel(n_rows, n_cols, place_ref, *refs):
     row_refs, refs = refs[:n_rows], refs[n_rows:]
     col_refs, refs = refs[:n_cols], refs[n_cols:]
-    table_ref, out_ref, cols, cols_t, rows, turned, cross, lagged = refs
-    step = pl.program_id(0)
-    lane = lax.broadcasted_iota(jnp.int32, (8, 128), 1)
-    same_bin = (lane % 8) == lax.broadcasted_iota(jnp.int32, (8, 128), 0)
-
-    @pl.when(step == 0)
-    def _():
-        for k, ref in enumerate(col_refs):
-            cols[pl.ds(pl.multiple_of(place_ref[n_rows + k] * OWN, OWN), OWN), :] = ref[...]
-
-        def turn(values, shift):
-            odd = (lax.broadcasted_iota(jnp.int32, values.shape, 1) // shift) % 2 == 1
-            return jnp.where(odd, -pltpu.roll(values, shift, 1), pltpu.roll(values, 128 - shift, 1))
-
-        for k, ref in enumerate(row_refs):
-            at = pl.ds(pl.multiple_of(place_ref[k] * OWN, OWN), OWN)
-
-            @pl.loop(0, NB)
-            def _(t):
-                o = pl.ds(pl.multiple_of(t * 128, 128), 128)
-                r = ref[:, o].astype(jnp.float32)
-                rows[at, o] = r
-                turned[at, o] = turn(r, 8)
-
-            @pl.loop(NB, TILES)
-            def _(t):
-                o = pl.ds(pl.multiple_of(t * 128, 128), 128)
-                r = ref[:, o].astype(jnp.float32)
-                rows[at, o] = r
-                turned[at, o] = turn(r, 32)
-
-        @pl.loop(0, TILES)
-        def _(t):
-            o = pl.ds(pl.multiple_of(t * 128, 128), 128)
-            cols_t[o, :] = cols[:, o].T
-
-    base = pl.multiple_of(step * GROUP, GROUP)
-
-    @pl.loop(0, NB)
-    def _(b):
-        mo = pl.ds(pl.multiple_of(b * 128, 128), 128)
-        ro = pl.ds(pl.multiple_of((NB + b // 4) * 128, 128), 128)
-        right = jnp.concatenate([cols_t[mo, :], cols_t[ro, :]], 0)
-        same_rest = same_bin & ((lane // 8) % 4 == b % 4)
-        for g in range(GROUP // 8):
-            at = pl.ds(pl.multiple_of(base + g * 8, 8), 8)
-            loaded = [rows[at, mo], turned[at, mo], rows[at, ro], turned[at, ro]]
-            left = []
+    table_ref, out_ref, cols, cross, lagged, staged, sems = refs
+    lane = lax.broadcasted_iota(jnp.int32, (16, 128), 1)
+    same_bin = (lane % 8) == lax.broadcasted_iota(jnp.int32, (16, 128), 0) % 8
+    zero = jnp.zeros((), jnp.bfloat16)
+    groups = HALF_ROWS // 8
+
+    for k, ref in enumerate(col_refs):
+        cols[pl.ds(pl.multiple_of(place_ref[n_rows + k] * OWN, OWN), OWN), :] = ref[...]
+
+    def turn(values, shift):
+        odd = (lax.broadcasted_iota(jnp.int32, values.shape, 1) // shift) % 2 == 1
+        return jnp.where(odd, -pltpu.roll(values, shift, 1), pltpu.roll(values, 128 - shift, 1))
+
+    def lanes_of(b):
+        return pl.ds(pl.multiple_of(b * 128, 128), 128), pl.ds(pl.multiple_of((NB + b // 4) * 128, 128), 128)
+
+    def cross_of(half, *accs):
+        def push(b, mxu):
+            mo, ro = lanes_of(b)
+            right = jnp.concatenate([cols[:, mo], cols[:, ro]], 1)
+            pltpu.matmul_push_rhs(right, 0, mxu, transpose=True)
+
+        def left(b, k, same_rest):
+            mo, ro = lanes_of(b)
+            ref = row_refs[half * (HALF_ROWS // OWN) + k // 2]
+            at = slice(k % 2 * 8, k % 2 * 8 + 8)
+            m, r = ref[at, mo].astype(jnp.float32), ref[at, ro].astype(jnp.float32)
+            loaded = [m, turn(m, 8), r, turn(r, 32)]
+            parts = []
             for u in range(8):
                 v = [jnp.broadcast_to(x[u : u + 1], (8, 128)) for x in loaded]
-                m = jnp.concatenate([jnp.where(same_bin, v[0], 0.0), jnp.where(same_bin, v[1], 0.0)], 0)
-                r = jnp.concatenate([jnp.where(same_rest, v[2], 0.0), jnp.where(same_rest, v[3], 0.0)], 0)
-                left.append(jnp.concatenate([m.astype(jnp.bfloat16), r.astype(jnp.bfloat16)], 1))
-            product = jnp.dot(jnp.concatenate(left, 0), right, preferred_element_type=jnp.float32)
-            product = product.astype(jnp.bfloat16)
+                m = jnp.where(same_bin, jnp.concatenate(v[:2], 0).astype(jnp.bfloat16), zero)
+                r = jnp.where(same_rest, jnp.concatenate(v[2:], 0).astype(jnp.bfloat16), zero)
+                parts.append(jnp.concatenate([m, r], 1))
+            return jnp.concatenate(parts, 0)
+
+        def acc_of(k):
+            return accs[DEPTH * (k % 2) + k // 2 % DEPTH]
+
+        def pop(b, k):
+            product = pltpu.matmul_pop(acc_of(k)).astype(jnp.bfloat16)
+            at = pl.ds(pl.multiple_of(b * 16, 16), 16)
             for u in range(8):
-                cross[g * 8 + u, pl.ds(pl.multiple_of(b * 16, 16), 16), :] = product[u * 16 : u * 16 + 16]
-
-    @pl.loop(0, GROUP // 16)
-    def _(g):
-        for u in range(16):
-            z = jnp.dot(table_ref[...], cross[g * 16 + u], preferred_element_type=jnp.float32)
-            for h in range(2):
-                lagged[h, u * LAG_ROWS : (u + 1) * LAG_ROWS, :] = z[:, h * 128 : (h + 1) * 128]
-        at = pl.ds(pl.multiple_of(g * 16, 16), 16)
-        for lag in range(LAGS):
-            for h in range(2):
-                v = lagged[h, pl.ds(lag, 16, stride=LAG_ROWS), :] * (1.0 / math.sqrt(W * F))
-                out_ref[lag, at, h * 128 : (h + 1) * 128] = v.astype(jnp.bfloat16)
+                cross[k * 8 + u, at, :] = product[u * 16 : u * 16 + 16]
+
+        def block(b, first, last):
+            same_rest = same_bin & ((lane // 8) % 4 == b % 4)
+            for k in range(groups):
+                pltpu.matmul_acc_lhs(acc_of(k), left(b, k, same_rest), 0 if k < 2 else None)
+                if not last and 2 <= k < 4:
+                    push(b + 1, k % 2)
+                if k >= LAG:
+                    pop(b, k - LAG)
+                elif not first:
+                    pop(b - 1, k - LAG + groups)
+
+        push(0, 0)
+        push(0, 1)
+        block(0, True, False)
+        pl.loop(1, NB - 1)(lambda b: block(b, False, False))
+        block(NB - 1, False, True)
+        for k in range(groups - LAG, groups):
+            pop(NB - 1, k)
+
+    def out_copy(slot, k):
+        at = pl.ds(pl.multiple_of(place_ref[k] * OWN, OWN), OWN)
+        return pltpu.make_async_copy(staged.at[slot], out_ref.at[:, at, :], sems.at[slot])
+
+    offsets = tile_offsets(2 * F)
+
+    def lags_of(half, *accs):
+        for g in range(HALF_ROWS // OWN):
+            k = half * (HALF_ROWS // OWN) + g
+
+            def pop(u):
+                z = pltpu.matmul_pop(accs[u % 8])
+                for h in range(2):
+                    lagged[h, u * LAG_ROWS : (u + 1) * LAG_ROWS, :] = z[:LAG_ROWS, h * 128 : (h + 1) * 128]
+
+            for u in range(0, OWN, 2):
+                for t, at in enumerate(offsets):
+                    for v in (u, u + 1):
+                        pltpu.matmul_push_rhs(cross[g * OWN + v, at : at + 256, :], t % 2, v % 2)
+                    for v in (u, u + 1):
+                        pltpu.matmul_acc_lhs(accs[v % 8], table_ref[t], t % 2)
+                if u >= 4:
+                    pop(u - 4)
+                    pop(u - 3)
+            for u in range(OWN - 4, OWN):
+                pop(u)
+            slot = k % 2
+            if k >= 2:
+                out_copy(slot, k - 2).wait()
+            for lag in range(LAGS):
+                for h in range(2):
+                    v = lagged[h, pl.ds(lag, OWN, stride=LAG_ROWS), :] * (1.0 / math.sqrt(W * F))
+                    staged[slot, lag, :, h * 128 : (h + 1) * 128] = v.astype(jnp.bfloat16)
+            out_copy(slot, k).start()
+
+    for half in range(n_rows * OWN // HALF_ROWS):
+        pl.run_scoped(
+            functools.partial(cross_of, half),
+            *[pltpu.ACC(mxu)((128, 256), jnp.float32) for mxu in [0] * DEPTH + [1] * DEPTH],
+        )
+        pl.run_scoped(
+            functools.partial(lags_of, half),
+            *[pltpu.ACC(mxu)((LAG_TILE, 256), jnp.float32) for mxu in (0, 1) * 4],
+        )
+    for k in range(n_rows - 2, n_rows):
+        out_copy(k % 2, k).wait()
 
 
 def correlate(places, row_blocks, col_blocks):
     n, m = OWN * len(row_blocks), OWN * len(col_blocks)
-    whole = pl.BlockSpec((OWN, LANES), lambda s: (0, 0))
+    vmem = pl.BlockSpec(memory_space=pltpu.VMEM)
+    tables = jnp.asarray(lag_tables(tile_offsets(2 * F)), jnp.bfloat16)
     return pl.pallas_call(
         functools.partial(correlate_kernel, len(row_blocks), len(col_blocks)),
-        grid=(n // GROUP,),
-        in_specs=[pl.BlockSpec(memory_space=pltpu.SMEM)]
-        + [whole] * (len(row_blocks) + len(col_blocks))
-        + [pl.BlockSpec((LAG_ROWS, 2 * F), lambda s: (0, 0))],
-        out_specs=pl.BlockSpec((LAGS, GROUP, m), lambda s: (0, s, 0)),
+        in_specs=[pl.BlockSpec(memory_space=pltpu.SMEM)] + [vmem] * (len(row_blocks) + len(col_blocks) + 1),
+        out_specs=pl.BlockSpec(memory_space=pl.ANY),
         out_shape=jax.ShapeDtypeStruct((LAGS, n, m), jnp.bfloat16),
         scratch_shapes=[
             pltpu.VMEM((m, LANES), jnp.bfloat16),
-            pltpu.VMEM((LANES, m), jnp.bfloat16),
-            pltpu.VMEM((n, LANES), jnp.float32),
-            pltpu.VMEM((n, LANES), jnp.float32),
-            pltpu.VMEM((GROUP, 2 * F, m), jnp.bfloat16),
-            pltpu.VMEM((2, 16 * LAG_ROWS, 128), jnp.float32),
+            pltpu.VMEM((HALF_ROWS, 2 * F, m), jnp.bfloat16),
+            pltpu.VMEM((2, OWN * LAG_ROWS, 128), jnp.float32),
+            pltpu.VMEM((2, LAGS, OWN, m), jnp.bfloat16),
+            pltpu.SemaphoreType.DMA((2,)),
         ],
-        compiler_params=pltpu.CompilerParams(vmem_limit_bytes=60 * 1024 * 1024),
-    )(places, *row_blocks, *col_blocks, jnp.asarray(lag_table(), jnp.bfloat16))
+        compiler_params=pltpu.CompilerParams(vmem_limit_bytes=56 * 1024 * 1024),
+    )(places, *row_blocks, *col_blocks, tables)
 
 
 def gather8(block, move):

time: 171 us -> 108 us (0.63)
  Pallas kernels: 110 us -> 46.8 us
    pallas_call x1, Pallas kernels: 107 us -> 43.4 us  [correlate(): pl.pallas_call(functools.partial(correlate_kernel, len(row_blocks), len(c...]
  transfers between devices with their start and end apart: 23 -> 23, of which waited for: 7 -> 7; matrix products, arithmetic and copies ran while one was open for 0% -> 1% of each run, Pallas kernels for 0% -> 0%
where the time goes in v2:
time: 108 us
  starting transfers between devices  49.9 us (46%)
  Pallas kernels  46.8 us (43%)
  waiting for transfers between devices  8.26 us (8%)
  local copies, waits for them, and re-layouts  2.58 us (2%)
    pallas_call x1, Pallas kernels, correlate(): pl.pallas_call(functools.partial(correlate_kernel, len(row_blocks), len(c...  43.4 us
    ppermute x7, starting transfers between devices, over_src(): lax.ppermute(value, 'src', [(i, 2 * step(i // 2, ring, side) + i % 2) for...  19.4 us
    ppermute x8, starting transfers between devices, other_core(): return lax.ppermute(value, 'src', [(i, i ^ 1) for i in range(16)])  16.9 us
    ppermute x7, starting transfers between devices, over_rcv(): lax.ppermute(value, 'rcv', [(i, step(i, ring, side)) for i in range(8)])  12 us
    ppermute x7, waiting for transfers between devices, over_rcv(): lax.ppermute(value, 'rcv', [(i, step(i, ring, side)) for i in range(8)])  5.21 us
    pallas_call x1, Pallas kernels, whiten(): pl.pallas_call(whiten_kernel, in_specs=[pl.BlockSpec(memory_space=pltpu.S...  3.39 us
    ppermute x7, waiting for transfers between devices, over_src(): lax.ppermute(value, 'src', [(i, 2 * step(i // 2, ring, side) + i % 2) for...  2.25 us
  transfers between devices with their start and end apart: 23, of which 7 were waited for; matrix products, arithmetic and copies ran while one was open for 1% of the time, Pallas kernels for 0%

profile of v2, /device:TPU:1, one launch (start us, length us, event | category | flops | bytes accessed | tf_op | source)
XLA Modules:
  0.0 107.9 jit_solution(16199978084420154553)
XLA Ops:
  0.0 1.8 %copy.5.spectra_ref = bf16[16,2,10,400]{3,2,1,0:T(8,128)(2,1)} copy(bf16[16,2,10,400]{3,1,2,0:T(2,128)(2,1)} %param.4) | data formatting | bytes 512000 | tf_op args[0]
  1.8 3.4 %shard_map.46.refs_0_ = bf16[16,8064]{1,0:T(8,128)(2,1)} custom-call(s32[16]{0:T(128)} %mask_ref.1, bf16[16,2,10,400]{3,2,1,0:T(8,128)(2,1)} %copy.5.spectra_ref, s32[16,10]{1,0:T(8,128)} %offsets_ref.1), custom_call_target="tpu_custom_call" | custom-call | tf_op jit(solution)/shard_map/pallas_call | solution.py:87
  5.2 1.6 %collective-permute-start.7 = (bf16[16,8064]{1,0:T(8,128)(2,1)}, bf16[16,8064]{1,0:T(8,128)(2,1)S(1)}, u32[]{:S(2)}, u32[]{:S(2)}) collective-permute-start(bf16[16,8064]{1,0:T(8,128)(2,1)} %shard_map.46.refs_0_), channel_id=1, source_target_pairs={{0,0},{1,16},{2,32},{3,48},{4,64},{5,80},{6,96},{7,112},{8,8},{9,2... | collective-permute-start | bytes 774152 | tf_op jit(solution)/shard_map/ppermute | solution.py:285
  6.8 6.3 %collective-permute-start.2 = (bf16[16,8064]{1,0:T(8,128)(2,1)}, bf16[16,8064]{1,0:T(8,128)(2,1)S(1)}, u32[]{:S(2)}, u32[]{:S(2)}) collective-permute-start(bf16[16,8064]{1,0:T(8,128)(2,1)} %shard_map.46.refs_0_), channel_id=1, source_target_pairs={{0,3},{1,0},{2,1},{3,2},{4,7},{5,4},{6,5},{7,6},{8,11},{9,8},{10,9... | collective-permute-start | bytes 774152 | tf_op jit(solution)/shard_map/ppermute | solution.py:276
  13.2 0.0 collective-permute-start.1
  13.2 3.0 %collective-permute-start = (bf16[16,8064]{1,0:T(8,128)(2,1)}, bf16[16,8064]{1,0:T(8,128)(2,1)S(1)}, u32[]{:S(2)}, u32[]{:S(2)}) collective-permute-start(bf16[16,8064]{1,0:T(8,128)(2,1)} %shard_map.46.refs_0_), channel_id=1, source_target_pairs={{0,4},{1,5},{2,6},{3,7},{4,0},{5,1},{6,2},{7,3},{8,12},{9,13},{10,... | collective-permute-start | bytes 774152 | tf_op jit(solution)/shard_map/ppermute | solution.py:276
  16.2 0.0 collective-permute-done.7.refs_8_
  16.2 1.5 %collective-permute-start.15 = (bf16[16,8064]{1,0:T(8,128)(2,1)S(1)}, bf16[16,8064]{1,0:T(8,128)(2,1)S(1)}, u32[]{:S(2)}, u32[]{:S(2)}) collective-permute-start(bf16[16,8064]{1,0:T(8,128)(2,1)S(1)} %collective-permute-done.7.refs_8_), channel_id=1, source_target_pairs={{0,8},{8,0},{16,24},{24,16},{32,40},{40,32},{48,56},{56,48},{64,72... | collective-permute-start | bytes 774152 | tf_op jit(solution)/shard_map/ppermute | solution.py:282
  17.7 11.3 %collective-permute-start.10 = (bf16[16,8064]{1,0:T(8,128)(2,1)S(1)}, bf16[16,8064]{1,0:T(8,128)(2,1)S(1)}, u32[]{:S(2)}, u32[]{:S(2)}) collective-permute-start(bf16[16,8064]{1,0:T(8,128)(2,1)S(1)} %collective-permute-done.7.refs_8_), channel_id=1, source_target_pairs={{0,48},{8,56},{16,0},{24,8},{32,16},{40,24},{48,32},{56,40},{64,11... | collective-permute-start | bytes 774152 | tf_op jit(solution)/shard_map/ppermute | solution.py:279
  29.0 0.0 collective-permute-done.2.refs_3_
  29.0 0.0 collective-permute-start.9
  29.0 1.5 %collective-permute-done.1.refs_2_ = bf16[16,8064]{1,0:T(8,128)(2,1)S(1)} collective-permute-done((bf16[16,8064]{1,0:T(8,128)(2,1)}, bf16[16,8064]{1,0:T(8,128)(2,1)S(1)}, u32[]{:S(2)}, u32[]{:S(2)}) %collective-permute-start.1) | collective-permute-done | bytes 258080 | tf_op jit(solution)/shard_map/ppermute | solution.py:276
  30.5 3.1 %collective-permute-start.8 = (bf16[16,8064]{1,0:T(8,128)(2,1)S(1)}, bf16[16,8064]{1,0:T(8,128)(2,1)S(1)}, u32[]{:S(2)}, u32[]{:S(2)}) collective-permute-start(bf16[16,8064]{1,0:T(8,128)(2,1)S(1)} %collective-permute-done.7.refs_8_), channel_id=1, source_target_pairs={{0,64},{8,72},{16,80},{24,88},{32,96},{40,104},{48,112},{56,120},{... | collective-permute-start | bytes 774152 | tf_op jit(solution)/shard_map/ppermute | solution.py:279
  33.7 0.0 collective-permute-done.refs_1_
  33.7 0.0 collective-permute-start.3
  33.7 0.0 collective-permute-done.15.refs_16_
  33.7 2.7 %collective-permute-start.5 = (bf16[16,8064]{1,0:T(8,128)(2,1)S(1)}, bf16[16,8064]{1,0:T(8,128)(2,1)S(1)}, u32[]{:S(2)}, u32[]{:S(2)}) collective-permute-start(bf16[16,8064]{1,0:T(8,128)(2,1)S(1)} %collective-permute-done.refs_1_), channel_id=1, source_target_pairs={{0,3},{1,0},{2,1},{3,2},{4,7},{5,4},{6,5},{7,6},{8,11},{9,8},{10,9... | collective-permute-start | bytes 774152 | tf_op jit(solution)/shard_map/ppermute | solution.py:276
  36.4 0.0 collective-permute-done.10.refs_11_
  36.4 0.0 collective-permute-start.4
  36.4 1.3 %collective-permute-done.9.refs_10_ = bf16[16,8064]{1,0:T(8,128)(2,1)S(1)} collective-permute-done((bf16[16,8064]{1,0:T(8,128)(2,1)S(1)}, bf16[16,8064]{1,0:T(8,128)(2,1)S(1)}, u32[]{:S(2)}, u32[]{:S(2)}) %collective-permute-start.9) | collective-permute-done | bytes 258080 | tf_op jit(solution)/shard_map/ppermute | solution.py:279
  37.7 1.1 %collective-permute-start.18 = (bf16[16,8064]{1,0:T(8,128)(2,1)S(1)}, bf16[16,8064]{1,0:T(8,128)(2,1)S(1)}, u32[]{:S(2)}, u32[]{:S(2)}) collective-permute-start(bf16[16,8064]{1,0:T(8,128)(2,1)S(1)} %collective-permute-done.10.refs_11_), channel_id=1, source_target_pairs={{0,8},{8,0},{16,24},{24,16},{32,40},{40,32},{48,56},{56,48},{64,72... | collective-permute-start | bytes 774152 | tf_op jit(solution)/shard_map/ppermute | solution.py:282
  38.8 0.3 collective-permute-done.8.refs_9_
  39.1 0.0 collective-permute-start.11
  39.1 2.2 %collective-permute-done.3.refs_4_ = bf16[16,8064]{1,0:T(8,128)(2,1)S(1)} collective-permute-done((bf16[16,8064]{1,0:T(8,128)(2,1)S(1)}, bf16[16,8064]{1,0:T(8,128)(2,1)S(1)}, u32[]{:S(2)}, u32[]{:S(2)}) %collective-permute-start.3) | collective-permute-done | bytes 258080 | tf_op jit(solution)/shard_map/ppermute | solution.py:276
  41.3 4.0 %collective-permute-start.17 = (bf16[16,8064]{1,0:T(8,128)(2,1)S(1)}, bf16[16,8064]{1,0:T(8,128)(2,1)S(1)}, u32[]{:S(2)}, u32[]{:S(2)}) collective-permute-start(bf16[16,8064]{1,0:T(8,128)(2,1)S(1)} %collective-permute-done.9.refs_10_), channel_id=1, source_target_pairs={{0,8},{8,0},{16,24},{24,16},{32,40},{40,32},{48,56},{56,48},{64,72... | collective-permute-start | bytes 774152 | tf_op jit(solution)/shard_map/ppermute | solution.py:282
  45.3 0.0 collective-permute-done.5.refs_6_
  45.3 0.1 collective-permute-start.16
  45.4 1.5 %collective-permute-done.4.refs_5_ = bf16[16,8064]{1,0:T(8,128)(2,1)S(1)} collective-permute-done((bf16[16,8064]{1,0:T(8,128)(2,1)S(1)}, bf16[16,8064]{1,0:T(8,128)(2,1)S(1)}, u32[]{:S(2)}, u32[]{:S(2)}) %collective-permute-start.4) | collective-permute-done | bytes 258080 | tf_op jit(solution)/shard_map/ppermute | solution.py:276
  46.9 2.9 %collective-permute-start.13 = (bf16[16,8064]{1,0:T(8,128)(2,1)S(1)}, bf16[16,8064]{1,0:T(8,128)(2,1)}, u32[]{:S(2)}, u32[]{:S(2)}) collective-permute-start(bf16[16,8064]{1,0:T(8,128)(2,1)S(1)} %collective-permute-done.8.refs_9_), channel_id=1, source_target_pairs={{0,48},{8,56},{16,0},{24,8},{32,16},{40,24},{48,32},{56,40},{64,11... | collective-permute-start | bytes 774152 | tf_op jit(solution)/shard_map/ppermute | solution.py:279
  49.8 0.0 collective-permute-done.18.refs_19_
  49.8 0.0 collective-permute-start.12
  49.8 0.0 collective-permute-done.11.refs_12_
  49.8 2.0 %collective-permute-start.14 = (bf16[16,8064]{1,0:T(8,128)(2,1)S(1)}, bf16[16,8064]{1,0:T(8,128)(2,1)}, u32[]{:S(2)}, u32[]{:S(2)}) collective-permute-start(bf16[16,8064]{1,0:T(8,128)(2,1)S(1)} %collective-permute-done.11.refs_12_), channel_id=1, source_target_pairs={{0,64},{8,72},{16,80},{24,88},{32,96},{40,104},{48,112},{56,120},{... | collective-permute-start | bytes 774152 | tf_op jit(solution)/shard_map/ppermute | solution.py:279
  51.8 0.0 collective-permute-done.17.refs_18_
  51.8 0.0 collective-permute-start.6
  51.8 0.0 collective-permute-done.16.refs_17_
  51.9 2.6 %collective-permute-start.19 = (bf16[16,8064]{1,0:T(8,128)(2,1)S(1)}, bf16[16,8064]{1,0:T(8,128)(2,1)}, u32[]{:S(2)}, u32[]{:S(2)}) collective-permute-start(bf16[16,8064]{1,0:T(8,128)(2,1)S(1)} %collective-permute-done.11.refs_12_), channel_id=1, source_target_pairs={{0,8},{8,0},{16,24},{24,16},{32,40},{40,32},{48,56},{56,48},{64,72... | collective-permute-start | bytes 774152 | tf_op jit(solution)/shard_map/ppermute | solution.py:282
  54.5 0.0 collective-permute-done.13.refs_14_
  54.5 1.7 %collective-permute-start.21 = (bf16[16,8064]{1,0:T(8,128)(2,1)}, bf16[16,8064]{1,0:T(8,128)(2,1)}, u32[]{:S(2)}, u32[]{:S(2)}) collective-permute-start(bf16[16,8064]{1,0:T(8,128)(2,1)} %collective-permute-done.13.refs_14_), channel_id=1, source_target_pairs={{0,8},{8,0},{16,24},{24,16},{32,40},{40,32},{48,56},{56,48},{64,72... | collective-permute-start | bytes 774152 | tf_op jit(solution)/shard_map/ppermute | solution.py:282
  56.2 0.6 collective-permute-done.12.refs_13_
  56.8 2.9 %collective-permute-start.20 = (bf16[16,8064]{1,0:T(8,128)(2,1)}, bf16[16,8064]{1,0:T(8,128)(2,1)}, u32[]{:S(2)}, u32[]{:S(2)}) collective-permute-start(bf16[16,8064]{1,0:T(8,128)(2,1)} %collective-permute-done.12.refs_13_), channel_id=1, source_target_pairs={{0,8},{8,0},{16,24},{24,16},{32,40},{40,32},{48,56},{56,48},{64,72... | collective-permute-start | bytes 774152 | tf_op jit(solution)/shard_map/ppermute | solution.py:282
  59.7 0.0 collective-permute-done.14.refs_15_
  59.8 2.9 %collective-permute-start.22 = (bf16[16,8064]{1,0:T(8,128)(2,1)}, bf16[16,8064]{1,0:T(8,128)(2,1)}, u32[]{:S(2)}, u32[]{:S(2)}) collective-permute-start(bf16[16,8064]{1,0:T(8,128)(2,1)} %collective-permute-done.14.refs_15_), channel_id=1, source_target_pairs={{0,8},{8,0},{16,24},{24,16},{32,40},{40,32},{48,56},{56,48},{64,72... | collective-permute-start | bytes 774152 | tf_op jit(solution)/shard_map/ppermute | solution.py:282
  62.7 0.7 stack.99.place_ref
  63.4 0.0 collective-permute-done.6.refs_7_
  63.4 0.0 collective-permute-done.21.refs_22_
  63.4 0.8 collective-permute-done.22.refs_23_
  64.3 43.4 %shard_map.47 = bf16[101,128,256]{2,1,0:T(8,128)(2,1)} custom-call(s32[24]{0:T(128)} %stack.99.place_ref, bf16[16,8064]{1,0:T(8,128)(2,1)} %shard_map.46.refs_0_, bf16[16,8064]{1,0:T(8,128)(2,1)} %copy-done.3, bf16[16,8064]{1,0:T(8,128)(2,1)} %copy-done.2, bf16[16,8064]{1,0:T(8,128)(2,1)} %copy-done.1, bf16[16,8064]{1,0:T(8,128)(2,1)} %copy-done.8, ...), custom_call_target="tpu_custom_call" | custom-call | tf_op jit(solution)/shard_map/pallas_call | solution.py:239
  (32 shorter events, 0.1 us)
Async XLA Ops:
  5.2 10.9 %collective-permute-start.7 = (bf16[16,8064]{1,0:T(8,128)(2,1)}, bf16[16,8064]{1,0:T(8,128)(2,1)S(1)}, u32[]{:S(2)}, u32[]{:S(2)}) collective-permute-start(bf16[16,8064]{1,0:T(8,128)(2,1)} %shard_map.46.refs_0_), channel_id=1, source_target_pairs={{0,0},{1,16},{2,32},{3,48},{4,64},{5,80},{6,96},{7,112},{8,8},{9,2... | collective-permute-start | bytes 774152 | tf_op jit(solution)/shard_map/ppermute | solution.py:285
  6.8 22.1 %collective-permute-start.2 = (bf16[16,8064]{1,0:T(8,128)(2,1)}, bf16[16,8064]{1,0:T(8,128)(2,1)S(1)}, u32[]{:S(2)}, u32[]{:S(2)}) collective-permute-start(bf16[16,8064]{1,0:T(8,128)(2,1)} %shard_map.46.refs_0_), channel_id=1, source_target_pairs={{0,3},{1,0},{2,1},{3,2},{4,7},{5,4},{6,5},{7,6},{8,11},{9,8},{10,9... | collective-permute-start | bytes 774152 | tf_op jit(solution)/shard_map/ppermute | solution.py:276
  13.2 17.4 %collective-permute-start.1 = (bf16[16,8064]{1,0:T(8,128)(2,1)}, bf16[16,8064]{1,0:T(8,128)(2,1)S(1)}, u32[]{:S(2)}, u32[]{:S(2)}) collective-permute-start(bf16[16,8064]{1,0:T(8,128)(2,1)} %shard_map.46.refs_0_), channel_id=1, source_target_pairs={{0,1},{1,2},{2,3},{3,0},{4,5},{5,6},{6,7},{7,4},{8,9},{9,10},{10,1... | collective-permute-start | bytes 774152 | tf_op jit(solution)/shard_map/ppermute | solution.py:276
  13.2 20.5 %collective-permute-start = (bf16[16,8064]{1,0:T(8,128)(2,1)}, bf16[16,8064]{1,0:T(8,128)(2,1)S(1)}, u32[]{:S(2)}, u32[]{:S(2)}) collective-permute-start(bf16[16,8064]{1,0:T(8,128)(2,1)} %shard_map.46.refs_0_), channel_id=1, source_target_pairs={{0,4},{1,5},{2,6},{3,7},{4,0},{5,1},{6,2},{7,3},{8,12},{9,13},{10,... | collective-permute-start | bytes 774152 | tf_op jit(solution)/shard_map/ppermute | solution.py:276
  16.2 48.0 %copy-start = (bf16[16,8064]{1,0:T(8,128)(2,1)}, bf16[16,8064]{1,0:T(8,128)(2,1)S(1)}, u32[]{:S(2)}) copy-start(bf16[16,8064]{1,0:T(8,128)(2,1)S(1)} %collective-permute-done.7.refs_8_) | copy-start | bytes 774148
  16.2 17.5 %collective-permute-start.15 = (bf16[16,8064]{1,0:T(8,128)(2,1)S(1)}, bf16[16,8064]{1,0:T(8,128)(2,1)S(1)}, u32[]{:S(2)}, u32[]{:S(2)}) collective-permute-start(bf16[16,8064]{1,0:T(8,128)(2,1)S(1)} %collective-permute-done.7.refs_8_), channel_id=1, source_target_pairs={{0,8},{8,0},{16,24},{24,16},{32,40},{40,32},{48,56},{56,48},{64,72... | collective-permute-start | bytes 774152 | tf_op jit(solution)/shard_map/ppermute | solution.py:282
  17.7 18.7 %collective-permute-start.10 = (bf16[16,8064]{1,0:T(8,128)(2,1)S(1)}, bf16[16,8064]{1,0:T(8,128)(2,1)S(1)}, u32[]{:S(2)}, u32[]{:S(2)}) collective-permute-start(bf16[16,8064]{1,0:T(8,128)(2,1)S(1)} %collective-permute-done.7.refs_8_), channel_id=1, source_target_pairs={{0,48},{8,56},{16,0},{24,8},{32,16},{40,24},{48,32},{56,40},{64,11... | collective-permute-start | bytes 774152 | tf_op jit(solution)/shard_map/ppermute | solution.py:279
  29.0 35.2 %copy-start.1 = (bf16[16,8064]{1,0:T(8,128)(2,1)}, bf16[16,8064]{1,0:T(8,128)(2,1)S(1)}, u32[]{:S(2)}) copy-start(bf16[16,8064]{1,0:T(8,128)(2,1)S(1)} %collective-permute-done.2.refs_3_) | copy-start | bytes 774148
  29.0 8.7 %collective-permute-start.9 = (bf16[16,8064]{1,0:T(8,128)(2,1)S(1)}, bf16[16,8064]{1,0:T(8,128)(2,1)S(1)}, u32[]{:S(2)}, u32[]{:S(2)}) collective-permute-start(bf16[16,8064]{1,0:T(8,128)(2,1)S(1)} %collective-permute-done.7.refs_8_), channel_id=1, source_target_pairs={{0,16},{8,24},{16,32},{24,40},{32,48},{40,56},{48,0},{56,8},{64,80... | collective-permute-start | bytes 774152 | tf_op jit(solution)/shard_map/ppermute | solution.py:279
  30.5 33.7 %copy-start.2 = (bf16[16,8064]{1,0:T(8,128)(2,1)}, bf16[16,8064]{1,0:T(8,128)(2,1)S(1)}, u32[]{:S(2)}) copy-start(bf16[16,8064]{1,0:T(8,128)(2,1)S(1)} %collective-permute-done.1.refs_2_) | copy-start | bytes 774148
  30.5 8.6 %collective-permute-start.8 = (bf16[16,8064]{1,0:T(8,128)(2,1)S(1)}, bf16[16,8064]{1,0:T(8,128)(2,1)S(1)}, u32[]{:S(2)}, u32[]{:S(2)}) collective-permute-start(bf16[16,8064]{1,0:T(8,128)(2,1)S(1)} %collective-permute-done.7.refs_8_), channel_id=1, source_target_pairs={{0,64},{8,72},{16,80},{24,88},{32,96},{40,104},{48,112},{56,120},{... | collective-permute-start | bytes 774152 | tf_op jit(solution)/shard_map/ppermute | solution.py:279
  33.7 30.5 %copy-start.3 = (bf16[16,8064]{1,0:T(8,128)(2,1)}, bf16[16,8064]{1,0:T(8,128)(2,1)S(1)}, u32[]{:S(2)}) copy-start(bf16[16,8064]{1,0:T(8,128)(2,1)S(1)} %collective-permute-done.refs_1_) | copy-start | bytes 774148
  33.7 7.7 %collective-permute-start.3 = (bf16[16,8064]{1,0:T(8,128)(2,1)S(1)}, bf16[16,8064]{1,0:T(8,128)(2,1)S(1)}, u32[]{:S(2)}, u32[]{:S(2)}) collective-permute-start(bf16[16,8064]{1,0:T(8,128)(2,1)S(1)} %collective-permute-done.1.refs_2_), channel_id=1, source_target_pairs={{0,1},{1,2},{2,3},{3,0},{4,5},{5,6},{6,7},{7,4},{8,9},{9,10},{10,1... | collective-permute-start | bytes 774152 | tf_op jit(solution)/shard_map/ppermute | solution.py:276
  33.7 30.5 %copy-start.4 = (bf16[16,8064]{1,0:T(8,128)(2,1)}, bf16[16,8064]{1,0:T(8,128)(2,1)S(1)}, u32[]{:S(2)}) copy-start(bf16[16,8064]{1,0:T(8,128)(2,1)S(1)} %collective-permute-done.15.refs_16_) | copy-start | bytes 774148
  33.7 11.6 %collective-permute-start.5 = (bf16[16,8064]{1,0:T(8,128)(2,1)S(1)}, bf16[16,8064]{1,0:T(8,128)(2,1)S(1)}, u32[]{:S(2)}, u32[]{:S(2)}) collective-permute-start(bf16[16,8064]{1,0:T(8,128)(2,1)S(1)} %collective-permute-done.refs_1_), channel_id=1, source_target_pairs={{0,3},{1,0},{2,1},{3,2},{4,7},{5,4},{6,5},{7,6},{8,11},{9,8},{10,9... | collective-permute-start | bytes 774152 | tf_op jit(solution)/shard_map/ppermute | solution.py:276
  36.4 27.9 %copy-start.5 = (bf16[16,8064]{1,0:T(8,128)(2,1)}, bf16[16,8064]{1,0:T(8,128)(2,1)S(1)}, u32[]{:S(2)}) copy-start(bf16[16,8064]{1,0:T(8,128)(2,1)S(1)} %collective-permute-done.10.refs_11_) | copy-start | bytes 774148
  36.4 10.5 %collective-permute-start.4 = (bf16[16,8064]{1,0:T(8,128)(2,1)S(1)}, bf16[16,8064]{1,0:T(8,128)(2,1)S(1)}, u32[]{:S(2)}, u32[]{:S(2)}) collective-permute-start(bf16[16,8064]{1,0:T(8,128)(2,1)S(1)} %collective-permute-done.refs_1_), channel_id=1, source_target_pairs={{0,1},{1,2},{2,3},{3,0},{4,5},{5,6},{6,7},{7,4},{8,9},{9,10},{10,1... | collective-permute-start | bytes 774152 | tf_op jit(solution)/shard_map/ppermute | solution.py:276
  37.7 26.5 %copy-start.6 = (bf16[16,8064]{1,0:T(8,128)(2,1)}, bf16[16,8064]{1,0:T(8,128)(2,1)S(1)}, u32[]{:S(2)}) copy-start(bf16[16,8064]{1,0:T(8,128)(2,1)S(1)} %collective-permute-done.9.refs_10_) | copy-start | bytes 774148
  37.7 12.1 %collective-permute-start.18 = (bf16[16,8064]{1,0:T(8,128)(2,1)S(1)}, bf16[16,8064]{1,0:T(8,128)(2,1)S(1)}, u32[]{:S(2)}, u32[]{:S(2)}) collective-permute-start(bf16[16,8064]{1,0:T(8,128)(2,1)S(1)} %collective-permute-done.10.refs_11_), channel_id=1, source_target_pairs={{0,8},{8,0},{16,24},{24,16},{32,40},{40,32},{48,56},{56,48},{64,72... | collective-permute-start | bytes 774152 | tf_op jit(solution)/shard_map/ppermute | solution.py:282
  39.1 25.1 %copy-start.7 = (bf16[16,8064]{1,0:T(8,128)(2,1)}, bf16[16,8064]{1,0:T(8,128)(2,1)S(1)}, u32[]{:S(2)}) copy-start(bf16[16,8064]{1,0:T(8,128)(2,1)S(1)} %collective-permute-done.8.refs_9_) | copy-start | bytes 774148
  39.1 10.7 %collective-permute-start.11 = (bf16[16,8064]{1,0:T(8,128)(2,1)S(1)}, bf16[16,8064]{1,0:T(8,128)(2,1)S(1)}, u32[]{:S(2)}, u32[]{:S(2)}) collective-permute-start(bf16[16,8064]{1,0:T(8,128)(2,1)S(1)} %collective-permute-done.9.refs_10_), channel_id=1, source_target_pairs={{0,16},{8,24},{16,32},{24,40},{32,48},{40,56},{48,0},{56,8},{64,80... | collective-permute-start | bytes 774152 | tf_op jit(solution)/shard_map/ppermute | solution.py:279
  41.3 22.9 %copy-start.8 = (bf16[16,8064]{1,0:T(8,128)(2,1)}, bf16[16,8064]{1,0:T(8,128)(2,1)S(1)}, u32[]{:S(2)}) copy-start(bf16[16,8064]{1,0:T(8,128)(2,1)S(1)} %collective-permute-done.3.refs_4_) | copy-start | bytes 774148
  41.3 10.5 %collective-permute-start.17 = (bf16[16,8064]{1,0:T(8,128)(2,1)S(1)}, bf16[16,8064]{1,0:T(8,128)(2,1)S(1)}, u32[]{:S(2)}, u32[]{:S(2)}) collective-permute-start(bf16[16,8064]{1,0:T(8,128)(2,1)S(1)} %collective-permute-done.9.refs_10_), channel_id=1, source_target_pairs={{0,8},{8,0},{16,24},{24,16},{32,40},{40,32},{48,56},{56,48},{64,72... | collective-permute-start | bytes 774152 | tf_op jit(solution)/shard_map/ppermute | solution.py:282
  45.3 18.9 %copy-start.9 = (bf16[16,8064]{1,0:T(8,128)(2,1)}, bf16[16,8064]{1,0:T(8,128)(2,1)S(1)}, u32[]{:S(2)}) copy-start(bf16[16,8064]{1,0:T(8,128)(2,1)S(1)} %collective-permute-done.5.refs_6_) | copy-start | bytes 774148
  45.3 6.5 %collective-permute-start.16 = (bf16[16,8064]{1,0:T(8,128)(2,1)S(1)}, bf16[16,8064]{1,0:T(8,128)(2,1)S(1)}, u32[]{:S(2)}, u32[]{:S(2)}) collective-permute-start(bf16[16,8064]{1,0:T(8,128)(2,1)S(1)} %collective-permute-done.8.refs_9_), channel_id=1, source_target_pairs={{0,8},{8,0},{16,24},{24,16},{32,40},{40,32},{48,56},{56,48},{64,72... | collective-permute-start | bytes 774152 | tf_op jit(solution)/shard_map/ppermute | solution.py:282
  46.9 17.4 %copy-start.10 = (bf16[16,8064]{1,0:T(8,128)(2,1)}, bf16[16,8064]{1,0:T(8,128)(2,1)S(1)}, u32[]{:S(2)}) copy-start(bf16[16,8064]{1,0:T(8,128)(2,1)S(1)} %collective-permute-done.4.refs_5_) | copy-start | bytes 774148
  46.9 7.6 %collective-permute-start.13 = (bf16[16,8064]{1,0:T(8,128)(2,1)S(1)}, bf16[16,8064]{1,0:T(8,128)(2,1)}, u32[]{:S(2)}, u32[]{:S(2)}) collective-permute-start(bf16[16,8064]{1,0:T(8,128)(2,1)S(1)} %collective-permute-done.8.refs_9_), channel_id=1, source_target_pairs={{0,48},{8,56},{16,0},{24,8},{32,16},{40,24},{48,32},{56,40},{64,11... | collective-permute-start | bytes 774152 | tf_op jit(solution)/shard_map/ppermute | solution.py:279
  49.8 14.5 %copy-start.11 = (bf16[16,8064]{1,0:T(8,128)(2,1)}, bf16[16,8064]{1,0:T(8,128)(2,1)S(1)}, u32[]{:S(2)}) copy-start(bf16[16,8064]{1,0:T(8,128)(2,1)S(1)} %collective-permute-done.18.refs_19_) | copy-start | bytes 774148
  49.8 7.0 %collective-permute-start.12 = (bf16[16,8064]{1,0:T(8,128)(2,1)S(1)}, bf16[16,8064]{1,0:T(8,128)(2,1)}, u32[]{:S(2)}, u32[]{:S(2)}) collective-permute-start(bf16[16,8064]{1,0:T(8,128)(2,1)S(1)} %collective-permute-done.8.refs_9_), channel_id=1, source_target_pairs={{0,16},{8,24},{16,32},{24,40},{32,48},{40,56},{48,0},{56,8},{64,80... | collective-permute-start | bytes 774152 | tf_op jit(solution)/shard_map/ppermute | solution.py:279
  49.8 14.5 %copy-start.12 = (bf16[16,8064]{1,0:T(8,128)(2,1)}, bf16[16,8064]{1,0:T(8,128)(2,1)S(1)}, u32[]{:S(2)}) copy-start(bf16[16,8064]{1,0:T(8,128)(2,1)S(1)} %collective-permute-done.11.refs_12_) | copy-start | bytes 774148
  49.8 9.9 %collective-permute-start.14 = (bf16[16,8064]{1,0:T(8,128)(2,1)S(1)}, bf16[16,8064]{1,0:T(8,128)(2,1)}, u32[]{:S(2)}, u32[]{:S(2)}) collective-permute-start(bf16[16,8064]{1,0:T(8,128)(2,1)S(1)} %collective-permute-done.11.refs_12_), channel_id=1, source_target_pairs={{0,64},{8,72},{16,80},{24,88},{32,96},{40,104},{48,112},{56,120},{... | collective-permute-start | bytes 774152 | tf_op jit(solution)/shard_map/ppermute | solution.py:279
  51.8 7.9 %copy-start.13 = (bf16[16,8064]{1,0:T(8,128)(2,1)}, bf16[16,8064]{1,0:T(8,128)(2,1)S(1)}, u32[]{:S(2)}) copy-start(bf16[16,8064]{1,0:T(8,128)(2,1)S(1)} %collective-permute-done.17.refs_18_) | copy-start | bytes 774148
  51.8 11.5 %collective-permute-start.6 = (bf16[16,8064]{1,0:T(8,128)(2,1)S(1)}, bf16[16,8064]{1,0:T(8,128)(2,1)}, u32[]{:S(2)}, u32[]{:S(2)}) collective-permute-start(bf16[16,8064]{1,0:T(8,128)(2,1)S(1)} %collective-permute-done.3.refs_4_), channel_id=1, source_target_pairs={{0,4},{1,5},{2,6},{3,7},{4,0},{5,1},{6,2},{7,3},{8,12},{9,13},{10,... | collective-permute-start | bytes 774152 | tf_op jit(solution)/shard_map/ppermute | solution.py:276
  51.8 10.8 %copy-start.14 = (bf16[16,8064]{1,0:T(8,128)(2,1)}, bf16[16,8064]{1,0:T(8,128)(2,1)S(1)}, u32[]{:S(2)}) copy-start(bf16[16,8064]{1,0:T(8,128)(2,1)S(1)} %collective-permute-done.16.refs_17_) | copy-start | bytes 774148
  51.9 11.5 %collective-permute-start.19 = (bf16[16,8064]{1,0:T(8,128)(2,1)S(1)}, bf16[16,8064]{1,0:T(8,128)(2,1)}, u32[]{:S(2)}, u32[]{:S(2)}) collective-permute-start(bf16[16,8064]{1,0:T(8,128)(2,1)S(1)} %collective-permute-done.11.refs_12_), channel_id=1, source_target_pairs={{0,8},{8,0},{16,24},{24,16},{32,40},{40,32},{48,56},{56,48},{64,72... | collective-permute-start | bytes 774152 | tf_op jit(solution)/shard_map/ppermute | solution.py:282
  54.5 8.9 %collective-permute-start.21 = (bf16[16,8064]{1,0:T(8,128)(2,1)}, bf16[16,8064]{1,0:T(8,128)(2,1)}, u32[]{:S(2)}, u32[]{:S(2)}) collective-permute-start(bf16[16,8064]{1,0:T(8,128)(2,1)} %collective-permute-done.13.refs_14_), channel_id=1, source_target_pairs={{0,8},{8,0},{16,24},{24,16},{32,40},{40,32},{48,56},{56,48},{64,72... | collective-permute-start | bytes 774152 | tf_op jit(solution)/shard_map/ppermute | solution.py:282
  56.8 6.6 %collective-permute-start.20 = (bf16[16,8064]{1,0:T(8,128)(2,1)}, bf16[16,8064]{1,0:T(8,128)(2,1)}, u32[]{:S(2)}, u32[]{:S(2)}) collective-permute-start(bf16[16,8064]{1,0:T(8,128)(2,1)} %collective-permute-done.12.refs_13_), channel_id=1, source_target_pairs={{0,8},{8,0},{16,24},{24,16},{32,40},{40,32},{48,56},{56,48},{64,72... | collective-permute-start | bytes 774152 | tf_op jit(solution)/shard_map/ppermute | solution.py:282
  59.8 4.4 %collective-permute-start.22 = (bf16[16,8064]{1,0:T(8,128)(2,1)}, bf16[16,8064]{1,0:T(8,128)(2,1)}, u32[]{:S(2)}, u32[]{:S(2)}) collective-permute-start(bf16[16,8064]{1,0:T(8,128)(2,1)} %collective-permute-done.14.refs_15_), channel_id=1, source_target_pairs={{0,8},{8,0},{16,24},{24,16},{32,40},{40,32},{48,56},{56,48},{64,72... | collective-permute-start | bytes 774152 | tf_op jit(solution)/shard_map/ppermute | solution.py:282

commit v3 on v2

--- a/solution.py
+++ b/solution.py
@@ -253,14 +253,12 @@
 
 
 def gather8(block, move):
-    side = move(block, 0, 1)
-    found = {(0, 0): block, (0, 1): side}
-    found[-1, 0] = move(block, 1, 0)
-    found[1, 0] = move(block, -1, 0)
-    found[2, 0] = move(found[-1, 0], 1, 0)
+    side, before, after = move(block, 0, 1), move(block, 1, 0), move(block, -1, 0)
+    found = {(0, 0): block, (0, 1): side, (-1, 0): before, (1, 0): after}
     found[-1, 1] = move(side, 1, 0)
     found[1, 1] = move(side, -1, 0)
-    found[2, 1] = move(found[2, 0], 0, 1)
+    found[2, 0] = move(before, 1, 0)
+    found[2, 1] = move(after, -1, 1)
     return found
 
 
@@ -281,14 +279,17 @@
     def other_core(value):
         return lax.ppermute(value, "src", [(i, i ^ 1) for i in range(16)])
 
-    flip = [((i * 2 + k) * 8 + j, (j * 2 + k) * 8 + i) for i in range(8) for k in range(2) for j in range(8)]
+    flip = [
+        ((i * 2 + k) * 8 + step(j, 2, 0), (j * 2 + k) * 8 + i) for i in range(8) for k in range(2) for j in range(8)
+    ]
     turned = lax.ppermute(white, ("src", "rcv"), flip)
+    white, turned = lax.optimization_barrier((white, turned))
     rows = gather8(white, over_rcv)
     cols = gather8(turned, over_src)
     swapped = {key: other_core(value) for key, value in cols.items()}
     places = [step(p, *key) for key in rows]
-    places += [core * 8 + step(q, *key) for key in cols]
-    places += [(1 - core) * 8 + step(q, *key) for key in swapped]
+    places += [core * 8 + step(step(q, *key), 2, 0) for key in cols]
+    places += [(1 - core) * 8 + step(step(q, *key), 2, 0) for key in swapped]
     places = jnp.stack(places).astype(jnp.int32)
     return correlate(places, list(rows.values()), list(cols.values()) + list(swapped.values()))
 

time: 108 us -> 114 us (1.056)
  waiting for transfers between devices: 8.26 us -> 22.6 us
  starting transfers between devices: 49.9 us -> 41.9 us
    ppermute x7, waiting for transfers between devices: 2.25 us -> 16.2 us  [over_src(): lax.ppermute(value, 'src', [(i, 2 * step(i // 2, ring, side) + i % 2) for...]
    ppermute x8, starting transfers between devices: 16.9 us -> 7.53 us  [other_core(): return lax.ppermute(value, 'src', [(i, i ^ 1) for i in range(16)])]
    ppermute x1, waiting for transfers between devices: 0.01 us -> 5.54 us  [body(): turned = lax.ppermute(white, ('src', 'rcv'), flip)]
    ppermute x7, waiting for transfers between devices: 5.21 us -> 0.02 us  [over_rcv(): lax.ppermute(value, 'rcv', [(i, step(i, ring, side)) for i in range(8)])]
    ppermute x7, starting transfers between devices: 19.4 us -> 17.2 us  [over_src(): lax.ppermute(value, 'src', [(i, 2 * step(i // 2, ring, side) + i % 2) for...]
    ppermute x1, starting transfers between devices: 1.59 us -> 3.74 us  [body(): turned = lax.ppermute(white, ('src', 'rcv'), flip)]
    ppermute x7, starting transfers between devices: 12 us -> 13.4 us  [over_rcv(): lax.ppermute(value, 'rcv', [(i, step(i, ring, side)) for i in range(8)])]
  transfers between devices with their start and end apart: 23 -> 23, of which waited for: 7 -> 6; matrix products, arithmetic and copies ran while one was open for 1% -> 1% of each run, Pallas kernels for 0% -> 0%
where the time goes in v3:
time: 114 us
  Pallas kernels  46.8 us (41%)
  starting transfers between devices  41.9 us (37%)
  waiting for transfers between devices  22.6 us (20%)
  local copies, waits for them, and re-layouts  2.52 us (2%)
    pallas_call x1, Pallas kernels, correlate(): pl.pallas_call(functools.partial(correlate_kernel, len(row_blocks), len(c...  43.4 us
    ppermute x7, starting transfers between devices, over_src(): lax.ppermute(value, 'src', [(i, 2 * step(i // 2, ring, side) + i % 2) for...  17.2 us
    ppermute x7, waiting for transfers between devices, over_src(): lax.ppermute(value, 'src', [(i, 2 * step(i // 2, ring, side) + i % 2) for...  16.2 us
    ppermute x7, starting transfers between devices, over_rcv(): lax.ppermute(value, 'rcv', [(i, step(i, ring, side)) for i in range(8)])  13.4 us
    ppermute x8, starting transfers between devices, other_core(): return lax.ppermute(value, 'src', [(i, i ^ 1) for i in range(16)])  7.53 us
    ppermute x1, waiting for transfers between devices, body(): turned = lax.ppermute(white, ('src', 'rcv'), flip)  5.54 us
    ppermute x1, starting transfers between devices, body(): turned = lax.ppermute(white, ('src', 'rcv'), flip)  3.74 us
    pallas_call x1, Pallas kernels, whiten(): pl.pallas_call(whiten_kernel, in_specs=[pl.BlockSpec(memory_space=pltpu.S...  3.39 us
  transfers between devices with their start and end apart: 23, of which 6 were waited for; matrix products, arithmetic and copies ran while one was open for 1% of the time, Pallas kernels for 0%

profile of v3, /device:TPU:1, one launch (start us, length us, event | category | flops | bytes accessed | tf_op | source)
XLA Modules:
  0.0 114.2 jit_solution(333782317419384207)
XLA Ops:
  0.0 1.8 %copy.5.spectra_ref = bf16[16,2,10,400]{3,2,1,0:T(8,128)(2,1)} copy(bf16[16,2,10,400]{3,1,2,0:T(2,128)(2,1)} %param.4) | data formatting | bytes 512000 | tf_op args[0]
  1.8 3.4 %shard_map.46.refs_0_ = bf16[16,8064]{1,0:T(8,128)(2,1)} custom-call(s32[16]{0:T(128)} %mask_ref.1, bf16[16,2,10,400]{3,2,1,0:T(8,128)(2,1)} %copy.5.spectra_ref, s32[16,10]{1,0:T(8,128)} %offsets_ref.1), custom_call_target="tpu_custom_call" | custom-call | tf_op jit(solution)/shard_map/pallas_call | solution.py:87
  5.2 3.7 %collective-permute-start = (bf16[16,8064]{1,0:T(8,128)(2,1)}, bf16[16,8064]{1,0:T(8,128)(2,1)S(1)}, u32[]{:S(2)}, u32[]{:S(2)}) collective-permute-start(bf16[16,8064]{1,0:T(8,128)(2,1)} %shard_map.46.refs_0_), channel_id=1, source_target_pairs={{2,0},{3,16},{0,32},{1,48},{6,64},{7,80},{4,96},{5,112},{10,8},{11... | collective-permute-start | bytes 774152 | tf_op jit(solution)/shard_map/ppermute | solution.py:285
  9.0 5.5 %collective-permute-done.refs_8_ = bf16[16,8064]{1,0:T(8,128)(2,1)S(1)} collective-permute-done((bf16[16,8064]{1,0:T(8,128)(2,1)}, bf16[16,8064]{1,0:T(8,128)(2,1)S(1)}, u32[]{:S(2)}, u32[]{:S(2)}) %collective-permute-start) | collective-permute-done | bytes 258080 | tf_op jit(solution)/shard_map/ppermute | solution.py:285
  14.5 6.1 %collective-permute-start.3 = (bf16[16,8064]{1,0:T(8,128)(2,1)}, bf16[16,8064]{1,0:T(8,128)(2,1)S(1)}, u32[]{:S(2)}, u32[]{:S(2)}) collective-permute-start(bf16[16,8064]{1,0:T(8,128)(2,1)} %shard_map.46.refs_0_), channel_id=1, source_target_pairs={{0,3},{1,0},{2,1},{3,2},{4,7},{5,4},{6,5},{7,6},{8,11},{9,8},{10,9... | collective-permute-start | bytes 774152 | tf_op jit(solution)/shard_map/ppermute | solution.py:274
  20.6 0.4 collective-permute-start.2
  21.0 3.2 %collective-permute-start.1 = (bf16[16,8064]{1,0:T(8,128)(2,1)}, bf16[16,8064]{1,0:T(8,128)(2,1)S(1)}, u32[]{:S(2)}, u32[]{:S(2)}) collective-permute-start(bf16[16,8064]{1,0:T(8,128)(2,1)} %shard_map.46.refs_0_), channel_id=1, source_target_pairs={{0,4},{1,5},{2,6},{3,7},{4,0},{5,1},{6,2},{7,3},{8,12},{9,13},{10,... | collective-permute-start | bytes 774152 | tf_op jit(solution)/shard_map/ppermute | solution.py:274
  24.2 1.8 %collective-permute-start.15 = (bf16[16,8064]{1,0:T(8,128)(2,1)S(1)}, bf16[16,8064]{1,0:T(8,128)(2,1)S(1)}, u32[]{:S(2)}, u32[]{:S(2)}) collective-permute-start(bf16[16,8064]{1,0:T(8,128)(2,1)S(1)} %collective-permute-done.refs_8_), channel_id=1, source_target_pairs={{0,8},{8,0},{16,24},{24,16},{32,40},{40,32},{48,56},{56,48},{64,72... | collective-permute-start | bytes 774152 | tf_op jit(solution)/shard_map/ppermute | solution.py:280
  26.0 3.1 %collective-permute-start.10 = (bf16[16,8064]{1,0:T(8,128)(2,1)S(1)}, bf16[16,8064]{1,0:T(8,128)(2,1)S(1)}, u32[]{:S(2)}, u32[]{:S(2)}) collective-permute-start(bf16[16,8064]{1,0:T(8,128)(2,1)S(1)} %collective-permute-done.refs_8_), channel_id=1, source_target_pairs={{0,48},{8,56},{16,0},{24,8},{32,16},{40,24},{48,32},{56,40},{64,11... | collective-permute-start | bytes 774152 | tf_op jit(solution)/shard_map/ppermute | solution.py:277
  29.0 0.0 collective-permute-done.3.refs_3_
  29.0 0.8 collective-permute-start.9
  29.9 0.0 collective-permute-done.2.refs_2_
  29.9 4.7 %collective-permute-start.8 = (bf16[16,8064]{1,0:T(8,128)(2,1)S(1)}, bf16[16,8064]{1,0:T(8,128)(2,1)S(1)}, u32[]{:S(2)}, u32[]{:S(2)}) collective-permute-start(bf16[16,8064]{1,0:T(8,128)(2,1)S(1)} %collective-permute-done.refs_8_), channel_id=1, source_target_pairs={{0,64},{8,72},{16,80},{24,88},{32,96},{40,104},{48,112},{56,120},{... | collective-permute-start | bytes 774152 | tf_op jit(solution)/shard_map/ppermute | solution.py:277
  34.6 0.0 collective-permute-done.1.refs_1_
  34.6 1.1 collective-permute-start.7
  35.7 0.0 collective-permute-done.15.refs_16_
  35.7 0.0 collective-permute-start.6
  35.7 0.0 collective-permute-done.10.refs_11_
  35.7 2.7 %collective-permute-start.5 = (bf16[16,8064]{1,0:T(8,128)(2,1)S(1)}, bf16[16,8064]{1,0:T(8,128)(2,1)S(1)}, u32[]{:S(2)}, u32[]{:S(2)}) collective-permute-start(bf16[16,8064]{1,0:T(8,128)(2,1)S(1)} %collective-permute-done.1.refs_1_), channel_id=1, source_target_pairs={{0,3},{1,0},{2,1},{3,2},{4,7},{5,4},{6,5},{7,6},{8,11},{9,8},{10,9... | collective-permute-start | bytes 774152 | tf_op jit(solution)/shard_map/ppermute | solution.py:274
  38.4 0.0 collective-permute-done.9.refs_10_
  38.4 0.0 collective-permute-start.4
  38.4 6.9 %collective-permute-done.8.refs_9_ = bf16[16,8064]{1,0:T(8,128)(2,1)S(1)} collective-permute-done((bf16[16,8064]{1,0:T(8,128)(2,1)S(1)}, bf16[16,8064]{1,0:T(8,128)(2,1)S(1)}, u32[]{:S(2)}, u32[]{:S(2)}) %collective-permute-start.8) | collective-permute-done | bytes 258080 | tf_op jit(solution)/shard_map/ppermute | solution.py:277
  45.3 2.0 %collective-permute-start.18 = (bf16[16,8064]{1,0:T(8,128)(2,1)S(1)}, bf16[16,8064]{1,0:T(8,128)(2,1)S(1)}, u32[]{:S(2)}, u32[]{:S(2)}) collective-permute-start(bf16[16,8064]{1,0:T(8,128)(2,1)S(1)} %collective-permute-done.10.refs_11_), channel_id=1, source_target_pairs={{0,8},{8,0},{16,24},{24,16},{32,40},{40,32},{48,56},{56,48},{64,72... | collective-permute-start | bytes 774152 | tf_op jit(solution)/shard_map/ppermute | solution.py:280
  47.3 0.0 collective-permute-done.7.refs_7_
  47.3 3.6 %collective-permute-start.14 = (bf16[16,8064]{1,0:T(8,128)(2,1)S(1)}, bf16[16,8064]{1,0:T(8,128)(2,1)}, u32[]{:S(2)}, u32[]{:S(2)}) collective-permute-start(bf16[16,8064]{1,0:T(8,128)(2,1)S(1)} %collective-permute-done.10.refs_11_), channel_id=1, source_target_pairs={{0,112},{8,120},{16,64},{24,72},{32,80},{40,88},{48,96},{56,104},{... | collective-permute-start | bytes 774152 | tf_op jit(solution)/shard_map/ppermute | solution.py:277
  50.9 0.0 collective-permute-done.6.refs_6_
  50.9 0.3 collective-permute-start.17
  51.3 0.0 collective-permute-done.5.refs_5_
  51.3 1.0 collective-permute-start.13
  52.3 0.0 collective-permute-done.4.refs_4_
  52.3 3.9 %collective-permute-start.12 = (bf16[16,8064]{1,0:T(8,128)(2,1)S(1)}, bf16[16,8064]{1,0:T(8,128)(2,1)}, u32[]{:S(2)}, u32[]{:S(2)}) collective-permute-start(bf16[16,8064]{1,0:T(8,128)(2,1)S(1)} %collective-permute-done.8.refs_9_), channel_id=1, source_target_pairs={{0,48},{8,56},{16,0},{24,8},{32,16},{40,24},{48,32},{56,40},{64,11... | collective-permute-start | bytes 774152 | tf_op jit(solution)/shard_map/ppermute | solution.py:277
  56.2 0.0 collective-permute-done.18.refs_19_
  56.3 0.0 collective-permute-start.11
  56.3 2.5 %collective-permute-done.14.refs_15_ = bf16[16,8064]{1,0:T(8,128)(2,1)} collective-permute-done((bf16[16,8064]{1,0:T(8,128)(2,1)S(1)}, bf16[16,8064]{1,0:T(8,128)(2,1)}, u32[]{:S(2)}, u32[]{:S(2)}) %collective-permute-start.14) | collective-permute-done | bytes 258080 | tf_op jit(solution)/shard_map/ppermute | solution.py:277
  58.8 0.9 collective-permute-start.16
  59.7 0.0 collective-permute-done.17.refs_18_
  59.7 0.1 collective-permute-start.22
  59.8 2.9 %collective-permute-done.13.refs_14_ = bf16[16,8064]{1,0:T(8,128)(2,1)} collective-permute-done((bf16[16,8064]{1,0:T(8,128)(2,1)S(1)}, bf16[16,8064]{1,0:T(8,128)(2,1)}, u32[]{:S(2)}, u32[]{:S(2)}) %collective-permute-start.13) | collective-permute-done | bytes 258080 | tf_op jit(solution)/shard_map/ppermute | solution.py:277
  62.7 1.1 collective-permute-start.21
  63.8 0.5 collective-permute-start.20
  64.3 3.9 %collective-permute-done.11.refs_12_ = bf16[16,8064]{1,0:T(8,128)(2,1)} collective-permute-done((bf16[16,8064]{1,0:T(8,128)(2,1)S(1)}, bf16[16,8064]{1,0:T(8,128)(2,1)}, u32[]{:S(2)}, u32[]{:S(2)}) %collective-permute-start.11) | collective-permute-done | bytes 258080 | tf_op jit(solution)/shard_map/ppermute | solution.py:277
  68.2 0.7 collective-permute-start.19
  69.0 0.6 stack.99.place_ref
  69.6 0.0 collective-permute-done.16.refs_17_
  69.6 0.0 collective-permute-done.22.refs_23_
  69.6 0.0 collective-permute-done.21.refs_22_
  69.6 0.8 collective-permute-done.19.refs_20_
  70.6 43.4 %shard_map.47 = bf16[101,128,256]{2,1,0:T(8,128)(2,1)} custom-call(s32[24]{0:T(128)} %stack.99.place_ref, bf16[16,8064]{1,0:T(8,128)(2,1)} %shard_map.46.refs_0_, bf16[16,8064]{1,0:T(8,128)(2,1)} %copy-done.3, bf16[16,8064]{1,0:T(8,128)(2,1)} %copy-done.2, bf16[16,8064]{1,0:T(8,128)(2,1)} %copy-done.1, bf16[16,8064]{1,0:T(8,128)(2,1)} %copy-done.11, ...), custom_call_target="tpu_custom_call" | custom-call | tf_op jit(solution)/shard_map/pallas_call | solution.py:239
  (30 shorter events, 0.1 us)
Async XLA Ops:
  5.2 9.3 %collective-permute-start = (bf16[16,8064]{1,0:T(8,128)(2,1)}, bf16[16,8064]{1,0:T(8,128)(2,1)S(1)}, u32[]{:S(2)}, u32[]{:S(2)}) collective-permute-start(bf16[16,8064]{1,0:T(8,128)(2,1)} %shard_map.46.refs_0_), channel_id=1, source_target_pairs={{2,0},{3,16},{0,32},{1,48},{6,64},{7,80},{4,96},{5,112},{10,8},{11... | collective-permute-start | bytes 774152 | tf_op jit(solution)/shard_map/ppermute | solution.py:285
  14.5 55.9 %copy-start = (bf16[16,8064]{1,0:T(8,128)(2,1)}, bf16[16,8064]{1,0:T(8,128)(2,1)S(1)}, u32[]{:S(2)}) copy-start(bf16[16,8064]{1,0:T(8,128)(2,1)S(1)} %collective-permute-done.refs_8_) | copy-start | bytes 774148
  14.5 14.5 %collective-permute-start.3 = (bf16[16,8064]{1,0:T(8,128)(2,1)}, bf16[16,8064]{1,0:T(8,128)(2,1)S(1)}, u32[]{:S(2)}, u32[]{:S(2)}) collective-permute-start(bf16[16,8064]{1,0:T(8,128)(2,1)} %shard_map.46.refs_0_), channel_id=1, source_target_pairs={{0,3},{1,0},{2,1},{3,2},{4,7},{5,4},{6,5},{7,6},{8,11},{9,8},{10,9... | collective-permute-start | bytes 774152 | tf_op jit(solution)/shard_map/ppermute | solution.py:274
  20.6 9.3 %collective-permute-start.2 = (bf16[16,8064]{1,0:T(8,128)(2,1)}, bf16[16,8064]{1,0:T(8,128)(2,1)S(1)}, u32[]{:S(2)}, u32[]{:S(2)}) collective-permute-start(bf16[16,8064]{1,0:T(8,128)(2,1)} %shard_map.46.refs_0_), channel_id=1, source_target_pairs={{0,1},{1,2},{2,3},{3,0},{4,5},{5,6},{6,7},{7,4},{8,9},{9,10},{10,1... | collective-permute-start | bytes 774152 | tf_op jit(solution)/shard_map/ppermute | solution.py:274
  21.0 13.6 %collective-permute-start.1 = (bf16[16,8064]{1,0:T(8,128)(2,1)}, bf16[16,8064]{1,0:T(8,128)(2,1)S(1)}, u32[]{:S(2)}, u32[]{:S(2)}) collective-permute-start(bf16[16,8064]{1,0:T(8,128)(2,1)} %shard_map.46.refs_0_), channel_id=1, source_target_pairs={{0,4},{1,5},{2,6},{3,7},{4,0},{5,1},{6,2},{7,3},{8,12},{9,13},{10,... | collective-permute-start | bytes 774152 | tf_op jit(solution)/shard_map/ppermute | solution.py:274
  24.2 11.5 %collective-permute-start.15 = (bf16[16,8064]{1,0:T(8,128)(2,1)S(1)}, bf16[16,8064]{1,0:T(8,128)(2,1)S(1)}, u32[]{:S(2)}, u32[]{:S(2)}) collective-permute-start(bf16[16,8064]{1,0:T(8,128)(2,1)S(1)} %collective-permute-done.refs_8_), channel_id=1, source_target_pairs={{0,8},{8,0},{16,24},{24,16},{32,40},{40,32},{48,56},{56,48},{64,72... | collective-permute-start | bytes 774152 | tf_op jit(solution)/shard_map/ppermute | solution.py:280
  26.0 9.8 %collective-permute-start.10 = (bf16[16,8064]{1,0:T(8,128)(2,1)S(1)}, bf16[16,8064]{1,0:T(8,128)(2,1)S(1)}, u32[]{:S(2)}, u32[]{:S(2)}) collective-permute-start(bf16[16,8064]{1,0:T(8,128)(2,1)S(1)} %collective-permute-done.refs_8_), channel_id=1, source_target_pairs={{0,48},{8,56},{16,0},{24,8},{32,16},{40,24},{48,32},{56,40},{64,11... | collective-permute-start | bytes 774152 | tf_op jit(solution)/shard_map/ppermute | solution.py:277
  29.0 41.4 %copy-start.1 = (bf16[16,8064]{1,0:T(8,128)(2,1)}, bf16[16,8064]{1,0:T(8,128)(2,1)S(1)}, u32[]{:S(2)}) copy-start(bf16[16,8064]{1,0:T(8,128)(2,1)S(1)} %collective-permute-done.3.refs_3_) | copy-start | bytes 774148
  29.0 9.4 %collective-permute-start.9 = (bf16[16,8064]{1,0:T(8,128)(2,1)S(1)}, bf16[16,8064]{1,0:T(8,128)(2,1)S(1)}, u32[]{:S(2)}, u32[]{:S(2)}) collective-permute-start(bf16[16,8064]{1,0:T(8,128)(2,1)S(1)} %collective-permute-done.refs_8_), channel_id=1, source_target_pairs={{0,16},{8,24},{16,32},{24,40},{32,48},{40,56},{48,0},{56,8},{64,80... | collective-permute-start | bytes 774152 | tf_op jit(solution)/shard_map/ppermute | solution.py:277
  29.9 40.6 %copy-start.2 = (bf16[16,8064]{1,0:T(8,128)(2,1)}, bf16[16,8064]{1,0:T(8,128)(2,1)S(1)}, u32[]{:S(2)}) copy-start(bf16[16,8064]{1,0:T(8,128)(2,1)S(1)} %collective-permute-done.2.refs_2_) | copy-start | bytes 774148
  29.9 15.4 %collective-permute-start.8 = (bf16[16,8064]{1,0:T(8,128)(2,1)S(1)}, bf16[16,8064]{1,0:T(8,128)(2,1)S(1)}, u32[]{:S(2)}, u32[]{:S(2)}) collective-permute-start(bf16[16,8064]{1,0:T(8,128)(2,1)S(1)} %collective-permute-done.refs_8_), channel_id=1, source_target_pairs={{0,64},{8,72},{16,80},{24,88},{32,96},{40,104},{48,112},{56,120},{... | collective-permute-start | bytes 774152 | tf_op jit(solution)/shard_map/ppermute | solution.py:277
  34.6 35.8 %copy-start.3 = (bf16[16,8064]{1,0:T(8,128)(2,1)}, bf16[16,8064]{1,0:T(8,128)(2,1)S(1)}, u32[]{:S(2)}) copy-start(bf16[16,8064]{1,0:T(8,128)(2,1)S(1)} %collective-permute-done.1.refs_1_) | copy-start | bytes 774148
  34.6 12.7 %collective-permute-start.7 = (bf16[16,8064]{1,0:T(8,128)(2,1)S(1)}, bf16[16,8064]{1,0:T(8,128)(2,1)S(1)}, u32[]{:S(2)}, u32[]{:S(2)}) collective-permute-start(bf16[16,8064]{1,0:T(8,128)(2,1)S(1)} %collective-permute-done.3.refs_3_), channel_id=1, source_target_pairs={{0,7},{1,4},{2,5},{3,6},{4,3},{5,0},{6,1},{7,2},{8,15},{9,12},{10,... | collective-permute-start | bytes 774152 | tf_op jit(solution)/shard_map/ppermute | solution.py:274
  35.7 34.8 %copy-start.4 = (bf16[16,8064]{1,0:T(8,128)(2,1)}, bf16[16,8064]{1,0:T(8,128)(2,1)S(1)}, u32[]{:S(2)}) copy-start(bf16[16,8064]{1,0:T(8,128)(2,1)S(1)} %collective-permute-done.15.refs_16_) | copy-start | bytes 774148
  35.7 15.2 %collective-permute-start.6 = (bf16[16,8064]{1,0:T(8,128)(2,1)S(1)}, bf16[16,8064]{1,0:T(8,128)(2,1)S(1)}, u32[]{:S(2)}, u32[]{:S(2)}) collective-permute-start(bf16[16,8064]{1,0:T(8,128)(2,1)S(1)} %collective-permute-done.2.refs_2_), channel_id=1, source_target_pairs={{0,1},{1,2},{2,3},{3,0},{4,5},{5,6},{6,7},{7,4},{8,9},{9,10},{10,1... | collective-permute-start | bytes 774152 | tf_op jit(solution)/shard_map/ppermute | solution.py:274
  35.7 34.8 %copy-start.5 = (bf16[16,8064]{1,0:T(8,128)(2,1)}, bf16[16,8064]{1,0:T(8,128)(2,1)S(1)}, u32[]{:S(2)}) copy-start(bf16[16,8064]{1,0:T(8,128)(2,1)S(1)} %collective-permute-done.10.refs_11_) | copy-start | bytes 774148
  35.7 15.5 %collective-permute-start.5 = (bf16[16,8064]{1,0:T(8,128)(2,1)S(1)}, bf16[16,8064]{1,0:T(8,128)(2,1)S(1)}, u32[]{:S(2)}, u32[]{:S(2)}) collective-permute-start(bf16[16,8064]{1,0:T(8,128)(2,1)S(1)} %collective-permute-done.1.refs_1_), channel_id=1, source_target_pairs={{0,3},{1,0},{2,1},{3,2},{4,7},{5,4},{6,5},{7,6},{8,11},{9,8},{10,9... | collective-permute-start | bytes 774152 | tf_op jit(solution)/shard_map/ppermute | solution.py:274
  38.4 32.1 %copy-start.6 = (bf16[16,8064]{1,0:T(8,128)(2,1)}, bf16[16,8064]{1,0:T(8,128)(2,1)S(1)}, u32[]{:S(2)}) copy-start(bf16[16,8064]{1,0:T(8,128)(2,1)S(1)} %collective-permute-done.9.refs_10_) | copy-start | bytes 774148
  38.4 13.9 %collective-permute-start.4 = (bf16[16,8064]{1,0:T(8,128)(2,1)S(1)}, bf16[16,8064]{1,0:T(8,128)(2,1)S(1)}, u32[]{:S(2)}, u32[]{:S(2)}) collective-permute-start(bf16[16,8064]{1,0:T(8,128)(2,1)S(1)} %collective-permute-done.1.refs_1_), channel_id=1, source_target_pairs={{0,1},{1,2},{2,3},{3,0},{4,5},{5,6},{6,7},{7,4},{8,9},{9,10},{10,1... | collective-permute-start | bytes 774152 | tf_op jit(solution)/shard_map/ppermute | solution.py:274
  45.3 25.2 %copy-start.7 = (bf16[16,8064]{1,0:T(8,128)(2,1)}, bf16[16,8064]{1,0:T(8,128)(2,1)S(1)}, u32[]{:S(2)}) copy-start(bf16[16,8064]{1,0:T(8,128)(2,1)S(1)} %collective-permute-done.8.refs_9_) | copy-start | bytes 774148
  45.3 11.0 %collective-permute-start.18 = (bf16[16,8064]{1,0:T(8,128)(2,1)S(1)}, bf16[16,8064]{1,0:T(8,128)(2,1)S(1)}, u32[]{:S(2)}, u32[]{:S(2)}) collective-permute-start(bf16[16,8064]{1,0:T(8,128)(2,1)S(1)} %collective-permute-done.10.refs_11_), channel_id=1, source_target_pairs={{0,8},{8,0},{16,24},{24,16},{32,40},{40,32},{48,56},{56,48},{64,72... | collective-permute-start | bytes 774152 | tf_op jit(solution)/shard_map/ppermute | solution.py:280
  47.3 23.2 %copy-start.8 = (bf16[16,8064]{1,0:T(8,128)(2,1)}, bf16[16,8064]{1,0:T(8,128)(2,1)S(1)}, u32[]{:S(2)}) copy-start(bf16[16,8064]{1,0:T(8,128)(2,1)S(1)} %collective-permute-done.7.refs_7_) | copy-start | bytes 774148
  47.3 11.5 %collective-permute-start.14 = (bf16[16,8064]{1,0:T(8,128)(2,1)S(1)}, bf16[16,8064]{1,0:T(8,128)(2,1)}, u32[]{:S(2)}, u32[]{:S(2)}) collective-permute-start(bf16[16,8064]{1,0:T(8,128)(2,1)S(1)} %collective-permute-done.10.refs_11_), channel_id=1, source_target_pairs={{0,112},{8,120},{16,64},{24,72},{32,80},{40,88},{48,96},{56,104},{... | collective-permute-start | bytes 774152 | tf_op jit(solution)/shard_map/ppermute | solution.py:277
  50.9 19.6 %copy-start.9 = (bf16[16,8064]{1,0:T(8,128)(2,1)}, bf16[16,8064]{1,0:T(8,128)(2,1)S(1)}, u32[]{:S(2)}) copy-start(bf16[16,8064]{1,0:T(8,128)(2,1)S(1)} %collective-permute-done.6.refs_6_) | copy-start | bytes 774148
  50.9 8.8 %collective-permute-start.17 = (bf16[16,8064]{1,0:T(8,128)(2,1)S(1)}, bf16[16,8064]{1,0:T(8,128)(2,1)S(1)}, u32[]{:S(2)}, u32[]{:S(2)}) collective-permute-start(bf16[16,8064]{1,0:T(8,128)(2,1)S(1)} %collective-permute-done.9.refs_10_), channel_id=1, source_target_pairs={{0,8},{8,0},{16,24},{24,16},{32,40},{40,32},{48,56},{56,48},{64,72... | collective-permute-start | bytes 774152 | tf_op jit(solution)/shard_map/ppermute | solution.py:280
  51.3 19.3 %copy-start.10 = (bf16[16,8064]{1,0:T(8,128)(2,1)}, bf16[16,8064]{1,0:T(8,128)(2,1)S(1)}, u32[]{:S(2)}) copy-start(bf16[16,8064]{1,0:T(8,128)(2,1)S(1)} %collective-permute-done.5.refs_5_) | copy-start | bytes 774148
  51.3 11.4 %collective-permute-start.13 = (bf16[16,8064]{1,0:T(8,128)(2,1)S(1)}, bf16[16,8064]{1,0:T(8,128)(2,1)}, u32[]{:S(2)}, u32[]{:S(2)}) collective-permute-start(bf16[16,8064]{1,0:T(8,128)(2,1)S(1)} %collective-permute-done.9.refs_10_), channel_id=1, source_target_pairs={{0,16},{8,24},{16,32},{24,40},{32,48},{40,56},{48,0},{56,8},{64,80... | collective-permute-start | bytes 774152 | tf_op jit(solution)/shard_map/ppermute | solution.py:277
  52.3 18.2 %copy-start.11 = (bf16[16,8064]{1,0:T(8,128)(2,1)}, bf16[16,8064]{1,0:T(8,128)(2,1)S(1)}, u32[]{:S(2)}) copy-start(bf16[16,8064]{1,0:T(8,128)(2,1)S(1)} %collective-permute-done.4.refs_4_) | copy-start | bytes 774148
  52.3 11.5 %collective-permute-start.12 = (bf16[16,8064]{1,0:T(8,128)(2,1)S(1)}, bf16[16,8064]{1,0:T(8,128)(2,1)}, u32[]{:S(2)}, u32[]{:S(2)}) collective-permute-start(bf16[16,8064]{1,0:T(8,128)(2,1)S(1)} %collective-permute-done.8.refs_9_), channel_id=1, source_target_pairs={{0,48},{8,56},{16,0},{24,8},{32,16},{40,24},{48,32},{56,40},{64,11... | collective-permute-start | bytes 774152 | tf_op jit(solution)/shard_map/ppermute | solution.py:277
  56.2 14.3 %copy-start.12 = (bf16[16,8064]{1,0:T(8,128)(2,1)}, bf16[16,8064]{1,0:T(8,128)(2,1)S(1)}, u32[]{:S(2)}) copy-start(bf16[16,8064]{1,0:T(8,128)(2,1)S(1)} %collective-permute-done.18.refs_19_) | copy-start | bytes 774148
  56.3 12.0 %collective-permute-start.11 = (bf16[16,8064]{1,0:T(8,128)(2,1)S(1)}, bf16[16,8064]{1,0:T(8,128)(2,1)}, u32[]{:S(2)}, u32[]{:S(2)}) collective-permute-start(bf16[16,8064]{1,0:T(8,128)(2,1)S(1)} %collective-permute-done.8.refs_9_), channel_id=1, source_target_pairs={{0,16},{8,24},{16,32},{24,40},{32,48},{40,56},{48,0},{56,8},{64,80... | collective-permute-start | bytes 774152 | tf_op jit(solution)/shard_map/ppermute | solution.py:277
  58.8 10.8 %collective-permute-start.16 = (bf16[16,8064]{1,0:T(8,128)(2,1)S(1)}, bf16[16,8064]{1,0:T(8,128)(2,1)}, u32[]{:S(2)}, u32[]{:S(2)}) collective-permute-start(bf16[16,8064]{1,0:T(8,128)(2,1)S(1)} %collective-permute-done.8.refs_9_), channel_id=1, source_target_pairs={{0,8},{8,0},{16,24},{24,16},{32,40},{40,32},{48,56},{56,48},{64,72... | collective-permute-start | bytes 774152 | tf_op jit(solution)/shard_map/ppermute | solution.py:280
  59.7 8.5 %copy-start.13 = (bf16[16,8064]{1,0:T(8,128)(2,1)}, bf16[16,8064]{1,0:T(8,128)(2,1)S(1)}, u32[]{:S(2)}) copy-start(bf16[16,8064]{1,0:T(8,128)(2,1)S(1)} %collective-permute-done.17.refs_18_) | copy-start | bytes 774148
  59.7 9.9 %collective-permute-start.22 = (bf16[16,8064]{1,0:T(8,128)(2,1)}, bf16[16,8064]{1,0:T(8,128)(2,1)}, u32[]{:S(2)}, u32[]{:S(2)}) collective-permute-start(bf16[16,8064]{1,0:T(8,128)(2,1)} %collective-permute-done.14.refs_15_), channel_id=1, source_target_pairs={{0,8},{8,0},{16,24},{24,16},{32,40},{40,32},{48,56},{56,48},{64,72... | collective-permute-start | bytes 774152 | tf_op jit(solution)/shard_map/ppermute | solution.py:280
  62.7 6.9 %collective-permute-start.21 = (bf16[16,8064]{1,0:T(8,128)(2,1)}, bf16[16,8064]{1,0:T(8,128)(2,1)}, u32[]{:S(2)}, u32[]{:S(2)}) collective-permute-start(bf16[16,8064]{1,0:T(8,128)(2,1)} %collective-permute-done.13.refs_14_), channel_id=1, source_target_pairs={{0,8},{8,0},{16,24},{24,16},{32,40},{40,32},{48,56},{56,48},{64,72... | collective-permute-start | bytes 774152 | tf_op jit(solution)/shard_map/ppermute | solution.py:280
  63.8 5.8 %collective-permute-start.20 = (bf16[16,8064]{1,0:T(8,128)(2,1)}, bf16[16,8064]{1,0:T(8,128)(2,1)}, u32[]{:S(2)}, u32[]{:S(2)}) collective-permute-start(bf16[16,8064]{1,0:T(8,128)(2,1)} %collective-permute-done.12.refs_13_), channel_id=1, source_target_pairs={{0,8},{8,0},{16,24},{24,16},{32,40},{40,32},{48,56},{56,48},{64,72... | collective-permute-start | bytes 774152 | tf_op jit(solution)/shard_map/ppermute | solution.py:280
  68.2 2.2 %collective-permute-start.19 = (bf16[16,8064]{1,0:T(8,128)(2,1)}, bf16[16,8064]{1,0:T(8,128)(2,1)}, u32[]{:S(2)}, u32[]{:S(2)}) collective-permute-start(bf16[16,8064]{1,0:T(8,128)(2,1)} %collective-permute-done.11.refs_12_), channel_id=1, source_target_pairs={{0,8},{8,0},{16,24},{24,16},{32,40},{40,32},{48,56},{56,48},{64,72... | collective-permute-start | bytes 774152 | tf_op jit(solution)/shard_map/ppermute | solution.py:280

commit v4 on v1

v4 whole, which is shorter than its diff:
```python
import functools
import math

import jax
import jax.numpy as jnp
import numpy as np
from jax import lax
from jax.experimental import pallas as pl
from jax.experimental.pallas import tpu as pltpu
from jax.sharding import PartitionSpec as P

W = 10
F = 400
KLO = 6
NT = 12000
HALF = 50
LAGS = 2 * HALF + 1
LAG_ROWS = 56
LAG_TILE = 64
UNROLL = 10
FB = 8
NB = F // FB
OWN = 16
MAIN = 16
TILES = NB + -(-NB // 4)
LANES = TILES * 128
DEPTH = 4
LAG = 3


def unit_circle(turns):
    turns = turns - NT * jnp.floor(turns * (1.0 / NT))
    quarter = jnp.floor(turns * (4.0 / NT) + 0.5)
    a = (turns - (NT // 4) * quarter) * (2.0 * math.pi / NT)
    s = a * a
    sin = a + a * s * (-1 / 6 + s * (1 / 120 + s * (-1 / 5040 + s * (1 / 362880))))
    cos = 1.0 + s * (-0.5 + s * (1 / 24 + s * (-1 / 720 + s * (1 / 40320 + s * (-1 / 3628800)))))
    swap = (quarter == 1.0) | (quarter == 3.0)
    c = jnp.where(swap, sin, cos)
    s = jnp.where(swap, cos, sin)
    c = jnp.where((quarter == 1.0) | (quarter == 2.0), -c, c)
    s = jnp.where((quarter == 2.0) | (quarter == 3.0), -s, s)
    return c, s


def whiten_kernel(mask_ref, spectra_ref, offsets_ref, white_ref, parts):
    freq = (KLO + lax.broadcasted_iota(jnp.int32, (W, F), 1)).astype(jnp.float32)
    eye = lax.broadcasted_iota(jnp.int32, (W, W), 0) == lax.broadcasted_iota(jnp.int32, (W, W), 1)
    parts[3] = jnp.zeros((OWN * 32, 128), jnp.float32)
    for ch in range(OWN):
        re = spectra_ref[ch, 0].astype(jnp.float32)
        im = spectra_ref[ch, 1].astype(jnp.float32)
        power = jnp.sum(re * re + im * im, axis=1, keepdims=True) * (1.0 / F)
        scale = lax.rsqrt(power + 1e-06) * mask_ref[ch].astype(jnp.float32)
        row = jnp.broadcast_to(offsets_ref[ch : ch + 1].astype(jnp.float32), (W, W))
        offset = jnp.sum(jnp.where(eye, row, 0.0), axis=1, keepdims=True)
        c, s = unit_circle(offset * freq)
        out = ((re * c + im * s) * scale, (im * c - re * s) * scale)
        for part in range(2):
            for t in range(4):
                n = min(128, F - 128 * t)
                parts[t, ch * 32 + part * 16 : ch * 32 + part * 16 + W, :n] = out[part][:, 128 * t : 128 * t + n]

    chunk = lax.broadcasted_iota(jnp.int32, (OWN, 128), 1) // 8
    for t in range(4):
        pairs = [parts[t, pl.ds(16 * (m % 2) + m // 2, OWN, stride=32), :] for m in range(2 * W)]
        main, rest = pairs[:MAIN], pairs[MAIN:]
        for values, low, bits in ((main, 0, 4), (rest, 2, 2)):
            for bit in range(bits):
                shift = 8 << (low + bit)
                upper = (chunk >> (low + bit)) % 2 == 1
                for m in range(len(values)):
                    if not m >> bit & 1:
                        a, b = values[m], values[m | 1 << bit]
                        values[m] = jnp.where(upper, pltpu.roll(b, shift, 1), a)
                        values[m | 1 << bit] = jnp.where(upper, b, pltpu.roll(a, 128 - shift, 1))
        for k in range(16):
            if 16 * t + k < NB:
                white_ref[:, (16 * t + k) * 128 : (16 * t + k + 1) * 128] = main[k].astype(jnp.bfloat16)
        for k in range(4):
            tile = NB + 4 * t + k
            if tile < TILES:
                white_ref[:, tile * 128 : (tile + 1) * 128] = rest[k].astype(jnp.bfloat16)


def whiten(spectra, offsets, channel_mask):
    return pl.pallas_call(
        whiten_kernel,
        in_specs=[
            pl.BlockSpec(memory_space=pltpu.SMEM),
            pl.BlockSpec(memory_space=pltpu.VMEM),
            pl.BlockSpec(memory_space=pltpu.VMEM),
        ],
        out_specs=pl.BlockSpec(memory_space=pltpu.VMEM),
        out_shape=jax.ShapeDtypeStruct((OWN, LANES), jnp.bfloat16),
        scratch_shapes=[pltpu.VMEM((4, OWN * 32, 128), jnp.float32)],
    )(channel_mask, spectra, offsets)


def segments():
    return [(t, u) for t in range(OWN * F // 256) for u in range(256 * t // F, (256 * t + 255) // F + 1)]


def lag_tables():
    freq = KLO + np.arange(F)
    angle = 2.0 * math.pi / NT * ((np.arange(HALF + 1)[:, None] * freq[None, :]) % NT)
    tables = np.pad(np.stack([np.cos(angle), -np.sin(angle)]), ((0, 0), (0, LAG_TILE - HALF - 1), (256, 256)))
    return np.stack([tables[:, :, 256 + 256 * t - F * u :][:, :, :256] for t, u in segments()], 1)


def step(index, ring, side):
    return (index ^ (4 * side)) & 4 | (index + ring) & 3


def correlate_kernel(row_keys, col_keys, n_kept, *refs):
    n_rows, n_cols = len(row_keys), 2 * len(col_keys)
    p, q, core = lax.axis_index("rcv"), lax.axis_index("src") // 2, lax.axis_index("src") % 2
    row_places = [step(p, *key) for key in row_keys]
    col_places = [c * 8 + step(step(q, *key), 2, 0) for c in (core, 1 - core) for key in col_keys]
    row_refs, refs = refs[:n_rows], refs[n_rows:]
    col_refs, refs = refs[:n_cols], refs[n_cols:]
    table_ref, out_ref, cols, rows, turned, cross, *lagged, staged, sems = refs[:1] + refs[1 + n_kept :]
    lane = lax.broadcasted_iota(jnp.int32, (16, 128), 1)
    same_bin = (lane % 8) == lax.broadcasted_iota(jnp.int32, (16, 128), 0) % 8
    zero = jnp.zeros((), jnp.bfloat16)
    groups = n_rows * OWN // 8

    for k, ref in enumerate(col_refs):
        cols[pl.ds(pl.multiple_of(col_places[k] * OWN, OWN), OWN), :] = ref[...]

    def spread(first, last, shift):
        minus = (lax.broadcasted_iota(jnp.int32, (OWN, 128), 1) // shift) % 2 == 1

        @pl.loop(first, last, unroll=UNROLL)
        def _(t):
            at = pl.ds(pl.multiple_of(t * 128, 128), 128)
            for k, ref in enumerate(row_refs):
                v = ref[:, at].astype(jnp.float32)
                rows[k * OWN : (k + 1) * OWN, at] = v
                v = jnp.where(minus, -pltpu.roll(v, shift, 1), pltpu.roll(v, 128 - shift, 1))
                turned[k * OWN : (k + 1) * OWN, at] = v

    spread(0, NB, 8)
    spread(NB, TILES, 32)

    def cross_of(*accs):
        accs = accs[:DEPTH], accs[DEPTH:]

        def main_lanes(b):
            return pl.ds(pl.multiple_of(b * 128, 128), 128)

        def rest_lanes(pair):
            return pl.ds(pl.multiple_of((NB + pair // 2) * 128, 128), 128)

        def push(pair):
            for mxu in range(2):
                right = jnp.concatenate([cols[:, main_lanes(2 * pair + mxu)], cols[:, rest_lanes(pair)]], 1)
                pltpu.matmul_push_rhs(right, 0, mxu, transpose=True)

        def wide(i, lanes):
            both = [jnp.broadcast_to(ref[i : i + 1, lanes], (8, 128)) for ref in (rows, turned)]
            return jnp.concatenate(both, 0).astype(jnp.bfloat16)

        def start(pair, k, same_rest):
            left = [], []
            for u in range(8):
                r = wide(8 * k + u, rest_lanes(pair))
                for mxu in range(2):
                    m = wide(8 * k + u, main_lanes(2 * pair + mxu))
                    m, q = jnp.where(same_bin, m, zero), jnp.where(same_rest[mxu], r, zero)
                    left[mxu].append(jnp.concatenate([m, q], 1))
            for mxu in range(2):
                left_rows = jnp.concatenate(left[mxu], 0)
                pltpu.matmul_acc_lhs(accs[mxu][k % DEPTH], left_rows, 0 if k == 0 else None)

        def finish(pair, k):
            product = [pltpu.matmul_pop(accs[mxu][k % DEPTH]) for mxu in range(2)]
            for part in range(2):
                for u in range(8):
                    o = u * 16 + part * 8
                    both = jnp.concatenate([p[o : o + 8] for p in product], 0)
                    at = pl.ds(pl.multiple_of((8 * k + u) * F + pair * 16, 16), 16)
                    cross[part, at, :] = both.astype(jnp.bfloat16)

        def work(pair, first, last):
            same_rest = [same_bin & ((lane // 8) % 4 == (2 * pair + mxu) % 4) for mxu in range(2)]
            for k in range(groups):
                start(pair, k, same_rest)
                if not last and k == 1:
                    push(pair + 1)
                if k >= LAG:
                    finish(pair, k - LAG)
                elif not first:
                    finish(pair - 1, k - LAG + groups)

        push(0)
        work(0, True, False)
        pl.loop(1, NB // 2 - 1)(lambda pair: work(pair, False, False))
        work(NB // 2 - 1, False, True)
        for k in range(groups - LAG, groups):
            finish(NB // 2 - 1, k)

    def out_copy(k):
        at = pl.ds(pl.multiple_of(row_places[k] * OWN, OWN), OWN)
        return pltpu.make_async_copy(staged.at[k % 2], out_ref.at[:, at, :], sems.at[k % 2])

    def emit(g):
        if g >= 2:
            out_copy(g - 2).wait()
        for lag in range(HALF + 1):
            for h in range(2):
                e, o = (lagged[2 * (g % 2) + part][h, pl.ds(lag, OWN, stride=LAG_ROWS), :] for part in range(2))
                lanes = slice(h * 128, (h + 1) * 128)
                staged[g % 2, HALF + lag, :, lanes] = ((e + o) * (1.0 / math.sqrt(W * F))).astype(jnp.bfloat16)
                if lag:
                    staged[g % 2, HALF - lag, :, lanes] = ((e - o) * (1.0 / math.sqrt(W * F))).astype(jnp.bfloat16)
        out_copy(g).start()

    def lags_of(*accs):
        accs = accs[:4], accs[4:]

        def push(g, t):
            at = g * OWN * F + t * 256
            for part in range(2):
                pltpu.matmul_push_rhs(cross[part, at : at + 256, :], t % 2, part)

        def finish(g, u):
            for part in range(2):
                z = pltpu.matmul_pop(accs[part][u % 4])
                for h in range(2):
                    rows_of = slice(u * LAG_ROWS, (u + 1) * LAG_ROWS)
                    lagged[2 * (g % 2) + part][h, rows_of, :] = z[:LAG_ROWS, h * 128 : (h + 1) * 128]

        for g in range(n_rows):
            pushed = done = -1
            for k, (t, u) in enumerate(segments()):
                if t != pushed:
                    push(g, t)
                for part in range(2):
                    pltpu.matmul_acc_lhs(accs[part][u % 4], table_ref[part, k], t % 2 if t != pushed else None)
                pushed = t
                if u - 2 > done:
                    done = u - 2
                    finish(g, done)
            for u in range(done + 1, OWN):
                finish(g, u)
            if g:
                emit(g - 1)
        emit(n_rows - 1)

    pl.run_scoped(cross_of, *[pltpu.ACC(mxu)((128, 256), jnp.float32) for mxu in [0] * DEPTH + [1] * DEPTH])
    pl.run_scoped(lags_of, *[pltpu.ACC(mxu)((LAG_TILE, 256), jnp.float32) for mxu in [0] * 4 + [1] * 4])
    for k in range(n_rows - 2, n_rows):
        out_copy(k).wait()


def correlate(rows, cols, swapped, shape, kept=()):
    row_blocks, col_blocks = list(rows.values()), list(cols.values()) + [swapped[key] for key in cols]
    n, m = OWN * len(row_blocks), OWN * len(col_blocks)
    vmem, anywhere = pl.BlockSpec(memory_space=pltpu.VMEM), pl.BlockSpec(memory_space=pl.ANY)
    inputs = (*row_blocks, *col_blocks, jnp.asarray(lag_tables(), jnp.bfloat16), *kept)
    return pl.pallas_call(
        functools.partial(correlate_kernel, tuple(rows), tuple(cols), len(kept)),
        in_specs=[vmem] * (len(row_blocks) + len(col_blocks) + 1) + [anywhere] * len(kept),
        out_specs=anywhere,
        out_shape=jax.ShapeDtypeStruct(shape, jnp.bfloat16),
        input_output_aliases={len(inputs) - 1: 0} if kept else {},
        scratch_shapes=[
            pltpu.VMEM((m, LANES), jnp.bfloat16),
            pltpu.VMEM((n, LANES), jnp.float32),
            pltpu.VMEM((n, LANES), jnp.float32),
            pltpu.VMEM((2, n * F, m), jnp.bfloat16),
            *[pltpu.VMEM((2, OWN * LAG_ROWS, 128), jnp.float32)] * 4,
            pltpu.VMEM((2, LAGS, OWN, m), jnp.bfloat16),
            pltpu.SemaphoreType.DMA((2,)),
        ],
        compiler_params=pltpu.CompilerParams(vmem_limit_bytes=52 * 1024 * 1024),
        cost_estimate=pl.CostEstimate(flops=n * 2 * 10**8, bytes_accessed=10**7, transcendentals=0),
    )(*inputs)


def near(block, move):
    return {(0, 0): block, (0, 1): move(block, 0, 1), (-1, 0): move(block, 1, 0), (1, 0): move(block, -1, 0)}


def far(found, move):
    return {
        (-1, 1): move(found[0, 1], 1, 0),
        (1, 1): move(found[0, 1], -1, 0),
        (2, 0): move(found[-1, 0], 1, 0),
        (2, 1): move(found[1, 0], -1, 1),
    }


def body(spectra, offsets, channel_mask):
    white = whiten(spectra, offsets, channel_mask)

    def over_rcv(value, ring, side):
        return lax.ppermute(value, "rcv", [(i, step(i, ring, side)) for i in range(8)])

    def over_src(value, ring, side):
        return lax.ppermute(value, "src", [(i, 2 * step(i // 2, ring, side) + i % 2) for i in range(16)])

    def other_core(value):
        return lax.ppermute(value, "src", [(i, i ^ 1) for i in range(16)])

    flip = [
        ((i * 2 + k) * 8 + step(j, 2, 0), (j * 2 + k) * 8 + i) for i in range(8) for k in range(2) for j in range(8)
    ]
    turned = lax.ppermute(white, ("src", "rcv"), flip)
    cols = near(turned, over_src)
    swapped = {(0, 0): other_core(turned)}
    white, swapped[0, 0] = lax.optimization_barrier((white, swapped[0, 0]))
    rows = near(white, over_rcv)
    more = far(cols, over_src)
    swapped |= {key: other_core(value) for key, value in (cols | more).items() if key != (0, 0)}
    cols |= more
    rows, swapped = lax.optimization_barrier((rows, swapped))
    shape = (LAGS, 8 * OWN, 16 * OWN)
    first = correlate(rows, cols, swapped, shape)
    return correlate(far(rows, over_rcv), cols, swapped, shape, (first,))


def solution(mesh):
    in_specs = (P(("src", "rcv"), None, None, None), P(("src", "rcv"), None), P(("src", "rcv")))
    out_specs = P(None, "src", "rcv")
    return jax.shard_map(body, mesh=mesh, in_specs=in_specs, out_specs=out_specs, check_vma=False)
```

time: 171 us -> 106 us (0.62)
  Pallas kernels: 110 us -> 44.4 us
  starting transfers between devices: 49.9 us -> 44.8 us
  waiting for transfers between devices: 8.26 us -> 12.5 us
    pallas_call x1 -> x2, Pallas kernels: 107 us -> 41 us  [correlate(): pl.pallas_call(functools.partial(correlate_kernel, tuple(rows), tuple(col...]
    ppermute x1, waiting for transfers between devices: 0.01 us -> 5.54 us  [body(): turned = lax.ppermute(white, ('src', 'rcv'), flip)]
    ppermute x7, waiting for transfers between devices: 5.21 us -> 0.89 us  [over_rcv(): lax.ppermute(value, 'rcv', [(i, step(i, ring, side)) for i in range(8)])]
    ppermute x8, starting transfers between devices: 16.9 us -> 13.3 us  [other_core(): return lax.ppermute(value, 'src', [(i, i ^ 1) for i in range(16)])]
    ppermute x7, starting transfers between devices: 12 us -> 8.39 us  [over_rcv(): lax.ppermute(value, 'rcv', [(i, step(i, ring, side)) for i in range(8)])]
    ppermute x7, waiting for transfers between devices: 2.25 us -> 5.58 us  [over_src(): lax.ppermute(value, 'src', [(i, 2 * step(i // 2, ring, side) + i % 2) for...]
    ppermute x1, starting transfers between devices: 1.59 us -> 3.74 us  [body(): turned = lax.ppermute(white, ('src', 'rcv'), flip)]
  transfers between devices with their start and end apart: 23 -> 23, of which waited for: 7 -> 9; matrix products, arithmetic and copies ran while one was open for 0% -> 0% of each run, Pallas kernels for 0% -> 19%
where the time goes in v4:
time: 106 us; the launch traced here: 105 us
  starting transfers between devices  44.8 us (42%)
  Pallas kernels  44.4 us (42%)
  waiting for transfers between devices  12.5 us (12%)
  local copies, waits for them, and re-layouts  2.83 us (3%)
    pallas_call x2, Pallas kernels, correlate(): pl.pallas_call(functools.partial(correlate_kernel, tuple(rows), tuple(col...  41 us
    ppermute x7, starting transfers between devices, over_src(): lax.ppermute(value, 'src', [(i, 2 * step(i // 2, ring, side) + i % 2) for...  19.4 us
    ppermute x8, starting transfers between devices, other_core(): return lax.ppermute(value, 'src', [(i, i ^ 1) for i in range(16)])  13.3 us
    ppermute x7, starting transfers between devices, over_rcv(): lax.ppermute(value, 'rcv', [(i, step(i, ring, side)) for i in range(8)])  8.39 us
    ppermute x7, waiting for transfers between devices, over_src(): lax.ppermute(value, 'src', [(i, 2 * step(i // 2, ring, side) + i % 2) for...  5.58 us
    ppermute x1, waiting for transfers between devices, body(): turned = lax.ppermute(white, ('src', 'rcv'), flip)  5.54 us
    ppermute x1, starting transfers between devices, body(): turned = lax.ppermute(white, ('src', 'rcv'), flip)  3.74 us
    pallas_call x1, Pallas kernels, whiten(): pl.pallas_call(whiten_kernel, in_specs=[pl.BlockSpec(memory_space=pltpu.S...  3.39 us
  transfers between devices with their start and end apart: 23, of which 9 were waited for; matrix products, arithmetic and copies ran while one was open for 0% of the time, Pallas kernels for 19%

profile of v4, /device:TPU:1, one launch (start us, length us, event | category | flops | bytes accessed | tf_op | source)
XLA Modules:
  0.0 104.9 jit_solution(7514073598217680193)
XLA Ops:
  0.0 1.8 %copy.7.spectra_ref = bf16[16,2,10,400]{3,2,1,0:T(8,128)(2,1)} copy(bf16[16,2,10,400]{3,1,2,0:T(2,128)(2,1)} %param.5) | data formatting | bytes 512000 | tf_op args[0]
  1.8 3.4 %shard_map.55.refs_1_ = bf16[16,8064]{1,0:T(8,128)(2,1)} custom-call(s32[16]{0:T(128)} %mask_ref.1, bf16[16,2,10,400]{3,2,1,0:T(8,128)(2,1)} %copy.7.spectra_ref, s32[16,10]{1,0:T(8,128)} %offsets_ref.1), custom_call_target="tpu_custom_call" | custom-call | tf_op jit(solution)/shard_map/pallas_call | solution.py:87
  5.2 3.7 %collective-permute-start = (bf16[16,8064]{1,0:T(8,128)(2,1)}, bf16[16,8064]{1,0:T(8,128)(2,1)S(1)}, u32[]{:S(2)}, u32[]{:S(2)}) collective-permute-start(bf16[16,8064]{1,0:T(8,128)(2,1)} %shard_map.55.refs_1_), channel_id=1, source_target_pairs={{2,0},{3,16},{0,32},{1,48},{6,64},{7,80},{4,96},{5,112},{10,8},{11... | collective-permute-start | bytes 774152 | tf_op jit(solution)/shard_map/ppermute | solution.py:310
  9.0 5.5 %collective-permute-done.refs_4_ = bf16[16,8064]{1,0:T(8,128)(2,1)S(1)} collective-permute-done((bf16[16,8064]{1,0:T(8,128)(2,1)}, bf16[16,8064]{1,0:T(8,128)(2,1)S(1)}, u32[]{:S(2)}, u32[]{:S(2)}) %collective-permute-start) | collective-permute-done | bytes 258080 | tf_op jit(solution)/shard_map/ppermute | solution.py:310
  14.5 8.6 %collective-permute-start.11 = (bf16[16,8064]{1,0:T(8,128)(2,1)S(1)}, bf16[16,8064]{1,0:T(8,128)(2,1)S(1)}, u32[]{:S(2)}, u32[]{:S(2)}) collective-permute-start(bf16[16,8064]{1,0:T(8,128)(2,1)S(1)} %collective-permute-done.refs_4_), channel_id=1, source_target_pairs={{0,48},{8,56},{16,0},{24,8},{32,16},{40,24},{48,32},{56,40},{64,11... | collective-permute-start | bytes 774152 | tf_op jit(solution)/shard_map/ppermute | solution.py:302
  23.1 3.1 %collective-permute-start.7 = (bf16[16,8064]{1,0:T(8,128)(2,1)S(1)}, bf16[16,8064]{1,0:T(8,128)(2,1)S(1)}, u32[]{:S(2)}, u32[]{:S(2)}) collective-permute-start(bf16[16,8064]{1,0:T(8,128)(2,1)S(1)} %collective-permute-done.refs_4_), channel_id=1, source_target_pairs={{0,64},{8,72},{16,80},{24,88},{32,96},{40,104},{48,112},{56,120},{... | collective-permute-start | bytes 774152 | tf_op jit(solution)/shard_map/ppermute | solution.py:302
  26.3 1.2 %collective-permute-start.1 = (bf16[16,8064]{1,0:T(8,128)(2,1)S(1)}, bf16[16,8064]{1,0:T(8,128)(2,1)S(1)}, u32[]{:S(2)}, u32[]{:S(2)}) collective-permute-start(bf16[16,8064]{1,0:T(8,128)(2,1)S(1)} %collective-permute-done.refs_4_), channel_id=1, source_target_pairs={{0,8},{8,0},{16,24},{24,16},{32,40},{40,32},{48,56},{56,48},{64,72... | collective-permute-start | bytes 774152 | tf_op jit(solution)/shard_map/ppermute | solution.py:305
  27.4 0.6 collective-permute-start.5
  28.0 0.5 collective-permute-done.11.refs_7_
  28.5 5.9 %collective-permute-start.17 = (bf16[16,8064]{1,0:T(8,128)(2,1)S(1)}, bf16[16,8064]{1,0:T(8,128)(2,1)S(1)}, u32[]{:S(2)}, u32[]{:S(2)}) collective-permute-start(bf16[16,8064]{1,0:T(8,128)(2,1)S(1)} %collective-permute-done.11.refs_7_), channel_id=1, source_target_pairs={{0,112},{8,120},{16,64},{24,72},{32,80},{40,88},{48,96},{56,104},{... | collective-permute-start | bytes 774152 | tf_op jit(solution)/shard_map/ppermute | solution.py:302
  34.4 1.8 %collective-permute-start.12 = (bf16[16,8064]{1,0:T(8,128)(2,1)S(1)}, bf16[16,8064]{1,0:T(8,128)(2,1)S(1)}, u32[]{:S(2)}, u32[]{:S(2)}) collective-permute-start(bf16[16,8064]{1,0:T(8,128)(2,1)S(1)} %collective-permute-done.11.refs_7_), channel_id=1, source_target_pairs={{0,8},{8,0},{16,24},{24,16},{32,40},{40,32},{48,56},{56,48},{64,72... | collective-permute-start | bytes 774152 | tf_op jit(solution)/shard_map/ppermute | solution.py:305
  36.1 0.0 collective-permute-done.7.refs_5_
  36.1 0.0 collective-permute-start.13
  36.1 0.0 collective-permute-done.1.refs_12_
  36.1 0.1 collective-permute-start.10
  36.3 0.4 collective-permute-done.5.refs_6_
  36.7 1.2 %collective-permute-start.8 = (bf16[16,8064]{1,0:T(8,128)(2,1)S(1)}, bf16[16,8064]{1,0:T(8,128)(2,1)S(1)}, u32[]{:S(2)}, u32[]{:S(2)}) collective-permute-start(bf16[16,8064]{1,0:T(8,128)(2,1)S(1)} %collective-permute-done.7.refs_5_), channel_id=1, source_target_pairs={{0,16},{8,24},{16,32},{24,40},{32,48},{40,56},{48,0},{56,8},{64,80... | collective-permute-start | bytes 774152 | tf_op jit(solution)/shard_map/ppermute | solution.py:302
  37.9 1.2 %collective-permute-done.17.refs_11_ = bf16[16,8064]{1,0:T(8,128)(2,1)S(1)} collective-permute-done((bf16[16,8064]{1,0:T(8,128)(2,1)S(1)}, bf16[16,8064]{1,0:T(8,128)(2,1)S(1)}, u32[]{:S(2)}, u32[]{:S(2)}) %collective-permute-start.17) | collective-permute-done | bytes 258080 | tf_op jit(solution)/shard_map/ppermute | solution.py:302
  39.0 0.0 collective-permute-start.15
  39.1 0.0 collective-permute-done.12.refs_15_
  39.1 4.2 %collective-permute-start.6 = (bf16[16,8064]{1,0:T(8,128)(2,1)S(1)}, bf16[16,8064]{1,0:T(8,128)(2,1)S(1)}, u32[]{:S(2)}, u32[]{:S(2)}) collective-permute-start(bf16[16,8064]{1,0:T(8,128)(2,1)S(1)} %collective-permute-done.5.refs_6_), channel_id=1, source_target_pairs={{0,8},{8,0},{16,24},{24,16},{32,40},{40,32},{48,56},{56,48},{64,72... | collective-permute-start | bytes 774152 | tf_op jit(solution)/shard_map/ppermute | solution.py:305
  43.2 1.9 %collective-permute-done.13.refs_9_ = bf16[16,8064]{1,0:T(8,128)(2,1)S(1)} collective-permute-done((bf16[16,8064]{1,0:T(8,128)(2,1)S(1)}, bf16[16,8064]{1,0:T(8,128)(2,1)S(1)}, u32[]{:S(2)}, u32[]{:S(2)}) %collective-permute-start.13) | collective-permute-done | bytes 258080 | tf_op jit(solution)/shard_map/ppermute | solution.py:302
  45.1 2.5 %collective-permute-start.4 = (bf16[16,8064]{1,0:T(8,128)(2,1)}, bf16[16,8064]{1,0:T(8,128)(2,1)S(1)}, u32[]{:S(2)}, u32[]{:S(2)}) collective-permute-start(bf16[16,8064]{1,0:T(8,128)(2,1)} %shard_map.55.refs_1_), channel_id=1, source_target_pairs={{0,3},{1,0},{2,1},{3,2},{4,7},{5,4},{6,5},{7,6},{8,11},{9,8},{10,9... | collective-permute-start | bytes 774152 | tf_op jit(solution)/shard_map/ppermute | solution.py:299
  47.7 0.0 collective-permute-done.10.refs_13_
  47.7 0.9 collective-permute-start.3
  48.6 0.0 collective-permute-done.8.refs_8_
  48.6 0.0 collective-permute-start.2
  48.6 1.6 %collective-permute-done.15.refs_10_ = bf16[16,8064]{1,0:T(8,128)(2,1)S(1)} collective-permute-done((bf16[16,8064]{1,0:T(8,128)(2,1)S(1)}, bf16[16,8064]{1,0:T(8,128)(2,1)S(1)}, u32[]{:S(2)}, u32[]{:S(2)}) %collective-permute-start.15) | collective-permute-done | bytes 258080 | tf_op jit(solution)/shard_map/ppermute | solution.py:302
  50.2 1.8 %collective-permute-start.18 = (bf16[16,8064]{1,0:T(8,128)(2,1)S(1)}, bf16[16,8064]{1,0:T(8,128)(2,1)S(1)}, u32[]{:S(2)}, u32[]{:S(2)}) collective-permute-start(bf16[16,8064]{1,0:T(8,128)(2,1)S(1)} %collective-permute-done.17.refs_11_), channel_id=1, source_target_pairs={{0,8},{8,0},{16,24},{24,16},{32,40},{40,32},{48,56},{56,48},{64,72... | collective-permute-start | bytes 774152 | tf_op jit(solution)/shard_map/ppermute | solution.py:305
  52.1 0.0 collective-permute-done.6.refs_14_
  52.1 0.1 collective-permute-start.14
  52.2 0.2 collective-permute-done.4.refs_3_
  52.4 2.0 %collective-permute-start.9 = (bf16[16,8064]{1,0:T(8,128)(2,1)S(1)}, bf16[16,8064]{1,0:T(8,128)(2,1)S(1)}, u32[]{:S(2)}, u32[]{:S(2)}) collective-permute-start(bf16[16,8064]{1,0:T(8,128)(2,1)S(1)} %collective-permute-done.8.refs_8_), channel_id=1, source_target_pairs={{0,8},{8,0},{16,24},{24,16},{32,40},{40,32},{48,56},{56,48},{64,72... | collective-permute-start | bytes 774152 | tf_op jit(solution)/shard_map/ppermute | solution.py:305
  54.4 0.0 collective-permute-done.3.refs_2_
  54.4 2.1 %collective-permute-start.16 = (bf16[16,8064]{1,0:T(8,128)(2,1)S(1)}, bf16[16,8064]{1,0:T(8,128)(2,1)S(1)}, u32[]{:S(2)}, u32[]{:S(2)}) collective-permute-start(bf16[16,8064]{1,0:T(8,128)(2,1)S(1)} %collective-permute-done.15.refs_10_), channel_id=1, source_target_pairs={{0,8},{8,0},{16,24},{24,16},{32,40},{40,32},{48,56},{56,48},{64,72... | collective-permute-start | bytes 774152 | tf_op jit(solution)/shard_map/ppermute | solution.py:305
  56.5 0.6 collective-permute-done.2.refs_0_
  57.2 0.0 collective-permute-done.18.refs_19_
  57.2 0.0 collective-permute-done.9.refs_16_
  57.2 0.5 collective-permute-done.16.refs_18_
  57.7 1.6 %collective-permute-start.20 = (bf16[16,8064]{1,0:T(8,128)(2,1)S(1)}, bf16[16,8064]{1,0:T(8,128)(2,1)S(1)}, u32[]{:S(2)}, u32[]{:S(2)}) collective-permute-start(bf16[16,8064]{1,0:T(8,128)(2,1)S(1)} %collective-permute-done.3.refs_2_), channel_id=1, source_target_pairs={{0,3},{1,0},{2,1},{3,2},{4,7},{5,4},{6,5},{7,6},{8,11},{9,8},{10,9... | collective-permute-start | bytes 774152 | tf_op jit(solution)/shard_map/ppermute | solution.py:299
  59.3 0.2 collective-permute-start.21
  59.4 3.2 %collective-permute-start.22 = (bf16[16,8064]{1,0:T(8,128)(2,1)S(1)}, bf16[16,8064]{1,0:T(8,128)(2,1)S(1)}, u32[]{:S(2)}, u32[]{:S(2)}) collective-permute-start(bf16[16,8064]{1,0:T(8,128)(2,1)S(1)} %collective-permute-done.4.refs_3_), channel_id=1, source_target_pairs={{0,7},{1,4},{2,5},{3,6},{4,3},{5,0},{6,1},{7,2},{8,15},{9,12},{10,... | collective-permute-start | bytes 774152 | tf_op jit(solution)/shard_map/ppermute | solution.py:299
  62.7 0.9 copy-done
  63.7 20.4 %shard_map.56.refs_21_ = bf16[101,128,256]{2,1,0:T(8,128)(2,1)} custom-call(bf16[16,8064]{1,0:T(8,128)(2,1)S(1)} %collective-permute-done.2.refs_0_, bf16[16,8064]{1,0:T(8,128)(2,1)S(1)} %copy-done, bf16[16,8064]{1,0:T(8,128)(2,1)S(1)} %collective-permute-done.3.refs_2_, bf16[16,8064]{1,0:T(8,128)(2,1)S(1)} %collective-permute-done.4.refs_3_, ...), custom_call_target="tpu_custom_call" | custom-call | flops 12800000000 | bytes 10000000 | tf_op jit(solution)/shard_map/pallas_call | solution.py:262
  84.1 0.0 collective-permute-done.21.refs_2_
  84.1 0.0 collective-permute-done.22.refs_3_
  84.1 0.0 collective-permute-done.19.refs_0_
  84.2 20.6 %shard_map.57 = bf16[101,128,256]{2,1,0:T(8,128)(2,1)} custom-call(bf16[16,8064]{1,0:T(8,128)(2,1)S(1)} %collective-permute-done.19.refs_0_, bf16[16,8064]{1,0:T(8,128)(2,1)S(1)} %collective-permute-done.20.refs_1_, bf16[16,8064]{1,0:T(8,128)(2,1)S(1)} %collective-permute-done.21.refs_2_, ...), custom_call_target="tpu_custom_call", output_to_operand_aliasing={{}: (21, {})} | custom-call | flops 12800000000 | bytes 10000000 | tf_op jit(solution)/shard_map/pallas_call | solution.py:262
  (30 shorter events, 0.1 us)
Async XLA Ops:
  5.2 9.3 %collective-permute-start = (bf16[16,8064]{1,0:T(8,128)(2,1)}, bf16[16,8064]{1,0:T(8,128)(2,1)S(1)}, u32[]{:S(2)}, u32[]{:S(2)}) collective-permute-start(bf16[16,8064]{1,0:T(8,128)(2,1)} %shard_map.55.refs_1_), channel_id=1, source_target_pairs={{2,0},{3,16},{0,32},{1,48},{6,64},{7,80},{4,96},{5,112},{10,8},{11... | collective-permute-start | bytes 774152 | tf_op jit(solution)/shard_map/ppermute | solution.py:310
  14.5 14.0 %collective-permute-start.11 = (bf16[16,8064]{1,0:T(8,128)(2,1)S(1)}, bf16[16,8064]{1,0:T(8,128)(2,1)S(1)}, u32[]{:S(2)}, u32[]{:S(2)}) collective-permute-start(bf16[16,8064]{1,0:T(8,128)(2,1)S(1)} %collective-permute-done.refs_4_), channel_id=1, source_target_pairs={{0,48},{8,56},{16,0},{24,8},{32,16},{40,24},{48,32},{56,40},{64,11... | collective-permute-start | bytes 774152 | tf_op jit(solution)/shard_map/ppermute | solution.py:302
  23.1 13.0 %collective-permute-start.7 = (bf16[16,8064]{1,0:T(8,128)(2,1)S(1)}, bf16[16,8064]{1,0:T(8,128)(2,1)S(1)}, u32[]{:S(2)}, u32[]{:S(2)}) collective-permute-start(bf16[16,8064]{1,0:T(8,128)(2,1)S(1)} %collective-permute-done.refs_4_), channel_id=1, source_target_pairs={{0,64},{8,72},{16,80},{24,88},{32,96},{40,104},{48,112},{56,120},{... | collective-permute-start | bytes 774152 | tf_op jit(solution)/shard_map/ppermute | solution.py:302
  26.3 9.9 %collective-permute-start.1 = (bf16[16,8064]{1,0:T(8,128)(2,1)S(1)}, bf16[16,8064]{1,0:T(8,128)(2,1)S(1)}, u32[]{:S(2)}, u32[]{:S(2)}) collective-permute-start(bf16[16,8064]{1,0:T(8,128)(2,1)S(1)} %collective-permute-done.refs_4_), channel_id=1, source_target_pairs={{0,8},{8,0},{16,24},{24,16},{32,40},{40,32},{48,56},{56,48},{64,72... | collective-permute-start | bytes 774152 | tf_op jit(solution)/shard_map/ppermute | solution.py:305
  27.4 9.2 %collective-permute-start.5 = (bf16[16,8064]{1,0:T(8,128)(2,1)S(1)}, bf16[16,8064]{1,0:T(8,128)(2,1)S(1)}, u32[]{:S(2)}, u32[]{:S(2)}) collective-permute-start(bf16[16,8064]{1,0:T(8,128)(2,1)S(1)} %collective-permute-done.refs_4_), channel_id=1, source_target_pairs={{0,16},{8,24},{16,32},{24,40},{32,48},{40,56},{48,0},{56,8},{64,80... | collective-permute-start | bytes 774152 | tf_op jit(solution)/shard_map/ppermute | solution.py:302
  28.5 34.1 %copy-start.1 = (bf16[16,8064]{1,0:T(8,128)(2,1)}, bf16[16,8064]{1,0:T(8,128)(2,1)S(1)}, u32[]{:S(2)}) copy-start(bf16[16,8064]{1,0:T(8,128)(2,1)S(1)} %collective-permute-done.11.refs_7_) | copy-start | bytes 774148
  28.5 10.5 %collective-permute-start.17 = (bf16[16,8064]{1,0:T(8,128)(2,1)S(1)}, bf16[16,8064]{1,0:T(8,128)(2,1)S(1)}, u32[]{:S(2)}, u32[]{:S(2)}) collective-permute-start(bf16[16,8064]{1,0:T(8,128)(2,1)S(1)} %collective-permute-done.11.refs_7_), channel_id=1, source_target_pairs={{0,112},{8,120},{16,64},{24,72},{32,80},{40,88},{48,96},{56,104},{... | collective-permute-start | bytes 774152 | tf_op jit(solution)/shard_map/ppermute | solution.py:302
  34.4 4.7 %collective-permute-start.12 = (bf16[16,8064]{1,0:T(8,128)(2,1)S(1)}, bf16[16,8064]{1,0:T(8,128)(2,1)S(1)}, u32[]{:S(2)}, u32[]{:S(2)}) collective-permute-start(bf16[16,8064]{1,0:T(8,128)(2,1)S(1)} %collective-permute-done.11.refs_7_), channel_id=1, source_target_pairs={{0,8},{8,0},{16,24},{24,16},{32,40},{40,32},{48,56},{56,48},{64,72... | collective-permute-start | bytes 774152 | tf_op jit(solution)/shard_map/ppermute | solution.py:305
  36.1 9.0 %collective-permute-start.13 = (bf16[16,8064]{1,0:T(8,128)(2,1)S(1)}, bf16[16,8064]{1,0:T(8,128)(2,1)S(1)}, u32[]{:S(2)}, u32[]{:S(2)}) collective-permute-start(bf16[16,8064]{1,0:T(8,128)(2,1)S(1)} %collective-permute-done.7.refs_5_), channel_id=1, source_target_pairs={{0,48},{8,56},{16,0},{24,8},{32,16},{40,24},{48,32},{56,40},{64,11... | collective-permute-start | bytes 774152 | tf_op jit(solution)/shard_map/ppermute | solution.py:302
  36.1 26.5 %copy-start.2 = (bf16[16,8064]{1,0:T(8,128)(2,1)}, bf16[16,8064]{1,0:T(8,128)(2,1)S(1)}, u32[]{:S(2)}) copy-start(bf16[16,8064]{1,0:T(8,128)(2,1)S(1)} %collective-permute-done.1.refs_12_) | copy-start | bytes 774148
  36.1 11.5 %collective-permute-start.10 = (bf16[16,8064]{1,0:T(8,128)(2,1)S(1)}, bf16[16,8064]{1,0:T(8,128)(2,1)S(1)}, u32[]{:S(2)}, u32[]{:S(2)}) collective-permute-start(bf16[16,8064]{1,0:T(8,128)(2,1)S(1)} %collective-permute-done.7.refs_5_), channel_id=1, source_target_pairs={{0,8},{8,0},{16,24},{24,16},{32,40},{40,32},{48,56},{56,48},{64,72... | collective-permute-start | bytes 774152 | tf_op jit(solution)/shard_map/ppermute | solution.py:305
  36.7 11.9 %collective-permute-start.8 = (bf16[16,8064]{1,0:T(8,128)(2,1)S(1)}, bf16[16,8064]{1,0:T(8,128)(2,1)S(1)}, u32[]{:S(2)}, u32[]{:S(2)}) collective-permute-start(bf16[16,8064]{1,0:T(8,128)(2,1)S(1)} %collective-permute-done.7.refs_5_), channel_id=1, source_target_pairs={{0,16},{8,24},{16,32},{24,40},{32,48},{40,56},{48,0},{56,8},{64,80... | collective-permute-start | bytes 774152 | tf_op jit(solution)/shard_map/ppermute | solution.py:302
  39.0 23.6 %copy-start.3 = (bf16[16,8064]{1,0:T(8,128)(2,1)}, bf16[16,8064]{1,0:T(8,128)(2,1)S(1)}, u32[]{:S(2)}) copy-start(bf16[16,8064]{1,0:T(8,128)(2,1)S(1)} %collective-permute-done.17.refs_11_) | copy-start | bytes 774148
  39.0 11.2 %collective-permute-start.15 = (bf16[16,8064]{1,0:T(8,128)(2,1)S(1)}, bf16[16,8064]{1,0:T(8,128)(2,1)S(1)}, u32[]{:S(2)}, u32[]{:S(2)}) collective-permute-start(bf16[16,8064]{1,0:T(8,128)(2,1)S(1)} %collective-permute-done.5.refs_6_), channel_id=1, source_target_pairs={{0,16},{8,24},{16,32},{24,40},{32,48},{40,56},{48,0},{56,8},{64,80... | collective-permute-start | bytes 774152 | tf_op jit(solution)/shard_map/ppermute | solution.py:302
  39.1 23.6 %copy-start.4 = (bf16[16,8064]{1,0:T(8,128)(2,1)}, bf16[16,8064]{1,0:T(8,128)(2,1)S(1)}, u32[]{:S(2)}) copy-start(bf16[16,8064]{1,0:T(8,128)(2,1)S(1)} %collective-permute-done.12.refs_15_) | copy-start | bytes 774148
  39.1 13.0 %collective-permute-start.6 = (bf16[16,8064]{1,0:T(8,128)(2,1)S(1)}, bf16[16,8064]{1,0:T(8,128)(2,1)S(1)}, u32[]{:S(2)}, u32[]{:S(2)}) collective-permute-start(bf16[16,8064]{1,0:T(8,128)(2,1)S(1)} %collective-permute-done.5.refs_6_), channel_id=1, source_target_pairs={{0,8},{8,0},{16,24},{24,16},{32,40},{40,32},{48,56},{56,48},{64,72... | collective-permute-start | bytes 774152 | tf_op jit(solution)/shard_map/ppermute | solution.py:305
  45.1 17.5 %copy-start.5 = (bf16[16,8064]{1,0:T(8,128)(2,1)}, bf16[16,8064]{1,0:T(8,128)(2,1)S(1)}, u32[]{:S(2)}) copy-start(bf16[16,8064]{1,0:T(8,128)(2,1)S(1)} %collective-permute-done.13.refs_9_) | copy-start | bytes 774148
  45.1 7.3 %collective-permute-start.4 = (bf16[16,8064]{1,0:T(8,128)(2,1)}, bf16[16,8064]{1,0:T(8,128)(2,1)S(1)}, u32[]{:S(2)}, u32[]{:S(2)}) collective-permute-start(bf16[16,8064]{1,0:T(8,128)(2,1)} %shard_map.55.refs_1_), channel_id=1, source_target_pairs={{0,3},{1,0},{2,1},{3,2},{4,7},{5,4},{6,5},{7,6},{8,11},{9,8},{10,9... | collective-permute-start | bytes 774152 | tf_op jit(solution)/shard_map/ppermute | solution.py:299
  47.7 15.0 %copy-start.6 = (bf16[16,8064]{1,0:T(8,128)(2,1)}, bf16[16,8064]{1,0:T(8,128)(2,1)S(1)}, u32[]{:S(2)}) copy-start(bf16[16,8064]{1,0:T(8,128)(2,1)S(1)} %collective-permute-done.10.refs_13_) | copy-start | bytes 774148
  47.7 6.7 %collective-permute-start.3 = (bf16[16,8064]{1,0:T(8,128)(2,1)}, bf16[16,8064]{1,0:T(8,128)(2,1)S(1)}, u32[]{:S(2)}, u32[]{:S(2)}) collective-permute-start(bf16[16,8064]{1,0:T(8,128)(2,1)} %shard_map.55.refs_1_), channel_id=1, source_target_pairs={{0,4},{1,5},{2,6},{3,7},{4,0},{5,1},{6,2},{7,3},{8,12},{9,13},{10,... | collective-permute-start | bytes 774152 | tf_op jit(solution)/shard_map/ppermute | solution.py:299
  48.6 14.0 %copy-start.7 = (bf16[16,8064]{1,0:T(8,128)(2,1)}, bf16[16,8064]{1,0:T(8,128)(2,1)S(1)}, u32[]{:S(2)}) copy-start(bf16[16,8064]{1,0:T(8,128)(2,1)S(1)} %collective-permute-done.8.refs_8_) | copy-start | bytes 774148
  48.6 8.6 %collective-permute-start.2 = (bf16[16,8064]{1,0:T(8,128)(2,1)}, bf16[16,8064]{1,0:T(8,128)(2,1)S(1)}, u32[]{:S(2)}, u32[]{:S(2)}) collective-permute-start(bf16[16,8064]{1,0:T(8,128)(2,1)} %shard_map.55.refs_1_), channel_id=1, source_target_pairs={{0,1},{1,2},{2,3},{3,0},{4,5},{5,6},{6,7},{7,4},{8,9},{9,10},{10,1... | collective-permute-start | bytes 774152 | tf_op jit(solution)/shard_map/ppermute | solution.py:299
  50.2 12.4 %copy-start.8 = (bf16[16,8064]{1,0:T(8,128)(2,1)}, bf16[16,8064]{1,0:T(8,128)(2,1)S(1)}, u32[]{:S(2)}) copy-start(bf16[16,8064]{1,0:T(8,128)(2,1)S(1)} %collective-permute-done.15.refs_10_) | copy-start | bytes 774148
  50.2 6.9 %collective-permute-start.18 = (bf16[16,8064]{1,0:T(8,128)(2,1)S(1)}, bf16[16,8064]{1,0:T(8,128)(2,1)S(1)}, u32[]{:S(2)}, u32[]{:S(2)}) collective-permute-start(bf16[16,8064]{1,0:T(8,128)(2,1)S(1)} %collective-permute-done.17.refs_11_), channel_id=1, source_target_pairs={{0,8},{8,0},{16,24},{24,16},{32,40},{40,32},{48,56},{56,48},{64,72... | collective-permute-start | bytes 774152 | tf_op jit(solution)/shard_map/ppermute | solution.py:305
  52.1 10.6 %copy-start.9 = (bf16[16,8064]{1,0:T(8,128)(2,1)}, bf16[16,8064]{1,0:T(8,128)(2,1)S(1)}, u32[]{:S(2)}) copy-start(bf16[16,8064]{1,0:T(8,128)(2,1)S(1)} %collective-permute-done.6.refs_14_) | copy-start | bytes 774148
  52.1 5.1 %collective-permute-start.14 = (bf16[16,8064]{1,0:T(8,128)(2,1)S(1)}, bf16[16,8064]{1,0:T(8,128)(2,1)S(1)}, u32[]{:S(2)}, u32[]{:S(2)}) collective-permute-start(bf16[16,8064]{1,0:T(8,128)(2,1)S(1)} %collective-permute-done.13.refs_9_), channel_id=1, source_target_pairs={{0,8},{8,0},{16,24},{24,16},{32,40},{40,32},{48,56},{56,48},{64,72... | collective-permute-start | bytes 774152 | tf_op jit(solution)/shard_map/ppermute | solution.py:305
  52.4 4.8 %collective-permute-start.9 = (bf16[16,8064]{1,0:T(8,128)(2,1)S(1)}, bf16[16,8064]{1,0:T(8,128)(2,1)S(1)}, u32[]{:S(2)}, u32[]{:S(2)}) collective-permute-start(bf16[16,8064]{1,0:T(8,128)(2,1)S(1)} %collective-permute-done.8.refs_8_), channel_id=1, source_target_pairs={{0,8},{8,0},{16,24},{24,16},{32,40},{40,32},{48,56},{56,48},{64,72... | collective-permute-start | bytes 774152 | tf_op jit(solution)/shard_map/ppermute | solution.py:305
  54.4 3.3 %collective-permute-start.16 = (bf16[16,8064]{1,0:T(8,128)(2,1)S(1)}, bf16[16,8064]{1,0:T(8,128)(2,1)S(1)}, u32[]{:S(2)}, u32[]{:S(2)}) collective-permute-start(bf16[16,8064]{1,0:T(8,128)(2,1)S(1)} %collective-permute-done.15.refs_10_), channel_id=1, source_target_pairs={{0,8},{8,0},{16,24},{24,16},{32,40},{40,32},{48,56},{56,48},{64,72... | collective-permute-start | bytes 774152 | tf_op jit(solution)/shard_map/ppermute | solution.py:305
  57.2 5.5 %copy-start.10 = (bf16[16,8064]{1,0:T(8,128)(2,1)}, bf16[16,8064]{1,0:T(8,128)(2,1)S(1)}, u32[]{:S(2)}) copy-start(bf16[16,8064]{1,0:T(8,128)(2,1)S(1)} %collective-permute-done.18.refs_19_) | copy-start | bytes 774148
  57.2 5.5 %copy-start.11 = (bf16[16,8064]{1,0:T(8,128)(2,1)}, bf16[16,8064]{1,0:T(8,128)(2,1)S(1)}, u32[]{:S(2)}) copy-start(bf16[16,8064]{1,0:T(8,128)(2,1)S(1)} %collective-permute-done.14.refs_17_) | copy-start | bytes 774148
  57.2 5.5 %copy-start.12 = (bf16[16,8064]{1,0:T(8,128)(2,1)}, bf16[16,8064]{1,0:T(8,128)(2,1)S(1)}, u32[]{:S(2)}) copy-start(bf16[16,8064]{1,0:T(8,128)(2,1)S(1)} %collective-permute-done.9.refs_16_) | copy-start | bytes 774148
  57.7 5.0 %copy-start.13 = (bf16[16,8064]{1,0:T(8,128)(2,1)}, bf16[16,8064]{1,0:T(8,128)(2,1)S(1)}, u32[]{:S(2)}) copy-start(bf16[16,8064]{1,0:T(8,128)(2,1)S(1)} %collective-permute-done.16.refs_18_) | copy-start | bytes 774148
  57.7 26.5 %collective-permute-start.20 = (bf16[16,8064]{1,0:T(8,128)(2,1)S(1)}, bf16[16,8064]{1,0:T(8,128)(2,1)S(1)}, u32[]{:S(2)}, u32[]{:S(2)}) collective-permute-start(bf16[16,8064]{1,0:T(8,128)(2,1)S(1)} %collective-permute-done.3.refs_2_), channel_id=1, source_target_pairs={{0,3},{1,0},{2,1},{3,2},{4,7},{5,4},{6,5},{7,6},{8,11},{9,8},{10,9... | collective-permute-start | bytes 774152 | tf_op jit(solution)/shard_map/ppermute | solution.py:299
  59.3 24.9 %collective-permute-start.19 = (bf16[16,8064]{1,0:T(8,128)(2,1)S(1)}, bf16[16,8064]{1,0:T(8,128)(2,1)S(1)}, u32[]{:S(2)}, u32[]{:S(2)}) collective-permute-start(bf16[16,8064]{1,0:T(8,128)(2,1)S(1)} %collective-permute-done.3.refs_2_), channel_id=1, source_target_pairs={{0,1},{1,2},{2,3},{3,0},{4,5},{5,6},{6,7},{7,4},{8,9},{9,10},{10,1... | collective-permute-start | bytes 774152 | tf_op jit(solution)/shard_map/ppermute | solution.py:299
  59.3 24.9 %collective-permute-start.21 = (bf16[16,8064]{1,0:T(8,128)(2,1)S(1)}, bf16[16,8064]{1,0:T(8,128)(2,1)S(1)}, u32[]{:S(2)}, u32[]{:S(2)}) collective-permute-start(bf16[16,8064]{1,0:T(8,128)(2,1)S(1)} %collective-permute-done.2.refs_0_), channel_id=1, source_target_pairs={{0,1},{1,2},{2,3},{3,0},{4,5},{5,6},{6,7},{7,4},{8,9},{9,10},{10,1... | collective-permute-start | bytes 774152 | tf_op jit(solution)/shard_map/ppermute | solution.py:299
  59.4 24.7 %collective-permute-start.22 = (bf16[16,8064]{1,0:T(8,128)(2,1)S(1)}, bf16[16,8064]{1,0:T(8,128)(2,1)S(1)}, u32[]{:S(2)}, u32[]{:S(2)}) collective-permute-start(bf16[16,8064]{1,0:T(8,128)(2,1)S(1)} %collective-permute-done.4.refs_3_), channel_id=1, source_target_pairs={{0,7},{1,4},{2,5},{3,6},{4,3},{5,0},{6,1},{7,2},{8,15},{9,12},{10,... | collective-permute-start | bytes 774152 | tf_op jit(solution)/shard_map/ppermute | solution.py:299
  62.7 0.9 copy-start

commit v5 on v4

--- a/solution.py
+++ b/solution.py
@@ -116,17 +116,25 @@
     n_rows, n_cols = len(row_keys), 2 * len(col_keys)
     p, q, core = lax.axis_index("rcv"), lax.axis_index("src") // 2, lax.axis_index("src") % 2
     row_places = [step(p, *key) for key in row_keys]
-    col_places = [c * 8 + step(step(q, *key), 2, 0) for c in (core, 1 - core) for key in col_keys]
     row_refs, refs = refs[:n_rows], refs[n_rows:]
     col_refs, refs = refs[:n_cols], refs[n_cols:]
-    table_ref, out_ref, cols, rows, turned, cross, *lagged, staged, sems = refs[:1] + refs[1 + n_kept :]
+    table_from, out_ref, cols, table_ref, rows, turned, cross, *lagged, staged, sems, in_sems = (
+        refs[:1] + refs[1 + n_kept :]
+    )
     lane = lax.broadcasted_iota(jnp.int32, (16, 128), 1)
     same_bin = (lane % 8) == lax.broadcasted_iota(jnp.int32, (16, 128), 0) % 8
     zero = jnp.zeros((), jnp.bfloat16)
     groups = n_rows * OWN // 8
 
+    loads = [pltpu.make_async_copy(table_from, table_ref, in_sems.at[4 * n_cols])]
     for k, ref in enumerate(col_refs):
-        cols[pl.ds(pl.multiple_of(col_places[k] * OWN, OWN), OWN), :] = ref[...]
+        c = core if k < n_cols // 2 else 1 - core
+        for u, key in enumerate(col_keys[k % len(col_keys)]):
+            at = pl.ds(pl.multiple_of((c * 8 + step(step(q, *key), 2, 0)) * OWN, OWN), OWN)
+            piece = ref.at[u * OWN : (u + 1) * OWN, :]
+            loads.append(pltpu.make_async_copy(piece, cols.at[at, :], in_sems.at[4 * k + u]))
+    for load in loads[1:] + loads[:1]:
+        load.start()
 
     def spread(first, last, shift):
         minus = (lax.broadcasted_iota(jnp.int32, (OWN, 128), 1) // shift) % 2 == 1
@@ -142,6 +150,8 @@
 
     spread(0, NB, 8)
     spread(NB, TILES, 32)
+    for load in loads[1:]:
+        load.wait()
 
     def cross_of(*accs):
         accs = accs[:DEPTH], accs[DEPTH:]
@@ -249,47 +259,37 @@
         emit(n_rows - 1)
 
     pl.run_scoped(cross_of, *[pltpu.ACC(mxu)((128, 256), jnp.float32) for mxu in [0] * DEPTH + [1] * DEPTH])
+    loads[0].wait()
     pl.run_scoped(lags_of, *[pltpu.ACC(mxu)((LAG_TILE, 256), jnp.float32) for mxu in [0] * 4 + [1] * 4])
     for k in range(n_rows - 2, n_rows):
         out_copy(k).wait()
 
 
 def correlate(rows, cols, swapped, shape, kept=()):
-    row_blocks, col_blocks = list(rows.values()), list(cols.values()) + [swapped[key] for key in cols]
-    n, m = OWN * len(row_blocks), OWN * len(col_blocks)
+    row_blocks, col_blocks = list(rows.values()), list(cols.values()) + [swapped[keys] for keys in cols]
+    n, m = OWN * len(row_blocks), 4 * OWN * len(col_blocks)
     vmem, anywhere = pl.BlockSpec(memory_space=pltpu.VMEM), pl.BlockSpec(memory_space=pl.ANY)
     inputs = (*row_blocks, *col_blocks, jnp.asarray(lag_tables(), jnp.bfloat16), *kept)
     return pl.pallas_call(
         functools.partial(correlate_kernel, tuple(rows), tuple(cols), len(kept)),
-        in_specs=[vmem] * (len(row_blocks) + len(col_blocks) + 1) + [anywhere] * len(kept),
+        in_specs=[vmem] * len(row_blocks) + [anywhere] * (len(col_blocks) + 1 + len(kept)),
         out_specs=anywhere,
         out_shape=jax.ShapeDtypeStruct(shape, jnp.bfloat16),
         input_output_aliases={len(inputs) - 1: 0} if kept else {},
         scratch_shapes=[
             pltpu.VMEM((m, LANES), jnp.bfloat16),
+            pltpu.VMEM((2, len(segments()), LAG_TILE, 256), jnp.bfloat16),
             pltpu.VMEM((n, LANES), jnp.float32),
             pltpu.VMEM((n, LANES), jnp.float32),
             pltpu.VMEM((2, n * F, m), jnp.bfloat16),
             *[pltpu.VMEM((2, OWN * LAG_ROWS, 128), jnp.float32)] * 4,
             pltpu.VMEM((2, LAGS, OWN, m), jnp.bfloat16),
             pltpu.SemaphoreType.DMA((2,)),
+            pltpu.SemaphoreType.DMA((4 * len(col_blocks) + 1,)),
         ],
-        compiler_params=pltpu.CompilerParams(vmem_limit_bytes=52 * 1024 * 1024),
+        compiler_params=pltpu.CompilerParams(vmem_limit_bytes=54 * 1024 * 1024),
         cost_estimate=pl.CostEstimate(flops=n * 2 * 10**8, bytes_accessed=10**7, transcendentals=0),
     )(*inputs)
-
-
-def near(block, move):
-    return {(0, 0): block, (0, 1): move(block, 0, 1), (-1, 0): move(block, 1, 0), (1, 0): move(block, -1, 0)}
-
-
-def far(found, move):
-    return {
-        (-1, 1): move(found[0, 1], 1, 0),
-        (1, 1): move(found[0, 1], -1, 0),
-        (2, 0): move(found[-1, 0], 1, 0),
-        (2, 1): move(found[1, 0], -1, 1),
-    }
 
 
 def body(spectra, offsets, channel_mask):
@@ -308,17 +308,30 @@
         ((i * 2 + k) * 8 + step(j, 2, 0), (j * 2 + k) * 8 + i) for i in range(8) for k in range(2) for j in range(8)
     ]
     turned = lax.ppermute(white, ("src", "rcv"), flip)
-    cols = near(turned, over_src)
-    swapped = {(0, 0): other_core(turned)}
-    white, swapped[0, 0] = lax.optimization_barrier((white, swapped[0, 0]))
-    rows = near(white, over_rcv)
-    more = far(cols, over_src)
-    swapped |= {key: other_core(value) for key, value in (cols | more).items() if key != (0, 0)}
-    cols |= more
-    rows, swapped = lax.optimization_barrier((rows, swapped))
+    side, turned = lax.optimization_barrier((over_rcv(white, 0, 1), turned))
+    rows = {(0, 0): white, (0, 1): side}
+
+    cols = {(0, 0): turned}
+    for key in ((-1, 0), (1, 0), (0, 1), (-1, 1), (1, 1)):
+        cols[key] = over_src(turned, -key[0], key[1])
+    cols[2, 0] = over_src(cols[-1, 0], 1, 0)
+    cols[2, 1] = over_src(cols[1, 1], -1, 0)
+    pieces = ((0, 0), (-1, 0), (1, 0), (0, 1)), ((-1, 1), (1, 1), (2, 0), (2, 1))
+    cols = {keys: jnp.concatenate([cols[key] for key in keys], 0) for keys in pieces}
+    swapped = {keys: other_core(value) for keys, value in cols.items()}
+
+    white, cols[pieces[0]] = lax.optimization_barrier((white, cols[pieces[0]]))
+    rows[-1, 0], rows[1, 0] = over_rcv(white, 1, 0), over_rcv(white, -1, 0)
+    side, before, after, swapped[pieces[0]] = lax.optimization_barrier((side, rows[-1, 0], rows[1, 0], swapped[pieces[0]]))
+    late = {
+        (-1, 1): over_rcv(side, 1, 0),
+        (1, 1): over_rcv(side, -1, 0),
+        (2, 0): over_rcv(before, 1, 0),
+        (2, 1): over_rcv(after, -1, 1),
+    }
     shape = (LAGS, 8 * OWN, 16 * OWN)
     first = correlate(rows, cols, swapped, shape)
-    return correlate(far(rows, over_rcv), cols, swapped, shape, (first,))
+    return correlate(late, cols, swapped, shape, (first,))
 
 
 def solution(mesh):

time: 106 us -> 116 us (1.094)
  waiting for transfers between devices: 12.5 us -> 34.2 us
  starting transfers between devices: 44.8 us -> 32.2 us
  local copies, waits for them, and re-layouts: 2.83 us -> 4.57 us
    ppermute x7, waiting for transfers between devices: 5.58 us -> 19.4 us  [over_src(): lax.ppermute(value, 'src', [(i, 2 * step(i // 2, ring, side) + i % 2) for...]
    ppermute x8 -> x2, starting transfers between devices: 13.3 us -> 1.51 us  [other_core(): return lax.ppermute(value, 'src', [(i, i ^ 1) for i in range(16)])]
    ppermute x7, waiting for transfers between devices: 0.89 us -> 12.2 us  [over_rcv(): lax.ppermute(value, 'rcv', [(i, step(i, ring, side)) for i in range(8)])]
    ppermute x7, starting transfers between devices: 19.4 us -> 16.2 us  [over_src(): lax.ppermute(value, 'src', [(i, 2 * step(i // 2, ring, side) + i % 2) for...]
    ppermute x1, waiting for transfers between devices: 5.54 us -> 2.55 us  [body(): turned = lax.ppermute(white, ('src', 'rcv'), flip)]
    ppermute x7, starting transfers between devices: 8.39 us -> 10.7 us  [over_rcv(): lax.ppermute(value, 'rcv', [(i, step(i, ring, side)) for i in range(8)])]
    unnamed x29, local copies, waits for them, and re-layouts: 2.83 us -> 4.52 us
  transfers between devices with their start and end apart: 23 -> 17, of which waited for: 9 -> 7; matrix products, arithmetic and copies ran while one was open for 0% -> 0% of each run, Pallas kernels for 19% -> 17%
where the time goes in v5:
time: 116 us; the launch traced here: 115 us
  Pallas kernels  43.4 us (37%)
  waiting for transfers between devices  34.2 us (29%)
  starting transfers between devices  32.2 us (28%)
  local copies, waits for them, and re-layouts  4.57 us (4%)
    pallas_call x2, Pallas kernels, correlate(): pl.pallas_call(functools.partial(correlate_kernel, tuple(rows), tuple(col...  40 us
    ppermute x7, waiting for transfers between devices, over_src(): lax.ppermute(value, 'src', [(i, 2 * step(i // 2, ring, side) + i % 2) for...  19.4 us
    ppermute x7, starting transfers between devices, over_src(): lax.ppermute(value, 'src', [(i, 2 * step(i // 2, ring, side) + i % 2) for...  16.2 us
    ppermute x7, waiting for transfers between devices, over_rcv(): lax.ppermute(value, 'rcv', [(i, step(i, ring, side)) for i in range(8)])  12.2 us
    ppermute x7, starting transfers between devices, over_rcv(): lax.ppermute(value, 'rcv', [(i, step(i, ring, side)) for i in range(8)])  10.7 us
    unnamed x29, local copies, waits for them, and re-layouts  4.52 us
    ppermute x1, starting transfers between devices, body(): turned = lax.ppermute(white, ('src', 'rcv'), flip)  3.74 us
    pallas_call x1, Pallas kernels, whiten(): pl.pallas_call(whiten_kernel, in_specs=[pl.BlockSpec(memory_space=pltpu.S...  3.41 us
  transfers between devices with their start and end apart: 17, of which 7 were waited for; matrix products, arithmetic and copies ran while one was open for 0% of the time, Pallas kernels for 17%

profile of v5, /device:TPU:1, one launch (start us, length us, event | category | flops | bytes accessed | tf_op | source)
XLA Modules:
  0.0 114.8 jit_solution(1943950918143777683)
XLA Ops:
  0.0 1.8 %copy.7.spectra_ref = bf16[16,2,10,400]{3,2,1,0:T(8,128)(2,1)} copy(bf16[16,2,10,400]{3,1,2,0:T(2,128)(2,1)} %param.5) | data formatting | bytes 512000 | tf_op args[0]
  1.8 3.4 %shard_map.55.refs_0_ = bf16[16,8064]{1,0:T(8,128)(2,1)} custom-call(s32[16]{0:T(128)} %mask_ref.1, bf16[16,2,10,400]{3,2,1,0:T(8,128)(2,1)} %copy.7.spectra_ref, s32[16,10]{1,0:T(8,128)} %offsets_ref.1), custom_call_target="tpu_custom_call" | custom-call | tf_op jit(solution)/shard_map/pallas_call | solution.py:87
  5.3 3.7 %collective-permute-start.1 = (bf16[16,8064]{1,0:T(8,128)(2,1)}, bf16[16,8064]{1,0:T(8,128)(2,1)S(1)}, u32[]{:S(2)}, u32[]{:S(2)}) collective-permute-start(bf16[16,8064]{1,0:T(8,128)(2,1)} %shard_map.55.refs_0_), channel_id=1, source_target_pairs={{2,0},{3,16},{0,32},{1,48},{6,64},{7,80},{4,96},{5,112},{10,8},{11... | collective-permute-start | bytes 774152 | tf_op jit(solution)/shard_map/ppermute | solution.py:310
  9.0 3.0 %collective-permute-start = (bf16[16,8064]{1,0:T(8,128)(2,1)}, bf16[16,8064]{1,0:T(8,128)(2,1)S(1)}, u32[]{:S(2)}, u32[]{:S(2)}) collective-permute-start(bf16[16,8064]{1,0:T(8,128)(2,1)} %shard_map.55.refs_0_), channel_id=1, source_target_pairs={{0,4},{1,5},{2,6},{3,7},{4,0},{5,1},{6,2},{7,3},{8,12},{9,13},{10,... | collective-permute-start | bytes 774152 | tf_op jit(solution)/shard_map/ppermute | solution.py:299
  12.0 2.5 %collective-permute-done.1 = bf16[16,8064]{1,0:T(8,128)(2,1)S(1)} collective-permute-done((bf16[16,8064]{1,0:T(8,128)(2,1)}, bf16[16,8064]{1,0:T(8,128)(2,1)S(1)}, u32[]{:S(2)}, u32[]{:S(2)}) %collective-permute-start.1) | collective-permute-done | bytes 258080 | tf_op jit(solution)/shard_map/ppermute | solution.py:310
  14.5 3.3 %collective-permute-done.refs_1_ = bf16[16,8064]{1,0:T(8,128)(2,1)S(1)} collective-permute-done((bf16[16,8064]{1,0:T(8,128)(2,1)}, bf16[16,8064]{1,0:T(8,128)(2,1)S(1)}, u32[]{:S(2)}, u32[]{:S(2)}) %collective-permute-start) | collective-permute-done | bytes 258080 | tf_op jit(solution)/shard_map/ppermute | solution.py:299
  17.9 8.2 %collective-permute-start.13 = (bf16[16,8064]{1,0:T(8,128)(2,1)S(1)}, bf16[16,8064]{1,0:T(8,128)(2,1)S(1)}, u32[]{:S(2)}, u32[]{:S(2)}) collective-permute-start(bf16[16,8064]{1,0:T(8,128)(2,1)S(1)} %collective-permute-done.1), channel_id=1, source_target_pairs={{0,112},{8,120},{16,64},{24,72},{32,80},{40,88},{48,96},{56,104},{... | collective-permute-start | bytes 774152 | tf_op jit(solution)/shard_map/ppermute | solution.py:302
  26.0 1.0 collective-permute-start.12
  27.0 0.0 collective-permute-start.4
  27.0 4.4 %collective-permute-start.3 = (bf16[16,8064]{1,0:T(8,128)(2,1)S(1)}, bf16[16,8064]{1,0:T(8,128)(2,1)S(1)}, u32[]{:S(2)}, u32[]{:S(2)}) collective-permute-start(bf16[16,8064]{1,0:T(8,128)(2,1)S(1)} %collective-permute-done.1), channel_id=1, source_target_pairs={{0,48},{8,56},{16,0},{24,8},{32,16},{40,24},{48,32},{56,40},{64,11... | collective-permute-start | bytes 774152 | tf_op jit(solution)/shard_map/ppermute | solution.py:302
  31.4 0.0 collective-permute-start.2
  31.4 9.8 %collective-permute-done.2 = bf16[16,8064]{1,0:T(8,128)(2,1)S(1)} collective-permute-done((bf16[16,8064]{1,0:T(8,128)(2,1)S(1)}, bf16[16,8064]{1,0:T(8,128)(2,1)S(1)}, u32[]{:S(2)}, u32[]{:S(2)}) %collective-permute-start.2) | collective-permute-done | bytes 258080 | tf_op jit(solution)/shard_map/ppermute | solution.py:302
  41.2 0.0 collective-permute-done.3
  41.2 3.4 %collective-permute-done.4 = bf16[16,8064]{1,0:T(8,128)(2,1)S(1)} collective-permute-done((bf16[16,8064]{1,0:T(8,128)(2,1)S(1)}, bf16[16,8064]{1,0:T(8,128)(2,1)S(1)}, u32[]{:S(2)}, u32[]{:S(2)}) %collective-permute-start.4) | collective-permute-done | bytes 258080 | tf_op jit(solution)/shard_map/ppermute | solution.py:302
  44.7 0.6 collective-permute-start.7
  45.3 0.5 collective-permute-start.14
  45.7 0.0 collective-permute-done.13
  45.7 2.2 %collective-permute-start.15 = (bf16[16,8064]{1,0:T(8,128)(2,1)S(1)}, bf16[16,8064]{1,0:T(8,128)(2,1)S(1)}, u32[]{:S(2)}, u32[]{:S(2)}) collective-permute-start(bf16[16,8064]{1,0:T(8,128)(2,1)S(1)} %collective-permute-done.13), channel_id=1, source_target_pairs={{0,48},{8,56},{16,0},{24,8},{32,16},{40,24},{48,32},{56,40},{64,11... | collective-permute-start | bytes 774152 | tf_op jit(solution)/shard_map/ppermute | solution.py:302
  48.0 0.0 collective-permute-done.12
  48.0 6.2 %collective-permute-done.14 = bf16[16,8064]{1,0:T(8,128)(2,1)S(1)} collective-permute-done((bf16[16,8064]{1,0:T(8,128)(2,1)S(1)}, bf16[16,8064]{1,0:T(8,128)(2,1)S(1)}, u32[]{:S(2)}, u32[]{:S(2)}) %collective-permute-start.14) | collective-permute-done | bytes 258080 | tf_op jit(solution)/shard_map/ppermute | solution.py:302
  54.3 0.0 collective-permute-done.15
  54.3 0.0 copy-start.1
  54.3 0.9 collective-permute-start.16
  55.3 2.1 %collective-permute-start.6 = (bf16[16,8064]{1,0:T(8,128)(2,1)}, bf16[16,8064]{1,0:T(8,128)(2,1)S(1)}, u32[]{:S(2)}, u32[]{:S(2)}) collective-permute-start(bf16[16,8064]{1,0:T(8,128)(2,1)} %shard_map.55.refs_0_), channel_id=1, source_target_pairs={{0,3},{1,0},{2,1},{3,2},{4,7},{5,4},{6,5},{7,6},{8,11},{9,8},{10,9... | collective-permute-start | bytes 774152 | tf_op jit(solution)/shard_map/ppermute | solution.py:299
  57.4 0.0 collective-permute-start.5
  57.4 5.9 %collective-permute-done.6.refs_3_ = bf16[16,8064]{1,0:T(8,128)(2,1)S(1)} collective-permute-done((bf16[16,8064]{1,0:T(8,128)(2,1)}, bf16[16,8064]{1,0:T(8,128)(2,1)S(1)}, u32[]{:S(2)}, u32[]{:S(2)}) %collective-permute-start.6) | collective-permute-done | bytes 258080 | tf_op jit(solution)/shard_map/ppermute | solution.py:299
  63.3 3.0 %collective-permute-done.5.refs_2_ = bf16[16,8064]{1,0:T(8,128)(2,1)S(1)} collective-permute-done((bf16[16,8064]{1,0:T(8,128)(2,1)}, bf16[16,8064]{1,0:T(8,128)(2,1)S(1)}, u32[]{:S(2)}, u32[]{:S(2)}) %collective-permute-start.5) | collective-permute-done | bytes 258080 | tf_op jit(solution)/shard_map/ppermute | solution.py:299
  66.2 0.0 collective-permute-done.7.refs_6_
  66.2 0.4 collective-permute-start.9
  66.6 1.1 collective-permute-start.8
  67.8 0.0 collective-permute-start.10
  67.8 4.1 %collective-permute-start.11 = (bf16[16,8064]{1,0:T(8,128)(2,1)S(1)}, bf16[16,8064]{1,0:T(8,128)(2,1)S(1)}, u32[]{:S(2)}, u32[]{:S(2)}) collective-permute-start(bf16[16,8064]{1,0:T(8,128)(2,1)S(1)} %collective-permute-done.6.refs_3_), channel_id=1, source_target_pairs={{0,7},{1,4},{2,5},{3,6},{4,3},{5,0},{6,1},{7,2},{8,15},{9,12},{10,... | collective-permute-start | bytes 774152 | tf_op jit(solution)/shard_map/ppermute | solution.py:299
  71.9 0.0 collective-permute-done.16.refs_7_
  71.9 0.0 copy-done.4
  71.9 0.0 copy-done
  71.9 0.0 copy-done.1
  72.0 0.9 copy-done.3
  72.9 19.9 %shard_map.56.refs_9_ = bf16[101,128,256]{2,1,0:T(8,128)(2,1)} custom-call(bf16[16,8064]{1,0:T(8,128)(2,1)} %shard_map.55.refs_0_, bf16[16,8064]{1,0:T(8,128)(2,1)} %copy-done.4, bf16[16,8064]{1,0:T(8,128)(2,1)} %copy-done.9, bf16[16,8064]{1,0:T(8,128)(2,1)} %copy-done.5, bf16[64,8064]{1,0:T(8,128)(2,1)} %copy-done, bf16[64,8064]{1,0:T(8,128)(2,1)} %copy-done.1, ...), custom_call_target="tpu_custom_call" | custom-call | flops 12800000000 | bytes 10000000 | tf_op jit(solution)/shard_map/pallas_call | solution.py:273
  92.8 0.0 collective-permute-done.10.refs_2_
  92.8 0.0 copy-start.8
  92.8 0.0 collective-permute-done.11.refs_3_
  92.9 0.0 collective-permute-done.9.refs_1_
  92.9 0.0 collective-permute-done.8.refs_0_
  92.9 0.6 copy-done.8
  93.5 0.1 copy-done.10
  93.6 0.1 copy-done.6
  93.8 0.7 copy-done.7
  94.5 20.1 %shard_map.57 = bf16[101,128,256]{2,1,0:T(8,128)(2,1)} custom-call(bf16[16,8064]{1,0:T(8,128)(2,1)} %copy-done.7, bf16[16,8064]{1,0:T(8,128)(2,1)} %copy-done.6, bf16[16,8064]{1,0:T(8,128)(2,1)} %copy-done.8, bf16[16,8064]{1,0:T(8,128)(2,1)} %copy-done.10, bf16[64,8064]{1,0:T(8,128)(2,1)} %copy-done, ...), custom_call_target="tpu_custom_call", output_to_operand_aliasing={{}: (9, {})} | custom-call | flops 12800000000 | bytes 10000000 | tf_op jit(solution)/shard_map/pallas_call | solution.py:273
  (20 shorter events, 0.2 us)
Async XLA Ops:
  5.3 9.3 %collective-permute-start.1 = (bf16[16,8064]{1,0:T(8,128)(2,1)}, bf16[16,8064]{1,0:T(8,128)(2,1)S(1)}, u32[]{:S(2)}, u32[]{:S(2)}) collective-permute-start(bf16[16,8064]{1,0:T(8,128)(2,1)} %shard_map.55.refs_0_), channel_id=1, source_target_pairs={{2,0},{3,16},{0,32},{1,48},{6,64},{7,80},{4,96},{5,112},{10,8},{11... | collective-permute-start | bytes 774152 | tf_op jit(solution)/shard_map/ppermute | solution.py:310
  9.0 8.9 %collective-permute-start = (bf16[16,8064]{1,0:T(8,128)(2,1)}, bf16[16,8064]{1,0:T(8,128)(2,1)S(1)}, u32[]{:S(2)}, u32[]{:S(2)}) collective-permute-start(bf16[16,8064]{1,0:T(8,128)(2,1)} %shard_map.55.refs_0_), channel_id=1, source_target_pairs={{0,4},{1,5},{2,6},{3,7},{4,0},{5,1},{6,2},{7,3},{8,12},{9,13},{10,... | collective-permute-start | bytes 774152 | tf_op jit(solution)/shard_map/ppermute | solution.py:299
  17.9 54.1 %copy-start.4 = (bf16[16,8064]{1,0:T(8,128)(2,1)}, bf16[16,8064]{1,0:T(8,128)(2,1)S(1)}, u32[]{:S(2)}) copy-start(bf16[16,8064]{1,0:T(8,128)(2,1)S(1)} %collective-permute-done.refs_1_) | copy-start | bytes 774148
  17.9 27.9 %collective-permute-start.13 = (bf16[16,8064]{1,0:T(8,128)(2,1)S(1)}, bf16[16,8064]{1,0:T(8,128)(2,1)S(1)}, u32[]{:S(2)}, u32[]{:S(2)}) collective-permute-start(bf16[16,8064]{1,0:T(8,128)(2,1)S(1)} %collective-permute-done.1), channel_id=1, source_target_pairs={{0,112},{8,120},{16,64},{24,72},{32,80},{40,88},{48,96},{56,104},{... | collective-permute-start | bytes 774152 | tf_op jit(solution)/shard_map/ppermute | solution.py:302
  26.0 21.9 %collective-permute-start.12 = (bf16[16,8064]{1,0:T(8,128)(2,1)S(1)}, bf16[16,8064]{1,0:T(8,128)(2,1)S(1)}, u32[]{:S(2)}, u32[]{:S(2)}) collective-permute-start(bf16[16,8064]{1,0:T(8,128)(2,1)S(1)} %collective-permute-done.1), channel_id=1, source_target_pairs={{0,80},{8,88},{16,96},{24,104},{32,112},{40,120},{48,64},{56,72},{... | collective-permute-start | bytes 774152 | tf_op jit(solution)/shard_map/ppermute | solution.py:302
  27.0 17.7 %collective-permute-start.4 = (bf16[16,8064]{1,0:T(8,128)(2,1)S(1)}, bf16[16,8064]{1,0:T(8,128)(2,1)S(1)}, u32[]{:S(2)}, u32[]{:S(2)}) collective-permute-start(bf16[16,8064]{1,0:T(8,128)(2,1)S(1)} %collective-permute-done.1), channel_id=1, source_target_pairs={{0,64},{8,72},{16,80},{24,88},{32,96},{40,104},{48,112},{56,120},{... | collective-permute-start | bytes 774152 | tf_op jit(solution)/shard_map/ppermute | solution.py:302
  27.0 14.2 %collective-permute-start.3 = (bf16[16,8064]{1,0:T(8,128)(2,1)S(1)}, bf16[16,8064]{1,0:T(8,128)(2,1)S(1)}, u32[]{:S(2)}, u32[]{:S(2)}) collective-permute-start(bf16[16,8064]{1,0:T(8,128)(2,1)S(1)} %collective-permute-done.1), channel_id=1, source_target_pairs={{0,48},{8,56},{16,0},{24,8},{32,16},{40,24},{48,32},{56,40},{64,11... | collective-permute-start | bytes 774152 | tf_op jit(solution)/shard_map/ppermute | solution.py:302
  31.4 9.8 %collective-permute-start.2 = (bf16[16,8064]{1,0:T(8,128)(2,1)S(1)}, bf16[16,8064]{1,0:T(8,128)(2,1)S(1)}, u32[]{:S(2)}, u32[]{:S(2)}) collective-permute-start(bf16[16,8064]{1,0:T(8,128)(2,1)S(1)} %collective-permute-done.1), channel_id=1, source_target_pairs={{0,16},{8,24},{16,32},{24,40},{32,48},{40,56},{48,0},{56,8},{64,80... | collective-permute-start | bytes 774152 | tf_op jit(solution)/shard_map/ppermute | solution.py:302
  44.7 27.2 %copy-start = (bf16[64,8064]{1,0:T(8,128)(2,1)}, bf16[64,8064]{1,0:T(8,128)(2,1)S(1)}, u32[]{:S(2)}) copy-start(bf16[64,8064]{1,0:T(8,128)(2,1)S(1)} %constant_dynamic-update-slice_fusion.refs_4_) | copy-start | bytes 3096580
  44.7 21.5 %collective-permute-start.7 = (bf16[64,8064]{1,0:T(8,128)(2,1)S(1)}, bf16[64,8064]{1,0:T(8,128)(2,1)S(1)}, u32[]{:S(2)}, u32[]{:S(2)}) collective-permute-start(bf16[64,8064]{1,0:T(8,128)(2,1)S(1)} %constant_dynamic-update-slice_fusion.refs_4_), channel_id=1, source_target_pairs={{0,8},{8,0},{16,24},{24,16},{32,40},{40,32},{48,56},{56,48},{64,72... | collective-permute-start | bytes 3096584 | tf_op jit(solution)/shard_map/ppermute | solution.py:305
  45.3 9.0 %collective-permute-start.14 = (bf16[16,8064]{1,0:T(8,128)(2,1)S(1)}, bf16[16,8064]{1,0:T(8,128)(2,1)S(1)}, u32[]{:S(2)}, u32[]{:S(2)}) collective-permute-start(bf16[16,8064]{1,0:T(8,128)(2,1)S(1)} %collective-permute-done.2), channel_id=1, source_target_pairs={{0,16},{8,24},{16,32},{24,40},{32,48},{40,56},{48,0},{56,8},{64,80... | collective-permute-start | bytes 774152 | tf_op jit(solution)/shard_map/ppermute | solution.py:302
  45.7 8.6 %collective-permute-start.15 = (bf16[16,8064]{1,0:T(8,128)(2,1)S(1)}, bf16[16,8064]{1,0:T(8,128)(2,1)S(1)}, u32[]{:S(2)}, u32[]{:S(2)}) collective-permute-start(bf16[16,8064]{1,0:T(8,128)(2,1)S(1)} %collective-permute-done.13), channel_id=1, source_target_pairs={{0,48},{8,56},{16,0},{24,8},{32,16},{40,24},{48,32},{56,40},{64,11... | collective-permute-start | bytes 774152 | tf_op jit(solution)/shard_map/ppermute | solution.py:302
  54.3 17.6 %copy-start.1 = (bf16[64,8064]{1,0:T(8,128)(2,1)}, bf16[64,8064]{1,0:T(8,128)(2,1)S(1)}, u32[]{:S(2)}) copy-start(bf16[64,8064]{1,0:T(8,128)(2,1)S(1)} %constant_dynamic-update-slice_fusion.4.refs_5_) | copy-start | bytes 3096580
  54.3 17.6 %collective-permute-start.16 = (bf16[64,8064]{1,0:T(8,128)(2,1)S(1)}, bf16[64,8064]{1,0:T(8,128)(2,1)S(1)}, u32[]{:S(2)}, u32[]{:S(2)}) collective-permute-start(bf16[64,8064]{1,0:T(8,128)(2,1)S(1)} %constant_dynamic-update-slice_fusion.4.refs_5_), channel_id=1, source_target_pairs={{0,8},{8,0},{16,24},{24,16},{32,40},{40,32},{48,56},{56,48},{64,72... | collective-permute-start | bytes 3096584 | tf_op jit(solution)/shard_map/ppermute | solution.py:305
  55.3 8.0 %collective-permute-start.6 = (bf16[16,8064]{1,0:T(8,128)(2,1)}, bf16[16,8064]{1,0:T(8,128)(2,1)S(1)}, u32[]{:S(2)}, u32[]{:S(2)}) collective-permute-start(bf16[16,8064]{1,0:T(8,128)(2,1)} %shard_map.55.refs_0_), channel_id=1, source_target_pairs={{0,3},{1,0},{2,1},{3,2},{4,7},{5,4},{6,5},{7,6},{8,11},{9,8},{10,9... | collective-permute-start | bytes 774152 | tf_op jit(solution)/shard_map/ppermute | solution.py:299
  57.4 8.9 %collective-permute-start.5 = (bf16[16,8064]{1,0:T(8,128)(2,1)}, bf16[16,8064]{1,0:T(8,128)(2,1)S(1)}, u32[]{:S(2)}, u32[]{:S(2)}) collective-permute-start(bf16[16,8064]{1,0:T(8,128)(2,1)} %shard_map.55.refs_0_), channel_id=1, source_target_pairs={{0,1},{1,2},{2,3},{3,0},{4,5},{5,6},{6,7},{7,4},{8,9},{9,10},{10,1... | collective-permute-start | bytes 774152 | tf_op jit(solution)/shard_map/ppermute | solution.py:299
  63.3 8.7 %copy-start.5 = (bf16[16,8064]{1,0:T(8,128)(2,1)}, bf16[16,8064]{1,0:T(8,128)(2,1)S(1)}, u32[]{:S(2)}) copy-start(bf16[16,8064]{1,0:T(8,128)(2,1)S(1)} %collective-permute-done.6.refs_3_) | copy-start | bytes 774148
  66.2 5.7 %copy-start.9 = (bf16[16,8064]{1,0:T(8,128)(2,1)}, bf16[16,8064]{1,0:T(8,128)(2,1)S(1)}, u32[]{:S(2)}) copy-start(bf16[16,8064]{1,0:T(8,128)(2,1)S(1)} %collective-permute-done.5.refs_2_) | copy-start | bytes 774148
  66.2 5.7 %copy-start.2 = (bf16[64,8064]{1,0:T(8,128)(2,1)}, bf16[64,8064]{1,0:T(8,128)(2,1)S(1)}, u32[]{:S(2)}) copy-start(bf16[64,8064]{1,0:T(8,128)(2,1)S(1)} %collective-permute-done.7.refs_6_) | copy-start | bytes 3096580
  66.2 26.6 %collective-permute-start.9 = (bf16[16,8064]{1,0:T(8,128)(2,1)S(1)}, bf16[16,8064]{1,0:T(8,128)(2,1)S(1)}, u32[]{:S(2)}, u32[]{:S(2)}) collective-permute-start(bf16[16,8064]{1,0:T(8,128)(2,1)S(1)} %collective-permute-done.refs_1_), channel_id=1, source_target_pairs={{0,3},{1,0},{2,1},{3,2},{4,7},{5,4},{6,5},{7,6},{8,11},{9,8},{10,9... | collective-permute-start | bytes 774152 | tf_op jit(solution)/shard_map/ppermute | solution.py:299
  66.6 26.2 %collective-permute-start.8 = (bf16[16,8064]{1,0:T(8,128)(2,1)S(1)}, bf16[16,8064]{1,0:T(8,128)(2,1)S(1)}, u32[]{:S(2)}, u32[]{:S(2)}) collective-permute-start(bf16[16,8064]{1,0:T(8,128)(2,1)S(1)} %collective-permute-done.refs_1_), channel_id=1, source_target_pairs={{0,1},{1,2},{2,3},{3,0},{4,5},{5,6},{6,7},{7,4},{8,9},{9,10},{10,1... | collective-permute-start | bytes 774152 | tf_op jit(solution)/shard_map/ppermute | solution.py:299
  67.8 25.1 %collective-permute-start.10 = (bf16[16,8064]{1,0:T(8,128)(2,1)S(1)}, bf16[16,8064]{1,0:T(8,128)(2,1)S(1)}, u32[]{:S(2)}, u32[]{:S(2)}) collective-permute-start(bf16[16,8064]{1,0:T(8,128)(2,1)S(1)} %collective-permute-done.5.refs_2_), channel_id=1, source_target_pairs={{0,1},{1,2},{2,3},{3,0},{4,5},{5,6},{6,7},{7,4},{8,9},{9,10},{10,1... | collective-permute-start | bytes 774152 | tf_op jit(solution)/shard_map/ppermute | solution.py:299
  67.8 25.0 %collective-permute-start.11 = (bf16[16,8064]{1,0:T(8,128)(2,1)S(1)}, bf16[16,8064]{1,0:T(8,128)(2,1)S(1)}, u32[]{:S(2)}, u32[]{:S(2)}) collective-permute-start(bf16[16,8064]{1,0:T(8,128)(2,1)S(1)} %collective-permute-done.6.refs_3_), channel_id=1, source_target_pairs={{0,7},{1,4},{2,5},{3,6},{4,3},{5,0},{6,1},{7,2},{8,15},{9,12},{10,... | collective-permute-start | bytes 774152 | tf_op jit(solution)/shard_map/ppermute | solution.py:299
  72.0 1.0 copy-start.3
  92.8 0.7 copy-start.8
  92.9 0.8 copy-start.10
  92.9 0.9 copy-start.6
  93.8 0.7 copy-start.7

commit v6 on v4

--- a/solution.py
+++ b/solution.py
@@ -18,14 +18,15 @@
 LAG_ROWS = 56
 LAG_TILE = 64
 UNROLL = 10
+TOGETHER = 2
 FB = 8
 NB = F // FB
 OWN = 16
 MAIN = 16
 TILES = NB + -(-NB // 4)
 LANES = TILES * 128
-DEPTH = 4
-LAG = 3
+DEPTH = 8
+LAG = 4
 
 
 def unit_circle(turns):
@@ -119,14 +120,21 @@
     col_places = [c * 8 + step(step(q, *key), 2, 0) for c in (core, 1 - core) for key in col_keys]
     row_refs, refs = refs[:n_rows], refs[n_rows:]
     col_refs, refs = refs[:n_cols], refs[n_cols:]
-    table_ref, out_ref, cols, rows, turned, cross, *lagged, staged, sems = refs[:1] + refs[1 + n_kept :]
+    table_from, out_ref, cols, table_ref, rows, turned, cross, *lagged, staged, sems, in_sems = (
+        refs[:1] + refs[1 + n_kept :]
+    )
     lane = lax.broadcasted_iota(jnp.int32, (16, 128), 1)
     same_bin = (lane % 8) == lax.broadcasted_iota(jnp.int32, (16, 128), 0) % 8
     zero = jnp.zeros((), jnp.bfloat16)
     groups = n_rows * OWN // 8
 
+    loads = []
     for k, ref in enumerate(col_refs):
-        cols[pl.ds(pl.multiple_of(col_places[k] * OWN, OWN), OWN), :] = ref[...]
+        at = pl.ds(pl.multiple_of(col_places[k] * OWN, OWN), OWN)
+        loads.append(pltpu.make_async_copy(ref, cols.at[at, :], in_sems.at[k]))
+    loads.append(pltpu.make_async_copy(table_from, table_ref, in_sems.at[n_cols]))
+    for load in loads:
+        load.start()
 
     def spread(first, last, shift):
         minus = (lax.broadcasted_iota(jnp.int32, (OWN, 128), 1) // shift) % 2 == 1
@@ -142,6 +150,8 @@
 
     spread(0, NB, 8)
     spread(NB, TILES, 32)
+    for load in loads[:-1]:
+        load.wait()
 
     def cross_of(*accs):
         accs = accs[:DEPTH], accs[DEPTH:]
@@ -209,7 +219,7 @@
             out_copy(g - 2).wait()
         for lag in range(HALF + 1):
             for h in range(2):
-                e, o = (lagged[2 * (g % 2) + part][h, pl.ds(lag, OWN, stride=LAG_ROWS), :] for part in range(2))
+                e, o = (lagged[2 * (g % TOGETHER) + part][h, pl.ds(lag, OWN, stride=LAG_ROWS), :] for part in range(2))
                 lanes = slice(h * 128, (h + 1) * 128)
                 staged[g % 2, HALF + lag, :, lanes] = ((e + o) * (1.0 / math.sqrt(W * F))).astype(jnp.bfloat16)
                 if lag:
@@ -217,39 +227,42 @@
         out_copy(g).start()
 
     def lags_of(*accs):
-        accs = accs[:4], accs[4:]
-
-        def push(g, t):
-            at = g * OWN * F + t * 256
-            for part in range(2):
-                pltpu.matmul_push_rhs(cross[part, at : at + 256, :], t % 2, part)
+        def acc_of(part, g, u):
+            return accs[(part * TOGETHER + g % TOGETHER) * 4 + u % 4]
 
         def finish(g, u):
             for part in range(2):
-                z = pltpu.matmul_pop(accs[part][u % 4])
+                z = pltpu.matmul_pop(acc_of(part, g, u))
                 for h in range(2):
                     rows_of = slice(u * LAG_ROWS, (u + 1) * LAG_ROWS)
-                    lagged[2 * (g % 2) + part][h, rows_of, :] = z[:LAG_ROWS, h * 128 : (h + 1) * 128]
-
-        for g in range(n_rows):
-            pushed = done = -1
-            for k, (t, u) in enumerate(segments()):
-                if t != pushed:
-                    push(g, t)
-                for part in range(2):
-                    pltpu.matmul_acc_lhs(accs[part][u % 4], table_ref[part, k], t % 2 if t != pushed else None)
-                pushed = t
-                if u - 2 > done:
-                    done = u - 2
-                    finish(g, done)
+                    lagged[2 * (g % TOGETHER) + part][h, rows_of, :] = z[:LAG_ROWS, h * 128 : (h + 1) * 128]
+
+        for first in range(0, n_rows, TOGETHER):
+            done = -1
+            for t in range(OWN * F // 256):
+                channels = [(k, u) for k, (tile, u) in enumerate(segments()) if tile == t]
+                tables = [[table_ref[part, k] for part in range(2)] for k, _ in channels]
+                for g in range(first, first + TOGETHER):
+                    at = g * OWN * F + t * 256
+                    staged_in = (t * TOGETHER + g) % 2
+                    for part in range(2):
+                        pltpu.matmul_push_rhs(cross[part, at : at + 256, :], staged_in, part)
+                    for n, (k, u) in enumerate(channels):
+                        for part in range(2):
+                            pltpu.matmul_acc_lhs(acc_of(part, g, u), tables[n][part], None if n else staged_in)
+                while done < channels[-1][1] - 2:
+                    done += 1
+                    for g in range(first, first + TOGETHER):
+                        finish(g, done)
             for u in range(done + 1, OWN):
-                finish(g, u)
-            if g:
-                emit(g - 1)
-        emit(n_rows - 1)
+                for g in range(first, first + TOGETHER):
+                    finish(g, u)
+            for g in range(first, first + TOGETHER):
+                emit(g)
 
     pl.run_scoped(cross_of, *[pltpu.ACC(mxu)((128, 256), jnp.float32) for mxu in [0] * DEPTH + [1] * DEPTH])
-    pl.run_scoped(lags_of, *[pltpu.ACC(mxu)((LAG_TILE, 256), jnp.float32) for mxu in [0] * 4 + [1] * 4])
+    loads[-1].wait()
+    pl.run_scoped(lags_of, *[pltpu.ACC(mxu)((LAG_TILE, 256), jnp.float32) for mxu in [0] * (4 * TOGETHER) + [1] * (4 * TOGETHER)])
     for k in range(n_rows - 2, n_rows):
         out_copy(k).wait()
 
@@ -261,26 +274,28 @@
     inputs = (*row_blocks, *col_blocks, jnp.asarray(lag_tables(), jnp.bfloat16), *kept)
     return pl.pallas_call(
         functools.partial(correlate_kernel, tuple(rows), tuple(cols), len(kept)),
-        in_specs=[vmem] * (len(row_blocks) + len(col_blocks) + 1) + [anywhere] * len(kept),
+        in_specs=[vmem] * len(row_blocks) + [anywhere] * (len(col_blocks) + 1 + len(kept)),
         out_specs=anywhere,
         out_shape=jax.ShapeDtypeStruct(shape, jnp.bfloat16),
         input_output_aliases={len(inputs) - 1: 0} if kept else {},
         scratch_shapes=[
             pltpu.VMEM((m, LANES), jnp.bfloat16),
+            pltpu.VMEM((2, len(segments()), LAG_TILE, 256), jnp.bfloat16),
             pltpu.VMEM((n, LANES), jnp.float32),
             pltpu.VMEM((n, LANES), jnp.float32),
             pltpu.VMEM((2, n * F, m), jnp.bfloat16),
-            *[pltpu.VMEM((2, OWN * LAG_ROWS, 128), jnp.float32)] * 4,
+            *[pltpu.VMEM((2, OWN * LAG_ROWS, 128), jnp.float32)] * (2 * TOGETHER),
             pltpu.VMEM((2, LAGS, OWN, m), jnp.bfloat16),
             pltpu.SemaphoreType.DMA((2,)),
+            pltpu.SemaphoreType.DMA((len(col_blocks) + 1,)),
         ],
         compiler_params=pltpu.CompilerParams(vmem_limit_bytes=52 * 1024 * 1024),
         cost_estimate=pl.CostEstimate(flops=n * 2 * 10**8, bytes_accessed=10**7, transcendentals=0),
     )(*inputs)
 
 
-def near(block, move):
-    return {(0, 0): block, (0, 1): move(block, 0, 1), (-1, 0): move(block, 1, 0), (1, 0): move(block, -1, 0)}
+def near(block, side, move):
+    return {(0, 0): block, (0, 1): side, (-1, 0): move(block, 1, 0), (1, 0): move(block, -1, 0)}
 
 
 def far(found, move):
@@ -308,14 +323,11 @@
         ((i * 2 + k) * 8 + step(j, 2, 0), (j * 2 + k) * 8 + i) for i in range(8) for k in range(2) for j in range(8)
     ]
     turned = lax.ppermute(white, ("src", "rcv"), flip)
-    cols = near(turned, over_src)
-    swapped = {(0, 0): other_core(turned)}
-    white, swapped[0, 0] = lax.optimization_barrier((white, swapped[0, 0]))
-    rows = near(white, over_rcv)
-    more = far(cols, over_src)
-    swapped |= {key: other_core(value) for key, value in (cols | more).items() if key != (0, 0)}
-    cols |= more
-    rows, swapped = lax.optimization_barrier((rows, swapped))
+    white, side, turned = lax.optimization_barrier((white, over_rcv(white, 0, 1), turned))
+    cols = near(turned, over_src(turned, 0, 1), over_src)
+    rows, cols = lax.optimization_barrier((near(white, side, over_rcv), cols))
+    cols |= far(cols, over_src)
+    swapped = {key: other_core(value) for key, value in cols.items()}
     shape = (LAGS, 8 * OWN, 16 * OWN)
     first = correlate(rows, cols, swapped, shape)
     return correlate(far(rows, over_rcv), cols, swapped, shape, (first,))

time: 106 us -> 102 us (0.962)
  starting transfers between devices: 44.8 us -> 34.9 us
  waiting for transfers between devices: 12.5 us -> 20.7 us
  Pallas kernels: 44.4 us -> 42.2 us
    ppermute x7, waiting for transfers between devices: 5.58 us -> 14.4 us  [over_src(): lax.ppermute(value, 'src', [(i, 2 * step(i // 2, ring, side) + i % 2) for...]
    ppermute x7, starting transfers between devices: 19.4 us -> 12.1 us  [over_src(): lax.ppermute(value, 'src', [(i, 2 * step(i // 2, ring, side) + i % 2) for...]
    ppermute x8, starting transfers between devices: 13.3 us -> 6.72 us  [other_core(): return lax.ppermute(value, 'src', [(i, i ^ 1) for i in range(16)])]
    ppermute x7, starting transfers between devices: 8.39 us -> 12.3 us  [over_rcv(): lax.ppermute(value, 'rcv', [(i, step(i, ring, side)) for i in range(8)])]
    ppermute x1, waiting for transfers between devices: 5.54 us -> 2.55 us  [body(): turned = lax.ppermute(white, ('src', 'rcv'), flip)]
    ppermute x7, waiting for transfers between devices: 0.89 us -> 3.72 us  [over_rcv(): lax.ppermute(value, 'rcv', [(i, step(i, ring, side)) for i in range(8)])]
    pallas_call x2, Pallas kernels: 41 us -> 38.8 us  [correlate(): pl.pallas_call(functools.partial(correlate_kernel, tuple(rows), tuple(col...]
where the time goes in v6:
time: 102 us
  Pallas kernels  42.2 us (41%)
  starting transfers between devices  34.9 us (34%)
  waiting for transfers between devices  20.7 us (20%)
  local copies, waits for them, and re-layouts  3.53 us (3%)
    pallas_call x2, Pallas kernels, correlate(): pl.pallas_call(functools.partial(correlate_kernel, tuple(rows), tuple(col...  38.8 us
    ppermute x7, waiting for transfers between devices, over_src(): lax.ppermute(value, 'src', [(i, 2 * step(i // 2, ring, side) + i % 2) for...  14.4 us
    ppermute x7, starting transfers between devices, over_rcv(): lax.ppermute(value, 'rcv', [(i, step(i, ring, side)) for i in range(8)])  12.3 us
    ppermute x7, starting transfers between devices, over_src(): lax.ppermute(value, 'src', [(i, 2 * step(i // 2, ring, side) + i % 2) for...  12.1 us
    ppermute x8, starting transfers between devices, other_core(): return lax.ppermute(value, 'src', [(i, i ^ 1) for i in range(16)])  6.72 us
    ppermute x1, starting transfers between devices, body(): turned = lax.ppermute(white, ('src', 'rcv'), flip)  3.74 us
    ppermute x7, waiting for transfers between devices, over_rcv(): lax.ppermute(value, 'rcv', [(i, step(i, ring, side)) for i in range(8)])  3.72 us
    unnamed x29, local copies, waits for them, and re-layouts  3.53 us
  transfers between devices with their start and end apart: 23, of which 9 were waited for; matrix products, arithmetic and copies ran while one was open for 0% of the time, Pallas kernels for 19%

profile of v6, /device:TPU:1, one launch (start us, length us, event | category | flops | bytes accessed | tf_op | source)
XLA Modules:
  0.0 101.7 jit_solution(12034204195953476485)
XLA Ops:
  0.0 1.8 %copy.7.spectra_ref = bf16[16,2,10,400]{3,2,1,0:T(8,128)(2,1)} copy(bf16[16,2,10,400]{3,1,2,0:T(2,128)(2,1)} %param.5) | data formatting | bytes 512000 | tf_op args[0]
  1.8 3.4 %shard_map.55.refs_1_ = bf16[16,8064]{1,0:T(8,128)(2,1)} custom-call(s32[16]{0:T(128)} %mask_ref.1, bf16[16,2,10,400]{3,2,1,0:T(8,128)(2,1)} %copy.7.spectra_ref, s32[16,10]{1,0:T(8,128)} %offsets_ref.1), custom_call_target="tpu_custom_call" | custom-call | tf_op jit(solution)/shard_map/pallas_call | solution.py:88
  5.2 3.7 %collective-permute-start.1 = (bf16[16,8064]{1,0:T(8,128)(2,1)}, bf16[16,8064]{1,0:T(8,128)(2,1)S(1)}, u32[]{:S(2)}, u32[]{:S(2)}) collective-permute-start(bf16[16,8064]{1,0:T(8,128)(2,1)} %shard_map.55.refs_1_), channel_id=1, source_target_pairs={{2,0},{3,16},{0,32},{1,48},{6,64},{7,80},{4,96},{5,112},{10,8},{11... | collective-permute-start | bytes 774152 | tf_op jit(solution)/shard_map/ppermute | solution.py:325
  9.0 3.0 %collective-permute-start = (bf16[16,8064]{1,0:T(8,128)(2,1)}, bf16[16,8064]{1,0:T(8,128)(2,1)S(1)}, u32[]{:S(2)}, u32[]{:S(2)}) collective-permute-start(bf16[16,8064]{1,0:T(8,128)(2,1)} %shard_map.55.refs_1_), channel_id=1, source_target_pairs={{0,4},{1,5},{2,6},{3,7},{4,0},{5,1},{6,2},{7,3},{8,12},{9,13},{10,... | collective-permute-start | bytes 774152 | tf_op jit(solution)/shard_map/ppermute | solution.py:314
  12.0 2.5 %collective-permute-done.1.refs_5_ = bf16[16,8064]{1,0:T(8,128)(2,1)S(1)} collective-permute-done((bf16[16,8064]{1,0:T(8,128)(2,1)}, bf16[16,8064]{1,0:T(8,128)(2,1)S(1)}, u32[]{:S(2)}, u32[]{:S(2)}) %collective-permute-start.1) | collective-permute-done | bytes 258080 | tf_op jit(solution)/shard_map/ppermute | solution.py:325
  14.5 3.3 %collective-permute-done.refs_2_ = bf16[16,8064]{1,0:T(8,128)(2,1)S(1)} collective-permute-done((bf16[16,8064]{1,0:T(8,128)(2,1)}, bf16[16,8064]{1,0:T(8,128)(2,1)S(1)}, u32[]{:S(2)}, u32[]{:S(2)}) %collective-permute-start) | collective-permute-done | bytes 258080 | tf_op jit(solution)/shard_map/ppermute | solution.py:314
  17.8 2.8 %collective-permute-start.3 = (bf16[16,8064]{1,0:T(8,128)(2,1)}, bf16[16,8064]{1,0:T(8,128)(2,1)S(1)}, u32[]{:S(2)}, u32[]{:S(2)}) collective-permute-start(bf16[16,8064]{1,0:T(8,128)(2,1)} %shard_map.55.refs_1_), channel_id=1, source_target_pairs={{0,3},{1,0},{2,1},{3,2},{4,7},{5,4},{6,5},{7,6},{8,11},{9,8},{10,9... | collective-permute-start | bytes 774152 | tf_op jit(solution)/shard_map/ppermute | solution.py:314
  20.6 0.4 collective-permute-start.2
  21.0 3.6 %collective-permute-start.6 = (bf16[16,8064]{1,0:T(8,128)(2,1)S(1)}, bf16[16,8064]{1,0:T(8,128)(2,1)S(1)}, u32[]{:S(2)}, u32[]{:S(2)}) collective-permute-start(bf16[16,8064]{1,0:T(8,128)(2,1)S(1)} %collective-permute-done.1.refs_5_), channel_id=1, source_target_pairs={{0,48},{8,56},{16,0},{24,8},{32,16},{40,24},{48,32},{56,40},{64,11... | collective-permute-start | bytes 774152 | tf_op jit(solution)/shard_map/ppermute | solution.py:317
  24.6 3.1 %collective-permute-start.5 = (bf16[16,8064]{1,0:T(8,128)(2,1)S(1)}, bf16[16,8064]{1,0:T(8,128)(2,1)S(1)}, u32[]{:S(2)}, u32[]{:S(2)}) collective-permute-start(bf16[16,8064]{1,0:T(8,128)(2,1)S(1)} %collective-permute-done.1.refs_5_), channel_id=1, source_target_pairs={{0,64},{8,72},{16,80},{24,88},{32,96},{40,104},{48,112},{56,120},{... | collective-permute-start | bytes 774152 | tf_op jit(solution)/shard_map/ppermute | solution.py:317
  27.7 0.9 collective-permute-start.4
  28.6 0.0 collective-permute-done.3.refs_3_
  28.7 0.4 collective-permute-done.2.refs_0_
  29.0 0.3 collective-permute-done.6.refs_7_
  29.3 3.4 %collective-permute-done.5.refs_6_ = bf16[16,8064]{1,0:T(8,128)(2,1)S(1)} collective-permute-done((bf16[16,8064]{1,0:T(8,128)(2,1)S(1)}, bf16[16,8064]{1,0:T(8,128)(2,1)S(1)}, u32[]{:S(2)}, u32[]{:S(2)}) %collective-permute-start.5) | collective-permute-done | bytes 258080 | tf_op jit(solution)/shard_map/ppermute | solution.py:317
  32.7 4.5 %collective-permute-done.4.refs_4_ = bf16[16,8064]{1,0:T(8,128)(2,1)S(1)} collective-permute-done((bf16[16,8064]{1,0:T(8,128)(2,1)S(1)}, bf16[16,8064]{1,0:T(8,128)(2,1)S(1)}, u32[]{:S(2)}, u32[]{:S(2)}) %collective-permute-start.4) | collective-permute-done | bytes 258080 | tf_op jit(solution)/shard_map/ppermute | solution.py:317
  37.2 2.1 %collective-permute-start.16 = (bf16[16,8064]{1,0:T(8,128)(2,1)S(1)}, bf16[16,8064]{1,0:T(8,128)(2,1)S(1)}, u32[]{:S(2)}, u32[]{:S(2)}) collective-permute-start(bf16[16,8064]{1,0:T(8,128)(2,1)S(1)} %collective-permute-done.1.refs_5_), channel_id=1, source_target_pairs={{0,8},{8,0},{16,24},{24,16},{32,40},{40,32},{48,56},{56,48},{64,72... | collective-permute-start | bytes 774152 | tf_op jit(solution)/shard_map/ppermute | solution.py:320
  39.3 0.0 collective-permute-start.15
  39.3 0.0 collective-permute-start.13
  39.3 0.5 collective-permute-start.18
  39.8 2.7 %collective-permute-start.14 = (bf16[16,8064]{1,0:T(8,128)(2,1)S(1)}, bf16[16,8064]{1,0:T(8,128)(2,1)S(1)}, u32[]{:S(2)}, u32[]{:S(2)}) collective-permute-start(bf16[16,8064]{1,0:T(8,128)(2,1)S(1)} %collective-permute-done.6.refs_7_), channel_id=1, source_target_pairs={{0,112},{8,120},{16,64},{24,72},{32,80},{40,88},{48,96},{56,104},{... | collective-permute-start | bytes 774152 | tf_op jit(solution)/shard_map/ppermute | solution.py:317
  42.5 0.0 collective-permute-done.16.refs_13_
  42.5 1.7 %collective-permute-start.12 = (bf16[16,8064]{1,0:T(8,128)(2,1)S(1)}, bf16[16,8064]{1,0:T(8,128)(2,1)S(1)}, u32[]{:S(2)}, u32[]{:S(2)}) collective-permute-start(bf16[16,8064]{1,0:T(8,128)(2,1)S(1)} %collective-permute-done.5.refs_6_), channel_id=1, source_target_pairs={{0,48},{8,56},{16,0},{24,8},{32,16},{40,24},{48,32},{56,40},{64,11... | collective-permute-start | bytes 774152 | tf_op jit(solution)/shard_map/ppermute | solution.py:317
  44.2 0.0 collective-permute-done.15.refs_12_
  44.2 0.0 collective-permute-start.11
  44.3 3.5 %collective-permute-done.13.refs_10_ = bf16[16,8064]{1,0:T(8,128)(2,1)S(1)} collective-permute-done((bf16[16,8064]{1,0:T(8,128)(2,1)S(1)}, bf16[16,8064]{1,0:T(8,128)(2,1)S(1)}, u32[]{:S(2)}, u32[]{:S(2)}) %collective-permute-start.13) | collective-permute-done | bytes 258080 | tf_op jit(solution)/shard_map/ppermute | solution.py:317
  47.8 1.9 %collective-permute-start.17 = (bf16[16,8064]{1,0:T(8,128)(2,1)S(1)}, bf16[16,8064]{1,0:T(8,128)(2,1)S(1)}, u32[]{:S(2)}, u32[]{:S(2)}) collective-permute-start(bf16[16,8064]{1,0:T(8,128)(2,1)S(1)} %collective-permute-done.5.refs_6_), channel_id=1, source_target_pairs={{0,8},{8,0},{16,24},{24,16},{32,40},{40,32},{48,56},{56,48},{64,72... | collective-permute-start | bytes 774152 | tf_op jit(solution)/shard_map/ppermute | solution.py:320
  49.6 0.0 collective-permute-done.18.refs_15_
  49.7 0.1 collective-permute-start.21
  49.7 0.3 collective-permute-done.14.refs_11_
  50.1 1.2 %collective-permute-start.22 = (bf16[16,8064]{1,0:T(8,128)(2,1)S(1)}, bf16[16,8064]{1,0:T(8,128)(2,1)S(1)}, u32[]{:S(2)}, u32[]{:S(2)}) collective-permute-start(bf16[16,8064]{1,0:T(8,128)(2,1)S(1)} %collective-permute-done.14.refs_11_), channel_id=1, source_target_pairs={{0,8},{8,0},{16,24},{24,16},{32,40},{40,32},{48,56},{56,48},{64,72... | collective-permute-start | bytes 774152 | tf_op jit(solution)/shard_map/ppermute | solution.py:320
  51.2 2.4 %collective-permute-done.12.refs_9_ = bf16[16,8064]{1,0:T(8,128)(2,1)S(1)} collective-permute-done((bf16[16,8064]{1,0:T(8,128)(2,1)S(1)}, bf16[16,8064]{1,0:T(8,128)(2,1)S(1)}, u32[]{:S(2)}, u32[]{:S(2)}) %collective-permute-start.12) | collective-permute-done | bytes 258080 | tf_op jit(solution)/shard_map/ppermute | solution.py:317
  53.7 0.8 collective-permute-start.20
  54.5 0.0 collective-permute-done.11.refs_8_
  54.5 0.2 collective-permute-start.19
  54.7 0.0 collective-permute-done.17.refs_14_
  54.7 2.7 %collective-permute-start.8 = (bf16[16,8064]{1,0:T(8,128)(2,1)S(1)}, bf16[16,8064]{1,0:T(8,128)(2,1)S(1)}, u32[]{:S(2)}, u32[]{:S(2)}) collective-permute-start(bf16[16,8064]{1,0:T(8,128)(2,1)S(1)} %collective-permute-done.refs_2_), channel_id=1, source_target_pairs={{0,3},{1,0},{2,1},{3,2},{4,7},{5,4},{6,5},{7,6},{8,11},{9,8},{10,9... | collective-permute-start | bytes 774152 | tf_op jit(solution)/shard_map/ppermute | solution.py:314
  57.4 0.0 collective-permute-done.21.refs_18_
  57.4 0.0 collective-permute-start.7
  57.4 0.1 collective-permute-start.9
  57.5 0.0 collective-permute-done.20.refs_17_
  57.5 3.4 %collective-permute-start.10 = (bf16[16,8064]{1,0:T(8,128)(2,1)S(1)}, bf16[16,8064]{1,0:T(8,128)(2,1)S(1)}, u32[]{:S(2)}, u32[]{:S(2)}) collective-permute-start(bf16[16,8064]{1,0:T(8,128)(2,1)S(1)} %collective-permute-done.3.refs_3_), channel_id=1, source_target_pairs={{0,7},{1,4},{2,5},{3,6},{4,3},{5,0},{6,1},{7,2},{8,15},{9,12},{10,... | collective-permute-start | bytes 774152 | tf_op jit(solution)/shard_map/ppermute | solution.py:314
  61.0 0.7 copy-done.13
  61.7 0.9 copy-done
  62.7 19.2 %shard_map.56.refs_21_ = bf16[101,128,256]{2,1,0:T(8,128)(2,1)} custom-call(bf16[16,8064]{1,0:T(8,128)(2,1)S(1)} %collective-permute-done.2.refs_0_, bf16[16,8064]{1,0:T(8,128)(2,1)S(1)} %copy-done, bf16[16,8064]{1,0:T(8,128)(2,1)S(1)} %collective-permute-done.refs_2_, bf16[16,8064]{1,0:T(8,128)(2,1)S(1)} %collective-permute-done.3.refs_3_, ...), custom_call_target="tpu_custom_call" | custom-call | flops 12800000000 | bytes 10000000 | tf_op jit(solution)/shard_map/pallas_call | solution.py:275
  81.9 0.0 collective-permute-done.8.refs_1_
  82.0 0.0 collective-permute-done.7.refs_0_
  82.0 19.6 %shard_map.57 = bf16[101,128,256]{2,1,0:T(8,128)(2,1)} custom-call(bf16[16,8064]{1,0:T(8,128)(2,1)S(1)} %collective-permute-done.7.refs_0_, bf16[16,8064]{1,0:T(8,128)(2,1)S(1)} %collective-permute-done.8.refs_1_, bf16[16,8064]{1,0:T(8,128)(2,1)S(1)} %collective-permute-done.9.refs_2_, ...), custom_call_target="tpu_custom_call", output_to_operand_aliasing={{}: (21, {})} | custom-call | flops 12800000000 | bytes 10000000 | tf_op jit(solution)/shard_map/pallas_call | solution.py:275
  (30 shorter events, 0.1 us)
Async XLA Ops:
  5.2 9.3 %collective-permute-start.1 = (bf16[16,8064]{1,0:T(8,128)(2,1)}, bf16[16,8064]{1,0:T(8,128)(2,1)S(1)}, u32[]{:S(2)}, u32[]{:S(2)}) collective-permute-start(bf16[16,8064]{1,0:T(8,128)(2,1)} %shard_map.55.refs_1_), channel_id=1, source_target_pairs={{2,0},{3,16},{0,32},{1,48},{6,64},{7,80},{4,96},{5,112},{10,8},{11... | collective-permute-start | bytes 774152 | tf_op jit(solution)/shard_map/ppermute | solution.py:325
  9.0 8.9 %collective-permute-start = (bf16[16,8064]{1,0:T(8,128)(2,1)}, bf16[16,8064]{1,0:T(8,128)(2,1)S(1)}, u32[]{:S(2)}, u32[]{:S(2)}) collective-permute-start(bf16[16,8064]{1,0:T(8,128)(2,1)} %shard_map.55.refs_1_), channel_id=1, source_target_pairs={{0,4},{1,5},{2,6},{3,7},{4,0},{5,1},{6,2},{7,3},{8,12},{9,13},{10,... | collective-permute-start | bytes 774152 | tf_op jit(solution)/shard_map/ppermute | solution.py:314
  17.8 10.8 %collective-permute-start.3 = (bf16[16,8064]{1,0:T(8,128)(2,1)}, bf16[16,8064]{1,0:T(8,128)(2,1)S(1)}, u32[]{:S(2)}, u32[]{:S(2)}) collective-permute-start(bf16[16,8064]{1,0:T(8,128)(2,1)} %shard_map.55.refs_1_), channel_id=1, source_target_pairs={{0,3},{1,0},{2,1},{3,2},{4,7},{5,4},{6,5},{7,6},{8,11},{9,8},{10,9... | collective-permute-start | bytes 774152 | tf_op jit(solution)/shard_map/ppermute | solution.py:314
  20.6 8.4 %collective-permute-start.2 = (bf16[16,8064]{1,0:T(8,128)(2,1)}, bf16[16,8064]{1,0:T(8,128)(2,1)S(1)}, u32[]{:S(2)}, u32[]{:S(2)}) collective-permute-start(bf16[16,8064]{1,0:T(8,128)(2,1)} %shard_map.55.refs_1_), channel_id=1, source_target_pairs={{0,1},{1,2},{2,3},{3,0},{4,5},{5,6},{6,7},{7,4},{8,9},{9,10},{10,1... | collective-permute-start | bytes 774152 | tf_op jit(solution)/shard_map/ppermute | solution.py:314
  21.0 8.3 %collective-permute-start.6 = (bf16[16,8064]{1,0:T(8,128)(2,1)S(1)}, bf16[16,8064]{1,0:T(8,128)(2,1)S(1)}, u32[]{:S(2)}, u32[]{:S(2)}) collective-permute-start(bf16[16,8064]{1,0:T(8,128)(2,1)S(1)} %collective-permute-done.1.refs_5_), channel_id=1, source_target_pairs={{0,48},{8,56},{16,0},{24,8},{32,16},{40,24},{48,32},{56,40},{64,11... | collective-permute-start | bytes 774152 | tf_op jit(solution)/shard_map/ppermute | solution.py:317
  24.6 8.1 %collective-permute-start.5 = (bf16[16,8064]{1,0:T(8,128)(2,1)S(1)}, bf16[16,8064]{1,0:T(8,128)(2,1)S(1)}, u32[]{:S(2)}, u32[]{:S(2)}) collective-permute-start(bf16[16,8064]{1,0:T(8,128)(2,1)S(1)} %collective-permute-done.1.refs_5_), channel_id=1, source_target_pairs={{0,64},{8,72},{16,80},{24,88},{32,96},{40,104},{48,112},{56,120},{... | collective-permute-start | bytes 774152 | tf_op jit(solution)/shard_map/ppermute | solution.py:317
  27.7 9.5 %collective-permute-start.4 = (bf16[16,8064]{1,0:T(8,128)(2,1)S(1)}, bf16[16,8064]{1,0:T(8,128)(2,1)S(1)}, u32[]{:S(2)}, u32[]{:S(2)}) collective-permute-start(bf16[16,8064]{1,0:T(8,128)(2,1)S(1)} %collective-permute-done.1.refs_5_), channel_id=1, source_target_pairs={{0,16},{8,24},{16,32},{24,40},{32,48},{40,56},{48,0},{56,8},{64,80... | collective-permute-start | bytes 774152 | tf_op jit(solution)/shard_map/ppermute | solution.py:317
  29.3 31.6 %copy-start.1 = (bf16[16,8064]{1,0:T(8,128)(2,1)}, bf16[16,8064]{1,0:T(8,128)(2,1)S(1)}, u32[]{:S(2)}) copy-start(bf16[16,8064]{1,0:T(8,128)(2,1)S(1)} %collective-permute-done.6.refs_7_) | copy-start | bytes 774148
  37.2 5.3 %collective-permute-start.16 = (bf16[16,8064]{1,0:T(8,128)(2,1)S(1)}, bf16[16,8064]{1,0:T(8,128)(2,1)S(1)}, u32[]{:S(2)}, u32[]{:S(2)}) collective-permute-start(bf16[16,8064]{1,0:T(8,128)(2,1)S(1)} %collective-permute-done.1.refs_5_), channel_id=1, source_target_pairs={{0,8},{8,0},{16,24},{24,16},{32,40},{40,32},{48,56},{56,48},{64,72... | collective-permute-start | bytes 774152 | tf_op jit(solution)/shard_map/ppermute | solution.py:320
  39.3 5.0 %collective-permute-start.15 = (bf16[16,8064]{1,0:T(8,128)(2,1)S(1)}, bf16[16,8064]{1,0:T(8,128)(2,1)S(1)}, u32[]{:S(2)}, u32[]{:S(2)}) collective-permute-start(bf16[16,8064]{1,0:T(8,128)(2,1)S(1)} %collective-permute-done.4.refs_4_), channel_id=1, source_target_pairs={{0,8},{8,0},{16,24},{24,16},{32,40},{40,32},{48,56},{56,48},{64,72... | collective-permute-start | bytes 774152 | tf_op jit(solution)/shard_map/ppermute | solution.py:320
  39.3 8.5 %collective-permute-start.13 = (bf16[16,8064]{1,0:T(8,128)(2,1)S(1)}, bf16[16,8064]{1,0:T(8,128)(2,1)S(1)}, u32[]{:S(2)}, u32[]{:S(2)}) collective-permute-start(bf16[16,8064]{1,0:T(8,128)(2,1)S(1)} %collective-permute-done.4.refs_4_), channel_id=1, source_target_pairs={{0,16},{8,24},{16,32},{24,40},{32,48},{40,56},{48,0},{56,8},{64,80... | collective-permute-start | bytes 774152 | tf_op jit(solution)/shard_map/ppermute | solution.py:317
  39.3 10.4 %collective-permute-start.18 = (bf16[16,8064]{1,0:T(8,128)(2,1)S(1)}, bf16[16,8064]{1,0:T(8,128)(2,1)S(1)}, u32[]{:S(2)}, u32[]{:S(2)}) collective-permute-start(bf16[16,8064]{1,0:T(8,128)(2,1)S(1)} %collective-permute-done.6.refs_7_), channel_id=1, source_target_pairs={{0,8},{8,0},{16,24},{24,16},{32,40},{40,32},{48,56},{56,48},{64,72... | collective-permute-start | bytes 774152 | tf_op jit(solution)/shard_map/ppermute | solution.py:320
  39.8 10.3 %collective-permute-start.14 = (bf16[16,8064]{1,0:T(8,128)(2,1)S(1)}, bf16[16,8064]{1,0:T(8,128)(2,1)S(1)}, u32[]{:S(2)}, u32[]{:S(2)}) collective-permute-start(bf16[16,8064]{1,0:T(8,128)(2,1)S(1)} %collective-permute-done.6.refs_7_), channel_id=1, source_target_pairs={{0,112},{8,120},{16,64},{24,72},{32,80},{40,88},{48,96},{56,104},{... | collective-permute-start | bytes 774152 | tf_op jit(solution)/shard_map/ppermute | solution.py:317
  42.5 18.4 %copy-start.2 = (bf16[16,8064]{1,0:T(8,128)(2,1)}, bf16[16,8064]{1,0:T(8,128)(2,1)S(1)}, u32[]{:S(2)}) copy-start(bf16[16,8064]{1,0:T(8,128)(2,1)S(1)} %collective-permute-done.16.refs_13_) | copy-start | bytes 774148
  42.5 11.2 %collective-permute-start.12 = (bf16[16,8064]{1,0:T(8,128)(2,1)S(1)}, bf16[16,8064]{1,0:T(8,128)(2,1)S(1)}, u32[]{:S(2)}, u32[]{:S(2)}) collective-permute-start(bf16[16,8064]{1,0:T(8,128)(2,1)S(1)} %collective-permute-done.5.refs_6_), channel_id=1, source_target_pairs={{0,48},{8,56},{16,0},{24,8},{32,16},{40,24},{48,32},{56,40},{64,11... | collective-permute-start | bytes 774152 | tf_op jit(solution)/shard_map/ppermute | solution.py:317
  44.2 16.7 %copy-start.3 = (bf16[16,8064]{1,0:T(8,128)(2,1)}, bf16[16,8064]{1,0:T(8,128)(2,1)S(1)}, u32[]{:S(2)}) copy-start(bf16[16,8064]{1,0:T(8,128)(2,1)S(1)} %collective-permute-done.15.refs_12_) | copy-start | bytes 774148
  44.2 10.2 %collective-permute-start.11 = (bf16[16,8064]{1,0:T(8,128)(2,1)S(1)}, bf16[16,8064]{1,0:T(8,128)(2,1)S(1)}, u32[]{:S(2)}, u32[]{:S(2)}) collective-permute-start(bf16[16,8064]{1,0:T(8,128)(2,1)S(1)} %collective-permute-done.5.refs_6_), channel_id=1, source_target_pairs={{0,16},{8,24},{16,32},{24,40},{32,48},{40,56},{48,0},{56,8},{64,80... | collective-permute-start | bytes 774152 | tf_op jit(solution)/shard_map/ppermute | solution.py:317
  47.8 13.2 %copy-start.4 = (bf16[16,8064]{1,0:T(8,128)(2,1)}, bf16[16,8064]{1,0:T(8,128)(2,1)S(1)}, u32[]{:S(2)}) copy-start(bf16[16,8064]{1,0:T(8,128)(2,1)S(1)} %collective-permute-done.13.refs_10_) | copy-start | bytes 774148
  47.8 6.9 %collective-permute-start.17 = (bf16[16,8064]{1,0:T(8,128)(2,1)S(1)}, bf16[16,8064]{1,0:T(8,128)(2,1)S(1)}, u32[]{:S(2)}, u32[]{:S(2)}) collective-permute-start(bf16[16,8064]{1,0:T(8,128)(2,1)S(1)} %collective-permute-done.5.refs_6_), channel_id=1, source_target_pairs={{0,8},{8,0},{16,24},{24,16},{32,40},{40,32},{48,56},{56,48},{64,72... | collective-permute-start | bytes 774152 | tf_op jit(solution)/shard_map/ppermute | solution.py:320
  49.7 11.3 %copy-start.5 = (bf16[16,8064]{1,0:T(8,128)(2,1)}, bf16[16,8064]{1,0:T(8,128)(2,1)S(1)}, u32[]{:S(2)}) copy-start(bf16[16,8064]{1,0:T(8,128)(2,1)S(1)} %collective-permute-done.18.refs_15_) | copy-start | bytes 774148
  49.7 7.7 %collective-permute-start.21 = (bf16[16,8064]{1,0:T(8,128)(2,1)S(1)}, bf16[16,8064]{1,0:T(8,128)(2,1)S(1)}, u32[]{:S(2)}, u32[]{:S(2)}) collective-permute-start(bf16[16,8064]{1,0:T(8,128)(2,1)S(1)} %collective-permute-done.13.refs_10_), channel_id=1, source_target_pairs={{0,8},{8,0},{16,24},{24,16},{32,40},{40,32},{48,56},{56,48},{64,72... | collective-permute-start | bytes 774152 | tf_op jit(solution)/shard_map/ppermute | solution.py:320
  50.1 10.9 %copy-start.6 = (bf16[16,8064]{1,0:T(8,128)(2,1)}, bf16[16,8064]{1,0:T(8,128)(2,1)S(1)}, u32[]{:S(2)}) copy-start(bf16[16,8064]{1,0:T(8,128)(2,1)S(1)} %collective-permute-done.14.refs_11_) | copy-start | bytes 774148
  50.1 7.3 %collective-permute-start.22 = (bf16[16,8064]{1,0:T(8,128)(2,1)S(1)}, bf16[16,8064]{1,0:T(8,128)(2,1)S(1)}, u32[]{:S(2)}, u32[]{:S(2)}) collective-permute-start(bf16[16,8064]{1,0:T(8,128)(2,1)S(1)} %collective-permute-done.14.refs_11_), channel_id=1, source_target_pairs={{0,8},{8,0},{16,24},{24,16},{32,40},{40,32},{48,56},{56,48},{64,72... | collective-permute-start | bytes 774152 | tf_op jit(solution)/shard_map/ppermute | solution.py:320
  53.7 7.3 %copy-start.7 = (bf16[16,8064]{1,0:T(8,128)(2,1)}, bf16[16,8064]{1,0:T(8,128)(2,1)S(1)}, u32[]{:S(2)}) copy-start(bf16[16,8064]{1,0:T(8,128)(2,1)S(1)} %collective-permute-done.12.refs_9_) | copy-start | bytes 774148
  53.7 3.8 %collective-permute-start.20 = (bf16[16,8064]{1,0:T(8,128)(2,1)S(1)}, bf16[16,8064]{1,0:T(8,128)(2,1)S(1)}, u32[]{:S(2)}, u32[]{:S(2)}) collective-permute-start(bf16[16,8064]{1,0:T(8,128)(2,1)S(1)} %collective-permute-done.12.refs_9_), channel_id=1, source_target_pairs={{0,8},{8,0},{16,24},{24,16},{32,40},{40,32},{48,56},{56,48},{64,72... | collective-permute-start | bytes 774152 | tf_op jit(solution)/shard_map/ppermute | solution.py:320
  54.5 6.5 %copy-start.8 = (bf16[16,8064]{1,0:T(8,128)(2,1)}, bf16[16,8064]{1,0:T(8,128)(2,1)S(1)}, u32[]{:S(2)}) copy-start(bf16[16,8064]{1,0:T(8,128)(2,1)S(1)} %collective-permute-done.11.refs_8_) | copy-start | bytes 774148
  54.5 6.4 %collective-permute-start.19 = (bf16[16,8064]{1,0:T(8,128)(2,1)S(1)}, bf16[16,8064]{1,0:T(8,128)(2,1)S(1)}, u32[]{:S(2)}, u32[]{:S(2)}) collective-permute-start(bf16[16,8064]{1,0:T(8,128)(2,1)S(1)} %collective-permute-done.11.refs_8_), channel_id=1, source_target_pairs={{0,8},{8,0},{16,24},{24,16},{32,40},{40,32},{48,56},{56,48},{64,72... | collective-permute-start | bytes 774152 | tf_op jit(solution)/shard_map/ppermute | solution.py:320
  54.7 6.3 %copy-start.9 = (bf16[16,8064]{1,0:T(8,128)(2,1)}, bf16[16,8064]{1,0:T(8,128)(2,1)S(1)}, u32[]{:S(2)}) copy-start(bf16[16,8064]{1,0:T(8,128)(2,1)S(1)} %collective-permute-done.17.refs_14_) | copy-start | bytes 774148
  54.7 27.3 %collective-permute-start.8 = (bf16[16,8064]{1,0:T(8,128)(2,1)S(1)}, bf16[16,8064]{1,0:T(8,128)(2,1)S(1)}, u32[]{:S(2)}, u32[]{:S(2)}) collective-permute-start(bf16[16,8064]{1,0:T(8,128)(2,1)S(1)} %collective-permute-done.refs_2_), channel_id=1, source_target_pairs={{0,3},{1,0},{2,1},{3,2},{4,7},{5,4},{6,5},{7,6},{8,11},{9,8},{10,9... | collective-permute-start | bytes 774152 | tf_op jit(solution)/shard_map/ppermute | solution.py:314
  57.4 3.6 %copy-start.10 = (bf16[16,8064]{1,0:T(8,128)(2,1)}, bf16[16,8064]{1,0:T(8,128)(2,1)S(1)}, u32[]{:S(2)}) copy-start(bf16[16,8064]{1,0:T(8,128)(2,1)S(1)} %collective-permute-done.21.refs_18_) | copy-start | bytes 774148
  57.4 24.6 %collective-permute-start.7 = (bf16[16,8064]{1,0:T(8,128)(2,1)S(1)}, bf16[16,8064]{1,0:T(8,128)(2,1)S(1)}, u32[]{:S(2)}, u32[]{:S(2)}) collective-permute-start(bf16[16,8064]{1,0:T(8,128)(2,1)S(1)} %collective-permute-done.refs_2_), channel_id=1, source_target_pairs={{0,1},{1,2},{2,3},{3,0},{4,5},{5,6},{6,7},{7,4},{8,9},{9,10},{10,1... | collective-permute-start | bytes 774152 | tf_op jit(solution)/shard_map/ppermute | solution.py:314
  57.4 3.6 %copy-start.11 = (bf16[16,8064]{1,0:T(8,128)(2,1)}, bf16[16,8064]{1,0:T(8,128)(2,1)S(1)}, u32[]{:S(2)}) copy-start(bf16[16,8064]{1,0:T(8,128)(2,1)S(1)} %collective-permute-done.22.refs_19_) | copy-start | bytes 774148
  57.4 24.5 %collective-permute-start.9 = (bf16[16,8064]{1,0:T(8,128)(2,1)S(1)}, bf16[16,8064]{1,0:T(8,128)(2,1)S(1)}, u32[]{:S(2)}, u32[]{:S(2)}) collective-permute-start(bf16[16,8064]{1,0:T(8,128)(2,1)S(1)} %collective-permute-done.2.refs_0_), channel_id=1, source_target_pairs={{0,1},{1,2},{2,3},{3,0},{4,5},{5,6},{6,7},{7,4},{8,9},{9,10},{10,1... | collective-permute-start | bytes 774152 | tf_op jit(solution)/shard_map/ppermute | solution.py:314
  57.5 3.5 %copy-start.12 = (bf16[16,8064]{1,0:T(8,128)(2,1)}, bf16[16,8064]{1,0:T(8,128)(2,1)S(1)}, u32[]{:S(2)}) copy-start(bf16[16,8064]{1,0:T(8,128)(2,1)S(1)} %collective-permute-done.20.refs_17_) | copy-start | bytes 774148
  57.5 24.4 %collective-permute-start.10 = (bf16[16,8064]{1,0:T(8,128)(2,1)S(1)}, bf16[16,8064]{1,0:T(8,128)(2,1)S(1)}, u32[]{:S(2)}, u32[]{:S(2)}) collective-permute-start(bf16[16,8064]{1,0:T(8,128)(2,1)S(1)} %collective-permute-done.3.refs_3_), channel_id=1, source_target_pairs={{0,7},{1,4},{2,5},{3,6},{4,3},{5,0},{6,1},{7,2},{8,15},{9,12},{10,... | collective-permute-start | bytes 774152 | tf_op jit(solution)/shard_map/ppermute | solution.py:314
  61.0 0.7 copy-start.13
  61.7 0.9 copy-start

commit v7 on v6

--- a/solution.py
+++ b/solution.py
@@ -289,7 +289,7 @@
             pltpu.SemaphoreType.DMA((2,)),
             pltpu.SemaphoreType.DMA((len(col_blocks) + 1,)),
         ],
-        compiler_params=pltpu.CompilerParams(vmem_limit_bytes=52 * 1024 * 1024),
+        compiler_params=pltpu.CompilerParams(vmem_limit_bytes=45 * 1024 * 1024),
         cost_estimate=pl.CostEstimate(flops=n * 2 * 10**8, bytes_accessed=10**7, transcendentals=0),
     )(*inputs)
 

time: 102 us -> 111 us (1.088)
  Pallas kernels: 42.2 us -> 50 us
    pallas_call x2, Pallas kernels: 38.8 us -> 46.6 us  [correlate(): pl.pallas_call(functools.partial(correlate_kernel, tuple(rows), tuple(col...]
    unnamed x29 -> x5, local copies, waits for them, and re-layouts: 3.53 us -> 4.53 us
  transfers between devices with their start and end apart: 23 -> 23, of which waited for: 9 -> 9; matrix products, arithmetic and copies ran while one was open for 0% -> 0% of each run, Pallas kernels for 19% -> 21%
where the time goes in v7:
time: 111 us; the launch traced here: 110 us
  Pallas kernels  50 us (45%)
  starting transfers between devices  34.8 us (31%)
  waiting for transfers between devices  20.8 us (19%)
  local copies, waits for them, and re-layouts  4.53 us (4%)
    pallas_call x2, Pallas kernels, correlate(): pl.pallas_call(functools.partial(correlate_kernel, tuple(rows), tuple(col...  46.6 us
    ppermute x7, waiting for transfers between devices, over_src(): lax.ppermute(value, 'src', [(i, 2 * step(i // 2, ring, side) + i % 2) for...  14.5 us
    ppermute x7, starting transfers between devices, over_rcv(): lax.ppermute(value, 'rcv', [(i, step(i, ring, side)) for i in range(8)])  12.3 us
    ppermute x7, starting transfers between devices, over_src(): lax.ppermute(value, 'src', [(i, 2 * step(i // 2, ring, side) + i % 2) for...  12.1 us
    ppermute x8, starting transfers between devices, other_core(): return lax.ppermute(value, 'src', [(i, i ^ 1) for i in range(16)])  6.64 us
    unnamed x5, local copies, waits for them, and re-layouts  4.53 us
    ppermute x1, starting transfers between devices, body(): turned = lax.ppermute(white, ('src', 'rcv'), flip)  3.74 us
    ppermute x7, waiting for transfers between devices, over_rcv(): lax.ppermute(value, 'rcv', [(i, step(i, ring, side)) for i in range(8)])  3.72 us
  transfers between devices with their start and end apart: 23, of which 9 were waited for; matrix products, arithmetic and copies ran while one was open for 0% of the time, Pallas kernels for 21%

profile of v7, /device:TPU:1, one launch (start us, length us, event | category | flops | bytes accessed | tf_op | source)
XLA Modules:
  0.0 110.4 jit_solution(15537794216468937762)
XLA Ops:
  0.0 1.8 %copy.7.spectra_ref = bf16[16,2,10,400]{3,2,1,0:T(8,128)(2,1)} copy(bf16[16,2,10,400]{3,1,2,0:T(2,128)(2,1)} %param.5) | data formatting | bytes 512000 | tf_op args[0]
  1.8 3.4 %shard_map.55.refs_1_ = bf16[16,8064]{1,0:T(8,128)(2,1)} custom-call(s32[16]{0:T(128)} %mask_ref.1, bf16[16,2,10,400]{3,2,1,0:T(8,128)(2,1)} %copy.7.spectra_ref, s32[16,10]{1,0:T(8,128)} %offsets_ref.1), custom_call_target="tpu_custom_call" | custom-call | tf_op jit(solution)/shard_map/pallas_call | solution.py:88
  5.2 3.7 %collective-permute-start.1 = (bf16[16,8064]{1,0:T(8,128)(2,1)}, bf16[16,8064]{1,0:T(8,128)(2,1)S(1)}, u32[]{:S(2)}, u32[]{:S(2)}) collective-permute-start(bf16[16,8064]{1,0:T(8,128)(2,1)} %shard_map.55.refs_1_), channel_id=1, source_target_pairs={{2,0},{3,16},{0,32},{1,48},{6,64},{7,80},{4,96},{5,112},{10,8},{11... | collective-permute-start | bytes 774152 | tf_op jit(solution)/shard_map/ppermute | solution.py:325
  9.0 3.0 %collective-permute-start = (bf16[16,8064]{1,0:T(8,128)(2,1)}, bf16[16,8064]{1,0:T(8,128)(2,1)S(1)}, u32[]{:S(2)}, u32[]{:S(2)}) collective-permute-start(bf16[16,8064]{1,0:T(8,128)(2,1)} %shard_map.55.refs_1_), channel_id=1, source_target_pairs={{0,4},{1,5},{2,6},{3,7},{4,0},{5,1},{6,2},{7,3},{8,12},{9,13},{10,... | collective-permute-start | bytes 774152 | tf_op jit(solution)/shard_map/ppermute | solution.py:314
  12.0 2.5 %collective-permute-done.1.refs_5_ = bf16[16,8064]{1,0:T(8,128)(2,1)S(1)} collective-permute-done((bf16[16,8064]{1,0:T(8,128)(2,1)}, bf16[16,8064]{1,0:T(8,128)(2,1)S(1)}, u32[]{:S(2)}, u32[]{:S(2)}) %collective-permute-start.1) | collective-permute-done | bytes 258080 | tf_op jit(solution)/shard_map/ppermute | solution.py:325
  14.5 3.3 %collective-permute-done.refs_2_ = bf16[16,8064]{1,0:T(8,128)(2,1)S(1)} collective-permute-done((bf16[16,8064]{1,0:T(8,128)(2,1)}, bf16[16,8064]{1,0:T(8,128)(2,1)S(1)}, u32[]{:S(2)}, u32[]{:S(2)}) %collective-permute-start) | collective-permute-done | bytes 258080 | tf_op jit(solution)/shard_map/ppermute | solution.py:314
  17.8 2.8 %collective-permute-start.3 = (bf16[16,8064]{1,0:T(8,128)(2,1)}, bf16[16,8064]{1,0:T(8,128)(2,1)S(1)}, u32[]{:S(2)}, u32[]{:S(2)}) collective-permute-start(bf16[16,8064]{1,0:T(8,128)(2,1)} %shard_map.55.refs_1_), channel_id=1, source_target_pairs={{0,3},{1,0},{2,1},{3,2},{4,7},{5,4},{6,5},{7,6},{8,11},{9,8},{10,9... | collective-permute-start | bytes 774152 | tf_op jit(solution)/shard_map/ppermute | solution.py:314
  20.6 0.4 collective-permute-start.2
  21.0 3.6 %collective-permute-start.6 = (bf16[16,8064]{1,0:T(8,128)(2,1)S(1)}, bf16[16,8064]{1,0:T(8,128)(2,1)S(1)}, u32[]{:S(2)}, u32[]{:S(2)}) collective-permute-start(bf16[16,8064]{1,0:T(8,128)(2,1)S(1)} %collective-permute-done.1.refs_5_), channel_id=1, source_target_pairs={{0,48},{8,56},{16,0},{24,8},{32,16},{40,24},{48,32},{56,40},{64,11... | collective-permute-start | bytes 774152 | tf_op jit(solution)/shard_map/ppermute | solution.py:317
  24.6 3.1 %collective-permute-start.5 = (bf16[16,8064]{1,0:T(8,128)(2,1)S(1)}, bf16[16,8064]{1,0:T(8,128)(2,1)S(1)}, u32[]{:S(2)}, u32[]{:S(2)}) collective-permute-start(bf16[16,8064]{1,0:T(8,128)(2,1)S(1)} %collective-permute-done.1.refs_5_), channel_id=1, source_target_pairs={{0,64},{8,72},{16,80},{24,88},{32,96},{40,104},{48,112},{56,120},{... | collective-permute-start | bytes 774152 | tf_op jit(solution)/shard_map/ppermute | solution.py:317
  27.7 0.9 collective-permute-start.4
  28.6 0.0 collective-permute-done.3.refs_3_
  28.7 0.4 collective-permute-done.2.refs_0_
  29.0 0.3 collective-permute-done.6.refs_7_
  29.3 3.4 %collective-permute-done.5.refs_6_ = bf16[16,8064]{1,0:T(8,128)(2,1)S(1)} collective-permute-done((bf16[16,8064]{1,0:T(8,128)(2,1)S(1)}, bf16[16,8064]{1,0:T(8,128)(2,1)S(1)}, u32[]{:S(2)}, u32[]{:S(2)}) %collective-permute-start.5) | collective-permute-done | bytes 258080 | tf_op jit(solution)/shard_map/ppermute | solution.py:317
  32.7 4.5 %collective-permute-done.4.refs_4_ = bf16[16,8064]{1,0:T(8,128)(2,1)S(1)} collective-permute-done((bf16[16,8064]{1,0:T(8,128)(2,1)S(1)}, bf16[16,8064]{1,0:T(8,128)(2,1)S(1)}, u32[]{:S(2)}, u32[]{:S(2)}) %collective-permute-start.4) | collective-permute-done | bytes 258080 | tf_op jit(solution)/shard_map/ppermute | solution.py:317
  37.2 2.1 %collective-permute-start.16 = (bf16[16,8064]{1,0:T(8,128)(2,1)S(1)}, bf16[16,8064]{1,0:T(8,128)(2,1)S(1)}, u32[]{:S(2)}, u32[]{:S(2)}) collective-permute-start(bf16[16,8064]{1,0:T(8,128)(2,1)S(1)} %collective-permute-done.1.refs_5_), channel_id=1, source_target_pairs={{0,8},{8,0},{16,24},{24,16},{32,40},{40,32},{48,56},{56,48},{64,72... | collective-permute-start | bytes 774152 | tf_op jit(solution)/shard_map/ppermute | solution.py:320
  39.3 0.0 collective-permute-start.15
  39.3 0.0 collective-permute-start.13
  39.3 0.5 collective-permute-start.18
  39.8 2.7 %collective-permute-start.14 = (bf16[16,8064]{1,0:T(8,128)(2,1)S(1)}, bf16[16,8064]{1,0:T(8,128)(2,1)S(1)}, u32[]{:S(2)}, u32[]{:S(2)}) collective-permute-start(bf16[16,8064]{1,0:T(8,128)(2,1)S(1)} %collective-permute-done.6.refs_7_), channel_id=1, source_target_pairs={{0,112},{8,120},{16,64},{24,72},{32,80},{40,88},{48,96},{56,104},{... | collective-permute-start | bytes 774152 | tf_op jit(solution)/shard_map/ppermute | solution.py:317
  42.5 0.0 collective-permute-done.16.refs_13_
  42.5 1.7 %collective-permute-start.12 = (bf16[16,8064]{1,0:T(8,128)(2,1)S(1)}, bf16[16,8064]{1,0:T(8,128)(2,1)S(1)}, u32[]{:S(2)}, u32[]{:S(2)}) collective-permute-start(bf16[16,8064]{1,0:T(8,128)(2,1)S(1)} %collective-permute-done.5.refs_6_), channel_id=1, source_target_pairs={{0,48},{8,56},{16,0},{24,8},{32,16},{40,24},{48,32},{56,40},{64,11... | collective-permute-start | bytes 774152 | tf_op jit(solution)/shard_map/ppermute | solution.py:317
  44.2 0.0 collective-permute-done.15.refs_12_
  44.2 0.0 collective-permute-start.11
  44.3 3.5 %collective-permute-done.13.refs_10_ = bf16[16,8064]{1,0:T(8,128)(2,1)S(1)} collective-permute-done((bf16[16,8064]{1,0:T(8,128)(2,1)S(1)}, bf16[16,8064]{1,0:T(8,128)(2,1)S(1)}, u32[]{:S(2)}, u32[]{:S(2)}) %collective-permute-start.13) | collective-permute-done | bytes 258080 | tf_op jit(solution)/shard_map/ppermute | solution.py:317
  47.8 1.9 %collective-permute-start.17 = (bf16[16,8064]{1,0:T(8,128)(2,1)S(1)}, bf16[16,8064]{1,0:T(8,128)(2,1)S(1)}, u32[]{:S(2)}, u32[]{:S(2)}) collective-permute-start(bf16[16,8064]{1,0:T(8,128)(2,1)S(1)} %collective-permute-done.5.refs_6_), channel_id=1, source_target_pairs={{0,8},{8,0},{16,24},{24,16},{32,40},{40,32},{48,56},{56,48},{64,72... | collective-permute-start | bytes 774152 | tf_op jit(solution)/shard_map/ppermute | solution.py:320
  49.7 0.0 collective-permute-done.18.refs_15_
  49.7 0.0 collective-permute-start.21
  49.7 0.4 collective-permute-done.14.refs_11_
  50.1 1.2 %collective-permute-start.22 = (bf16[16,8064]{1,0:T(8,128)(2,1)S(1)}, bf16[16,8064]{1,0:T(8,128)(2,1)S(1)}, u32[]{:S(2)}, u32[]{:S(2)}) collective-permute-start(bf16[16,8064]{1,0:T(8,128)(2,1)S(1)} %collective-permute-done.14.refs_11_), channel_id=1, source_target_pairs={{0,8},{8,0},{16,24},{24,16},{32,40},{40,32},{48,56},{56,48},{64,72... | collective-permute-start | bytes 774152 | tf_op jit(solution)/shard_map/ppermute | solution.py:320
  51.2 2.4 %collective-permute-done.12.refs_9_ = bf16[16,8064]{1,0:T(8,128)(2,1)S(1)} collective-permute-done((bf16[16,8064]{1,0:T(8,128)(2,1)S(1)}, bf16[16,8064]{1,0:T(8,128)(2,1)S(1)}, u32[]{:S(2)}, u32[]{:S(2)}) %collective-permute-start.12) | collective-permute-done | bytes 258080 | tf_op jit(solution)/shard_map/ppermute | solution.py:317
  53.7 0.8 collective-permute-start.20
  54.5 0.0 collective-permute-done.11.refs_8_
  54.5 0.2 collective-permute-start.19
  54.7 0.0 collective-permute-done.17.refs_14_
  54.7 2.7 %collective-permute-start.8 = (bf16[16,8064]{1,0:T(8,128)(2,1)S(1)}, bf16[16,8064]{1,0:T(8,128)(2,1)S(1)}, u32[]{:S(2)}, u32[]{:S(2)}) collective-permute-start(bf16[16,8064]{1,0:T(8,128)(2,1)S(1)} %collective-permute-done.refs_2_), channel_id=1, source_target_pairs={{0,3},{1,0},{2,1},{3,2},{4,7},{5,4},{6,5},{7,6},{8,11},{9,8},{10,9... | collective-permute-start | bytes 774152 | tf_op jit(solution)/shard_map/ppermute | solution.py:314
  57.4 0.0 collective-permute-done.21.refs_18_
  57.4 0.1 collective-permute-start.9
  57.5 3.4 %collective-permute-start.10 = (bf16[16,8064]{1,0:T(8,128)(2,1)S(1)}, bf16[16,8064]{1,0:T(8,128)(2,1)S(1)}, u32[]{:S(2)}, u32[]{:S(2)}) collective-permute-start(bf16[16,8064]{1,0:T(8,128)(2,1)S(1)} %collective-permute-done.3.refs_3_), channel_id=1, source_target_pairs={{0,7},{1,4},{2,5},{3,6},{4,3},{5,0},{6,1},{7,2},{8,15},{9,12},{10,... | collective-permute-start | bytes 774152 | tf_op jit(solution)/shard_map/ppermute | solution.py:314
  60.9 0.0 collective-permute-done.19.refs_16_
  60.9 0.9 copy-done
  61.8 1.7 %copy-done.1 = bf16[2,40,64,256]{3,2,1,0:T(8,128)(2,1)S(1)} copy-done((bf16[2,40,64,256]{3,2,1,0:T(8,128)(2,1)S(1)}, bf16[2,40,64,256]{3,2,1,0:T(8,128)(2,1)}, u32[]{:S(2)}) %copy-start.1) | copy-done | bytes 2621464
  63.6 23.1 %shard_map.56.refs_21_ = bf16[101,128,256]{2,1,0:T(8,128)(2,1)} custom-call(bf16[16,8064]{1,0:T(8,128)(2,1)S(1)} %collective-permute-done.2.refs_0_, bf16[16,8064]{1,0:T(8,128)(2,1)S(1)} %copy-done, bf16[16,8064]{1,0:T(8,128)(2,1)S(1)} %collective-permute-done.refs_2_, bf16[16,8064]{1,0:T(8,128)(2,1)S(1)} %collective-permute-done.3.refs_3_, ...), custom_call_target="tpu_custom_call" | custom-call | flops 12800000000 | bytes 10000000 | tf_op jit(solution)/shard_map/pallas_call | solution.py:275
  86.7 0.0 collective-permute-done.9.refs_2_
  86.7 0.0 collective-permute-done.8.refs_1_
  86.7 0.0 collective-permute-done.7.refs_0_
  86.7 23.4 %shard_map.57 = bf16[101,128,256]{2,1,0:T(8,128)(2,1)} custom-call(bf16[16,8064]{1,0:T(8,128)(2,1)S(1)} %collective-permute-done.7.refs_0_, bf16[16,8064]{1,0:T(8,128)(2,1)S(1)} %collective-permute-done.8.refs_1_, bf16[16,8064]{1,0:T(8,128)(2,1)S(1)} %collective-permute-done.9.refs_2_, ...), custom_call_target="tpu_custom_call", output_to_operand_aliasing={{}: (21, {})} | custom-call | flops 12800000000 | bytes 10000000 | tf_op jit(solution)/shard_map/pallas_call | solution.py:275
  (6 shorter events, 0.0 us)
Async XLA Ops:
  5.2 9.3 %collective-permute-start.1 = (bf16[16,8064]{1,0:T(8,128)(2,1)}, bf16[16,8064]{1,0:T(8,128)(2,1)S(1)}, u32[]{:S(2)}, u32[]{:S(2)}) collective-permute-start(bf16[16,8064]{1,0:T(8,128)(2,1)} %shard_map.55.refs_1_), channel_id=1, source_target_pairs={{2,0},{3,16},{0,32},{1,48},{6,64},{7,80},{4,96},{5,112},{10,8},{11... | collective-permute-start | bytes 774152 | tf_op jit(solution)/shard_map/ppermute | solution.py:325
  9.0 8.9 %collective-permute-start = (bf16[16,8064]{1,0:T(8,128)(2,1)}, bf16[16,8064]{1,0:T(8,128)(2,1)S(1)}, u32[]{:S(2)}, u32[]{:S(2)}) collective-permute-start(bf16[16,8064]{1,0:T(8,128)(2,1)} %shard_map.55.refs_1_), channel_id=1, source_target_pairs={{0,4},{1,5},{2,6},{3,7},{4,0},{5,1},{6,2},{7,3},{8,12},{9,13},{10,... | collective-permute-start | bytes 774152 | tf_op jit(solution)/shard_map/ppermute | solution.py:314
  17.8 10.8 %collective-permute-start.3 = (bf16[16,8064]{1,0:T(8,128)(2,1)}, bf16[16,8064]{1,0:T(8,128)(2,1)S(1)}, u32[]{:S(2)}, u32[]{:S(2)}) collective-permute-start(bf16[16,8064]{1,0:T(8,128)(2,1)} %shard_map.55.refs_1_), channel_id=1, source_target_pairs={{0,3},{1,0},{2,1},{3,2},{4,7},{5,4},{6,5},{7,6},{8,11},{9,8},{10,9... | collective-permute-start | bytes 774152 | tf_op jit(solution)/shard_map/ppermute | solution.py:314
  20.6 8.4 %collective-permute-start.2 = (bf16[16,8064]{1,0:T(8,128)(2,1)}, bf16[16,8064]{1,0:T(8,128)(2,1)S(1)}, u32[]{:S(2)}, u32[]{:S(2)}) collective-permute-start(bf16[16,8064]{1,0:T(8,128)(2,1)} %shard_map.55.refs_1_), channel_id=1, source_target_pairs={{0,1},{1,2},{2,3},{3,0},{4,5},{5,6},{6,7},{7,4},{8,9},{9,10},{10,1... | collective-permute-start | bytes 774152 | tf_op jit(solution)/shard_map/ppermute | solution.py:314
  21.0 8.3 %collective-permute-start.6 = (bf16[16,8064]{1,0:T(8,128)(2,1)S(1)}, bf16[16,8064]{1,0:T(8,128)(2,1)S(1)}, u32[]{:S(2)}, u32[]{:S(2)}) collective-permute-start(bf16[16,8064]{1,0:T(8,128)(2,1)S(1)} %collective-permute-done.1.refs_5_), channel_id=1, source_target_pairs={{0,48},{8,56},{16,0},{24,8},{32,16},{40,24},{48,32},{56,40},{64,11... | collective-permute-start | bytes 774152 | tf_op jit(solution)/shard_map/ppermute | solution.py:317
  24.6 8.1 %collective-permute-start.5 = (bf16[16,8064]{1,0:T(8,128)(2,1)S(1)}, bf16[16,8064]{1,0:T(8,128)(2,1)S(1)}, u32[]{:S(2)}, u32[]{:S(2)}) collective-permute-start(bf16[16,8064]{1,0:T(8,128)(2,1)S(1)} %collective-permute-done.1.refs_5_), channel_id=1, source_target_pairs={{0,64},{8,72},{16,80},{24,88},{32,96},{40,104},{48,112},{56,120},{... | collective-permute-start | bytes 774152 | tf_op jit(solution)/shard_map/ppermute | solution.py:317
  27.7 9.5 %collective-permute-start.4 = (bf16[16,8064]{1,0:T(8,128)(2,1)S(1)}, bf16[16,8064]{1,0:T(8,128)(2,1)S(1)}, u32[]{:S(2)}, u32[]{:S(2)}) collective-permute-start(bf16[16,8064]{1,0:T(8,128)(2,1)S(1)} %collective-permute-done.1.refs_5_), channel_id=1, source_target_pairs={{0,16},{8,24},{16,32},{24,40},{32,48},{40,56},{48,0},{56,8},{64,80... | collective-permute-start | bytes 774152 | tf_op jit(solution)/shard_map/ppermute | solution.py:317
  37.2 5.3 %collective-permute-start.16 = (bf16[16,8064]{1,0:T(8,128)(2,1)S(1)}, bf16[16,8064]{1,0:T(8,128)(2,1)S(1)}, u32[]{:S(2)}, u32[]{:S(2)}) collective-permute-start(bf16[16,8064]{1,0:T(8,128)(2,1)S(1)} %collective-permute-done.1.refs_5_), channel_id=1, source_target_pairs={{0,8},{8,0},{16,24},{24,16},{32,40},{40,32},{48,56},{56,48},{64,72... | collective-permute-start | bytes 774152 | tf_op jit(solution)/shard_map/ppermute | solution.py:320
  39.3 5.0 %collective-permute-start.15 = (bf16[16,8064]{1,0:T(8,128)(2,1)S(1)}, bf16[16,8064]{1,0:T(8,128)(2,1)S(1)}, u32[]{:S(2)}, u32[]{:S(2)}) collective-permute-start(bf16[16,8064]{1,0:T(8,128)(2,1)S(1)} %collective-permute-done.4.refs_4_), channel_id=1, source_target_pairs={{0,8},{8,0},{16,24},{24,16},{32,40},{40,32},{48,56},{56,48},{64,72... | collective-permute-start | bytes 774152 | tf_op jit(solution)/shard_map/ppermute | solution.py:320
  39.3 8.5 %collective-permute-start.13 = (bf16[16,8064]{1,0:T(8,128)(2,1)S(1)}, bf16[16,8064]{1,0:T(8,128)(2,1)S(1)}, u32[]{:S(2)}, u32[]{:S(2)}) collective-permute-start(bf16[16,8064]{1,0:T(8,128)(2,1)S(1)} %collective-permute-done.4.refs_4_), channel_id=1, source_target_pairs={{0,16},{8,24},{16,32},{24,40},{32,48},{40,56},{48,0},{56,8},{64,80... | collective-permute-start | bytes 774152 | tf_op jit(solution)/shard_map/ppermute | solution.py:317
  39.3 10.4 %collective-permute-start.18 = (bf16[16,8064]{1,0:T(8,128)(2,1)S(1)}, bf16[16,8064]{1,0:T(8,128)(2,1)S(1)}, u32[]{:S(2)}, u32[]{:S(2)}) collective-permute-start(bf16[16,8064]{1,0:T(8,128)(2,1)S(1)} %collective-permute-done.6.refs_7_), channel_id=1, source_target_pairs={{0,8},{8,0},{16,24},{24,16},{32,40},{40,32},{48,56},{56,48},{64,72... | collective-permute-start | bytes 774152 | tf_op jit(solution)/shard_map/ppermute | solution.py:320
  39.8 10.3 %collective-permute-start.14 = (bf16[16,8064]{1,0:T(8,128)(2,1)S(1)}, bf16[16,8064]{1,0:T(8,128)(2,1)S(1)}, u32[]{:S(2)}, u32[]{:S(2)}) collective-permute-start(bf16[16,8064]{1,0:T(8,128)(2,1)S(1)} %collective-permute-done.6.refs_7_), channel_id=1, source_target_pairs={{0,112},{8,120},{16,64},{24,72},{32,80},{40,88},{48,96},{56,104},{... | collective-permute-start | bytes 774152 | tf_op jit(solution)/shard_map/ppermute | solution.py:317
  42.5 11.2 %collective-permute-start.12 = (bf16[16,8064]{1,0:T(8,128)(2,1)S(1)}, bf16[16,8064]{1,0:T(8,128)(2,1)S(1)}, u32[]{:S(2)}, u32[]{:S(2)}) collective-permute-start(bf16[16,8064]{1,0:T(8,128)(2,1)S(1)} %collective-permute-done.5.refs_6_), channel_id=1, source_target_pairs={{0,48},{8,56},{16,0},{24,8},{32,16},{40,24},{48,32},{56,40},{64,11... | collective-permute-start | bytes 774152 | tf_op jit(solution)/shard_map/ppermute | solution.py:317
  44.2 10.2 %collective-permute-start.11 = (bf16[16,8064]{1,0:T(8,128)(2,1)S(1)}, bf16[16,8064]{1,0:T(8,128)(2,1)S(1)}, u32[]{:S(2)}, u32[]{:S(2)}) collective-permute-start(bf16[16,8064]{1,0:T(8,128)(2,1)S(1)} %collective-permute-done.5.refs_6_), channel_id=1, source_target_pairs={{0,16},{8,24},{16,32},{24,40},{32,48},{40,56},{48,0},{56,8},{64,80... | collective-permute-start | bytes 774152 | tf_op jit(solution)/shard_map/ppermute | solution.py:317
  47.8 6.9 %collective-permute-start.17 = (bf16[16,8064]{1,0:T(8,128)(2,1)S(1)}, bf16[16,8064]{1,0:T(8,128)(2,1)S(1)}, u32[]{:S(2)}, u32[]{:S(2)}) collective-permute-start(bf16[16,8064]{1,0:T(8,128)(2,1)S(1)} %collective-permute-done.5.refs_6_), channel_id=1, source_target_pairs={{0,8},{8,0},{16,24},{24,16},{32,40},{40,32},{48,56},{56,48},{64,72... | collective-permute-start | bytes 774152 | tf_op jit(solution)/shard_map/ppermute | solution.py:320
  49.7 7.7 %collective-permute-start.21 = (bf16[16,8064]{1,0:T(8,128)(2,1)S(1)}, bf16[16,8064]{1,0:T(8,128)(2,1)S(1)}, u32[]{:S(2)}, u32[]{:S(2)}) collective-permute-start(bf16[16,8064]{1,0:T(8,128)(2,1)S(1)} %collective-permute-done.13.refs_10_), channel_id=1, source_target_pairs={{0,8},{8,0},{16,24},{24,16},{32,40},{40,32},{48,56},{56,48},{64,72... | collective-permute-start | bytes 774152 | tf_op jit(solution)/shard_map/ppermute | solution.py:320
  50.1 7.3 %collective-permute-start.22 = (bf16[16,8064]{1,0:T(8,128)(2,1)S(1)}, bf16[16,8064]{1,0:T(8,128)(2,1)S(1)}, u32[]{:S(2)}, u32[]{:S(2)}) collective-permute-start(bf16[16,8064]{1,0:T(8,128)(2,1)S(1)} %collective-permute-done.14.refs_11_), channel_id=1, source_target_pairs={{0,8},{8,0},{16,24},{24,16},{32,40},{40,32},{48,56},{56,48},{64,72... | collective-permute-start | bytes 774152 | tf_op jit(solution)/shard_map/ppermute | solution.py:320
  53.7 3.8 %collective-permute-start.20 = (bf16[16,8064]{1,0:T(8,128)(2,1)S(1)}, bf16[16,8064]{1,0:T(8,128)(2,1)S(1)}, u32[]{:S(2)}, u32[]{:S(2)}) collective-permute-start(bf16[16,8064]{1,0:T(8,128)(2,1)S(1)} %collective-permute-done.12.refs_9_), channel_id=1, source_target_pairs={{0,8},{8,0},{16,24},{24,16},{32,40},{40,32},{48,56},{56,48},{64,72... | collective-permute-start | bytes 774152 | tf_op jit(solution)/shard_map/ppermute | solution.py:320
  54.5 6.4 %collective-permute-start.19 = (bf16[16,8064]{1,0:T(8,128)(2,1)S(1)}, bf16[16,8064]{1,0:T(8,128)(2,1)S(1)}, u32[]{:S(2)}, u32[]{:S(2)}) collective-permute-start(bf16[16,8064]{1,0:T(8,128)(2,1)S(1)} %collective-permute-done.11.refs_8_), channel_id=1, source_target_pairs={{0,8},{8,0},{16,24},{24,16},{32,40},{40,32},{48,56},{56,48},{64,72... | collective-permute-start | bytes 774152 | tf_op jit(solution)/shard_map/ppermute | solution.py:320
  54.7 32.0 %collective-permute-start.8 = (bf16[16,8064]{1,0:T(8,128)(2,1)S(1)}, bf16[16,8064]{1,0:T(8,128)(2,1)S(1)}, u32[]{:S(2)}, u32[]{:S(2)}) collective-permute-start(bf16[16,8064]{1,0:T(8,128)(2,1)S(1)} %collective-permute-done.refs_2_), channel_id=1, source_target_pairs={{0,3},{1,0},{2,1},{3,2},{4,7},{5,4},{6,5},{7,6},{8,11},{9,8},{10,9... | collective-permute-start | bytes 774152 | tf_op jit(solution)/shard_map/ppermute | solution.py:314
  57.4 29.4 %collective-permute-start.7 = (bf16[16,8064]{1,0:T(8,128)(2,1)S(1)}, bf16[16,8064]{1,0:T(8,128)(2,1)S(1)}, u32[]{:S(2)}, u32[]{:S(2)}) collective-permute-start(bf16[16,8064]{1,0:T(8,128)(2,1)S(1)} %collective-permute-done.refs_2_), channel_id=1, source_target_pairs={{0,1},{1,2},{2,3},{3,0},{4,5},{5,6},{6,7},{7,4},{8,9},{9,10},{10,1... | collective-permute-start | bytes 774152 | tf_op jit(solution)/shard_map/ppermute | solution.py:314
  57.4 29.3 %collective-permute-start.9 = (bf16[16,8064]{1,0:T(8,128)(2,1)S(1)}, bf16[16,8064]{1,0:T(8,128)(2,1)S(1)}, u32[]{:S(2)}, u32[]{:S(2)}) collective-permute-start(bf16[16,8064]{1,0:T(8,128)(2,1)S(1)} %collective-permute-done.2.refs_0_), channel_id=1, source_target_pairs={{0,1},{1,2},{2,3},{3,0},{4,5},{5,6},{6,7},{7,4},{8,9},{9,10},{10,1... | collective-permute-start | bytes 774152 | tf_op jit(solution)/shard_map/ppermute | solution.py:314
  57.5 29.3 %collective-permute-start.10 = (bf16[16,8064]{1,0:T(8,128)(2,1)S(1)}, bf16[16,8064]{1,0:T(8,128)(2,1)S(1)}, u32[]{:S(2)}, u32[]{:S(2)}) collective-permute-start(bf16[16,8064]{1,0:T(8,128)(2,1)S(1)} %collective-permute-done.3.refs_3_), channel_id=1, source_target_pairs={{0,7},{1,4},{2,5},{3,6},{4,3},{5,0},{6,1},{7,2},{8,15},{9,12},{10,... | collective-permute-start | bytes 774152 | tf_op jit(solution)/shard_map/ppermute | solution.py:314
  60.9 0.9 copy-start
  61.8 1.7 %copy-start.1 = (bf16[2,40,64,256]{3,2,1,0:T(8,128)(2,1)S(1)}, bf16[2,40,64,256]{3,2,1,0:T(8,128)(2,1)}, u32[]{:S(2)}) copy-start(bf16[2,40,64,256]{3,2,1,0:T(8,128)(2,1)} %constant.2.clone.refs_20_) | copy-start | bytes 7864324

commit v8 on v6

--- a/solution.py
+++ b/solution.py
@@ -25,8 +25,9 @@
 MAIN = 16
 TILES = NB + -(-NB // 4)
 LANES = TILES * 128
+SOME = 4
 DEPTH = 8
-LAG = 4
+LAG = 6
 
 
 def unit_circle(turns):
@@ -126,7 +127,7 @@
     lane = lax.broadcasted_iota(jnp.int32, (16, 128), 1)
     same_bin = (lane % 8) == lax.broadcasted_iota(jnp.int32, (16, 128), 0) % 8
     zero = jnp.zeros((), jnp.bfloat16)
-    groups = n_rows * OWN // 8
+    groups = n_rows * OWN // SOME
 
     loads = []
     for k, ref in enumerate(col_refs):
@@ -173,10 +174,10 @@
 
         def start(pair, k, same_rest):
             left = [], []
-            for u in range(8):
-                r = wide(8 * k + u, rest_lanes(pair))
+            for u in range(SOME):
+                r = wide(SOME * k + u, rest_lanes(pair))
                 for mxu in range(2):
-                    m = wide(8 * k + u, main_lanes(2 * pair + mxu))
+                    m = wide(SOME * k + u, main_lanes(2 * pair + mxu))
                     m, q = jnp.where(same_bin, m, zero), jnp.where(same_rest[mxu], r, zero)
                     left[mxu].append(jnp.concatenate([m, q], 1))
             for mxu in range(2):
@@ -186,10 +187,10 @@
         def finish(pair, k):
             product = [pltpu.matmul_pop(accs[mxu][k % DEPTH]) for mxu in range(2)]
             for part in range(2):
-                for u in range(8):
+                for u in range(SOME):
                     o = u * 16 + part * 8
                     both = jnp.concatenate([p[o : o + 8] for p in product], 0)
-                    at = pl.ds(pl.multiple_of((8 * k + u) * F + pair * 16, 16), 16)
+                    at = pl.ds(pl.multiple_of((SOME * k + u) * F + pair * 16, 16), 16)
                     cross[part, at, :] = both.astype(jnp.bfloat16)
 
         def work(pair, first, last):
@@ -260,7 +261,7 @@
             for g in range(first, first + TOGETHER):
                 emit(g)
 
-    pl.run_scoped(cross_of, *[pltpu.ACC(mxu)((128, 256), jnp.float32) for mxu in [0] * DEPTH + [1] * DEPTH])
+    pl.run_scoped(cross_of, *[pltpu.ACC(mxu)((SOME * 16, 256), jnp.float32) for mxu in [0] * DEPTH + [1] * DEPTH])
     loads[-1].wait()
     pl.run_scoped(lags_of, *[pltpu.ACC(mxu)((LAG_TILE, 256), jnp.float32) for mxu in [0] * (4 * TOGETHER) + [1] * (4 * TOGETHER)])
     for k in range(n_rows - 2, n_rows):

time: 102 us -> 99.8 us (0.978)
  Pallas kernels: 42.2 us -> 39.6 us
    pallas_call x2, Pallas kernels: 38.8 us -> 36.2 us  [correlate(): pl.pallas_call(functools.partial(correlate_kernel, tuple(rows), tuple(col...]
  transfers between devices with their start and end apart: 23 -> 23, of which waited for: 9 -> 9; matrix products, arithmetic and copies ran while one was open for 0% -> 0% of each run, Pallas kernels for 19% -> 18%
where the time goes in v8:
time: 99.8 us; the launch traced here: 99.1 us
  Pallas kernels  39.6 us (40%)
  starting transfers between devices  34.9 us (35%)
  waiting for transfers between devices  20.7 us (21%)
  local copies, waits for them, and re-layouts  3.53 us (4%)
    pallas_call x2, Pallas kernels, correlate(): pl.pallas_call(functools.partial(correlate_kernel, tuple(rows), tuple(col...  36.2 us
    ppermute x7, waiting for transfers between devices, over_src(): lax.ppermute(value, 'src', [(i, 2 * step(i // 2, ring, side) + i % 2) for...  14.4 us
    ppermute x7, starting transfers between devices, over_rcv(): lax.ppermute(value, 'rcv', [(i, step(i, ring, side)) for i in range(8)])  12.3 us
    ppermute x7, starting transfers between devices, over_src(): lax.ppermute(value, 'src', [(i, 2 * step(i // 2, ring, side) + i % 2) for...  12.1 us
    ppermute x8, starting transfers between devices, other_core(): return lax.ppermute(value, 'src', [(i, i ^ 1) for i in range(16)])  6.72 us
    ppermute x1, starting transfers between devices, body(): turned = lax.ppermute(white, ('src', 'rcv'), flip)  3.74 us
    ppermute x7, waiting for transfers between devices, over_rcv(): lax.ppermute(value, 'rcv', [(i, step(i, ring, side)) for i in range(8)])  3.72 us
    unnamed x29, local copies, waits for them, and re-layouts  3.53 us
  transfers between devices with their start and end apart: 23, of which 9 were waited for; matrix products, arithmetic and copies ran while one was open for 0% of the time, Pallas kernels for 18%

profile of v8, /device:TPU:1, one launch (start us, length us, event | category | flops | bytes accessed | tf_op | source)
XLA Modules:
  0.0 99.1 jit_solution(10997970971647881013)
XLA Ops:
  0.0 1.8 %copy.7.spectra_ref = bf16[16,2,10,400]{3,2,1,0:T(8,128)(2,1)} copy(bf16[16,2,10,400]{3,1,2,0:T(2,128)(2,1)} %param.5) | data formatting | bytes 512000 | tf_op args[0]
  1.8 3.4 %shard_map.55.refs_1_ = bf16[16,8064]{1,0:T(8,128)(2,1)} custom-call(s32[16]{0:T(128)} %mask_ref.1, bf16[16,2,10,400]{3,2,1,0:T(8,128)(2,1)} %copy.7.spectra_ref, s32[16,10]{1,0:T(8,128)} %offsets_ref.1), custom_call_target="tpu_custom_call" | custom-call | tf_op jit(solution)/shard_map/pallas_call | solution.py:89
  5.2 3.7 %collective-permute-start.1 = (bf16[16,8064]{1,0:T(8,128)(2,1)}, bf16[16,8064]{1,0:T(8,128)(2,1)S(1)}, u32[]{:S(2)}, u32[]{:S(2)}) collective-permute-start(bf16[16,8064]{1,0:T(8,128)(2,1)} %shard_map.55.refs_1_), channel_id=1, source_target_pairs={{2,0},{3,16},{0,32},{1,48},{6,64},{7,80},{4,96},{5,112},{10,8},{11... | collective-permute-start | bytes 774152 | tf_op jit(solution)/shard_map/ppermute | solution.py:326
  9.0 3.0 %collective-permute-start = (bf16[16,8064]{1,0:T(8,128)(2,1)}, bf16[16,8064]{1,0:T(8,128)(2,1)S(1)}, u32[]{:S(2)}, u32[]{:S(2)}) collective-permute-start(bf16[16,8064]{1,0:T(8,128)(2,1)} %shard_map.55.refs_1_), channel_id=1, source_target_pairs={{0,4},{1,5},{2,6},{3,7},{4,0},{5,1},{6,2},{7,3},{8,12},{9,13},{10,... | collective-permute-start | bytes 774152 | tf_op jit(solution)/shard_map/ppermute | solution.py:315
  12.0 2.5 %collective-permute-done.1.refs_5_ = bf16[16,8064]{1,0:T(8,128)(2,1)S(1)} collective-permute-done((bf16[16,8064]{1,0:T(8,128)(2,1)}, bf16[16,8064]{1,0:T(8,128)(2,1)S(1)}, u32[]{:S(2)}, u32[]{:S(2)}) %collective-permute-start.1) | collective-permute-done | bytes 258080 | tf_op jit(solution)/shard_map/ppermute | solution.py:326
  14.5 3.3 %collective-permute-done.refs_2_ = bf16[16,8064]{1,0:T(8,128)(2,1)S(1)} collective-permute-done((bf16[16,8064]{1,0:T(8,128)(2,1)}, bf16[16,8064]{1,0:T(8,128)(2,1)S(1)}, u32[]{:S(2)}, u32[]{:S(2)}) %collective-permute-start) | collective-permute-done | bytes 258080 | tf_op jit(solution)/shard_map/ppermute | solution.py:315
  17.8 2.8 %collective-permute-start.3 = (bf16[16,8064]{1,0:T(8,128)(2,1)}, bf16[16,8064]{1,0:T(8,128)(2,1)S(1)}, u32[]{:S(2)}, u32[]{:S(2)}) collective-permute-start(bf16[16,8064]{1,0:T(8,128)(2,1)} %shard_map.55.refs_1_), channel_id=1, source_target_pairs={{0,3},{1,0},{2,1},{3,2},{4,7},{5,4},{6,5},{7,6},{8,11},{9,8},{10,9... | collective-permute-start | bytes 774152 | tf_op jit(solution)/shard_map/ppermute | solution.py:315
  20.6 0.4 collective-permute-start.2
  21.0 3.6 %collective-permute-start.6 = (bf16[16,8064]{1,0:T(8,128)(2,1)S(1)}, bf16[16,8064]{1,0:T(8,128)(2,1)S(1)}, u32[]{:S(2)}, u32[]{:S(2)}) collective-permute-start(bf16[16,8064]{1,0:T(8,128)(2,1)S(1)} %collective-permute-done.1.refs_5_), channel_id=1, source_target_pairs={{0,48},{8,56},{16,0},{24,8},{32,16},{40,24},{48,32},{56,40},{64,11... | collective-permute-start | bytes 774152 | tf_op jit(solution)/shard_map/ppermute | solution.py:318
  24.6 3.1 %collective-permute-start.5 = (bf16[16,8064]{1,0:T(8,128)(2,1)S(1)}, bf16[16,8064]{1,0:T(8,128)(2,1)S(1)}, u32[]{:S(2)}, u32[]{:S(2)}) collective-permute-start(bf16[16,8064]{1,0:T(8,128)(2,1)S(1)} %collective-permute-done.1.refs_5_), channel_id=1, source_target_pairs={{0,64},{8,72},{16,80},{24,88},{32,96},{40,104},{48,112},{56,120},{... | collective-permute-start | bytes 774152 | tf_op jit(solution)/shard_map/ppermute | solution.py:318
  27.7 0.9 collective-permute-start.4
  28.6 0.0 collective-permute-done.3.refs_3_
  28.7 0.4 collective-permute-done.2.refs_0_
  29.0 0.3 collective-permute-done.6.refs_7_
  29.3 3.4 %collective-permute-done.5.refs_6_ = bf16[16,8064]{1,0:T(8,128)(2,1)S(1)} collective-permute-done((bf16[16,8064]{1,0:T(8,128)(2,1)S(1)}, bf16[16,8064]{1,0:T(8,128)(2,1)S(1)}, u32[]{:S(2)}, u32[]{:S(2)}) %collective-permute-start.5) | collective-permute-done | bytes 258080 | tf_op jit(solution)/shard_map/ppermute | solution.py:318
  32.7 4.5 %collective-permute-done.4.refs_4_ = bf16[16,8064]{1,0:T(8,128)(2,1)S(1)} collective-permute-done((bf16[16,8064]{1,0:T(8,128)(2,1)S(1)}, bf16[16,8064]{1,0:T(8,128)(2,1)S(1)}, u32[]{:S(2)}, u32[]{:S(2)}) %collective-permute-start.4) | collective-permute-done | bytes 258080 | tf_op jit(solution)/shard_map/ppermute | solution.py:318
  37.2 2.1 %collective-permute-start.16 = (bf16[16,8064]{1,0:T(8,128)(2,1)S(1)}, bf16[16,8064]{1,0:T(8,128)(2,1)S(1)}, u32[]{:S(2)}, u32[]{:S(2)}) collective-permute-start(bf16[16,8064]{1,0:T(8,128)(2,1)S(1)} %collective-permute-done.1.refs_5_), channel_id=1, source_target_pairs={{0,8},{8,0},{16,24},{24,16},{32,40},{40,32},{48,56},{56,48},{64,72... | collective-permute-start | bytes 774152 | tf_op jit(solution)/shard_map/ppermute | solution.py:321
  39.3 0.0 collective-permute-start.15
  39.3 0.0 collective-permute-start.13
  39.3 0.5 collective-permute-start.18
  39.8 2.7 %collective-permute-start.14 = (bf16[16,8064]{1,0:T(8,128)(2,1)S(1)}, bf16[16,8064]{1,0:T(8,128)(2,1)S(1)}, u32[]{:S(2)}, u32[]{:S(2)}) collective-permute-start(bf16[16,8064]{1,0:T(8,128)(2,1)S(1)} %collective-permute-done.6.refs_7_), channel_id=1, source_target_pairs={{0,112},{8,120},{16,64},{24,72},{32,80},{40,88},{48,96},{56,104},{... | collective-permute-start | bytes 774152 | tf_op jit(solution)/shard_map/ppermute | solution.py:318
  42.5 0.0 collective-permute-done.16.refs_13_
  42.5 1.7 %collective-permute-start.12 = (bf16[16,8064]{1,0:T(8,128)(2,1)S(1)}, bf16[16,8064]{1,0:T(8,128)(2,1)S(1)}, u32[]{:S(2)}, u32[]{:S(2)}) collective-permute-start(bf16[16,8064]{1,0:T(8,128)(2,1)S(1)} %collective-permute-done.5.refs_6_), channel_id=1, source_target_pairs={{0,48},{8,56},{16,0},{24,8},{32,16},{40,24},{48,32},{56,40},{64,11... | collective-permute-start | bytes 774152 | tf_op jit(solution)/shard_map/ppermute | solution.py:318
  44.2 0.0 collective-permute-done.15.refs_12_
  44.2 0.0 collective-permute-start.11
  44.3 3.5 %collective-permute-done.13.refs_10_ = bf16[16,8064]{1,0:T(8,128)(2,1)S(1)} collective-permute-done((bf16[16,8064]{1,0:T(8,128)(2,1)S(1)}, bf16[16,8064]{1,0:T(8,128)(2,1)S(1)}, u32[]{:S(2)}, u32[]{:S(2)}) %collective-permute-start.13) | collective-permute-done | bytes 258080 | tf_op jit(solution)/shard_map/ppermute | solution.py:318
  47.8 1.9 %collective-permute-start.17 = (bf16[16,8064]{1,0:T(8,128)(2,1)S(1)}, bf16[16,8064]{1,0:T(8,128)(2,1)S(1)}, u32[]{:S(2)}, u32[]{:S(2)}) collective-permute-start(bf16[16,8064]{1,0:T(8,128)(2,1)S(1)} %collective-permute-done.5.refs_6_), channel_id=1, source_target_pairs={{0,8},{8,0},{16,24},{24,16},{32,40},{40,32},{48,56},{56,48},{64,72... | collective-permute-start | bytes 774152 | tf_op jit(solution)/shard_map/ppermute | solution.py:321
  49.6 0.0 collective-permute-done.18.refs_15_
  49.7 0.1 collective-permute-start.21
  49.7 0.3 collective-permute-done.14.refs_11_
  50.1 1.2 %collective-permute-start.22 = (bf16[16,8064]{1,0:T(8,128)(2,1)S(1)}, bf16[16,8064]{1,0:T(8,128)(2,1)S(1)}, u32[]{:S(2)}, u32[]{:S(2)}) collective-permute-start(bf16[16,8064]{1,0:T(8,128)(2,1)S(1)} %collective-permute-done.14.refs_11_), channel_id=1, source_target_pairs={{0,8},{8,0},{16,24},{24,16},{32,40},{40,32},{48,56},{56,48},{64,72... | collective-permute-start | bytes 774152 | tf_op jit(solution)/shard_map/ppermute | solution.py:321
  51.2 2.4 %collective-permute-done.12.refs_9_ = bf16[16,8064]{1,0:T(8,128)(2,1)S(1)} collective-permute-done((bf16[16,8064]{1,0:T(8,128)(2,1)S(1)}, bf16[16,8064]{1,0:T(8,128)(2,1)S(1)}, u32[]{:S(2)}, u32[]{:S(2)}) %collective-permute-start.12) | collective-permute-done | bytes 258080 | tf_op jit(solution)/shard_map/ppermute | solution.py:318
  53.7 0.8 collective-permute-start.20
  54.5 0.0 collective-permute-done.11.refs_8_
  54.5 0.2 collective-permute-start.19
  54.7 0.0 collective-permute-done.17.refs_14_
  54.7 2.7 %collective-permute-start.8 = (bf16[16,8064]{1,0:T(8,128)(2,1)S(1)}, bf16[16,8064]{1,0:T(8,128)(2,1)S(1)}, u32[]{:S(2)}, u32[]{:S(2)}) collective-permute-start(bf16[16,8064]{1,0:T(8,128)(2,1)S(1)} %collective-permute-done.refs_2_), channel_id=1, source_target_pairs={{0,3},{1,0},{2,1},{3,2},{4,7},{5,4},{6,5},{7,6},{8,11},{9,8},{10,9... | collective-permute-start | bytes 774152 | tf_op jit(solution)/shard_map/ppermute | solution.py:315
  57.4 0.0 collective-permute-done.21.refs_18_
  57.4 0.0 collective-permute-start.7
  57.4 0.1 collective-permute-start.9
  57.5 0.0 collective-permute-done.20.refs_17_
  57.5 3.4 %collective-permute-start.10 = (bf16[16,8064]{1,0:T(8,128)(2,1)S(1)}, bf16[16,8064]{1,0:T(8,128)(2,1)S(1)}, u32[]{:S(2)}, u32[]{:S(2)}) collective-permute-start(bf16[16,8064]{1,0:T(8,128)(2,1)S(1)} %collective-permute-done.3.refs_3_), channel_id=1, source_target_pairs={{0,7},{1,4},{2,5},{3,6},{4,3},{5,0},{6,1},{7,2},{8,15},{9,12},{10,... | collective-permute-start | bytes 774152 | tf_op jit(solution)/shard_map/ppermute | solution.py:315
  61.0 0.7 copy-done.13
  61.7 0.9 copy-done
  62.7 18.0 %shard_map.56.refs_21_ = bf16[101,128,256]{2,1,0:T(8,128)(2,1)} custom-call(bf16[16,8064]{1,0:T(8,128)(2,1)S(1)} %collective-permute-done.2.refs_0_, bf16[16,8064]{1,0:T(8,128)(2,1)S(1)} %copy-done, bf16[16,8064]{1,0:T(8,128)(2,1)S(1)} %collective-permute-done.refs_2_, bf16[16,8064]{1,0:T(8,128)(2,1)S(1)} %collective-permute-done.3.refs_3_, ...), custom_call_target="tpu_custom_call" | custom-call | flops 12800000000 | bytes 10000000 | tf_op jit(solution)/shard_map/pallas_call | solution.py:276
  80.7 0.0 collective-permute-done.8.refs_1_
  80.7 0.0 collective-permute-done.7.refs_0_
  80.7 18.3 %shard_map.57 = bf16[101,128,256]{2,1,0:T(8,128)(2,1)} custom-call(bf16[16,8064]{1,0:T(8,128)(2,1)S(1)} %collective-permute-done.7.refs_0_, bf16[16,8064]{1,0:T(8,128)(2,1)S(1)} %collective-permute-done.8.refs_1_, bf16[16,8064]{1,0:T(8,128)(2,1)S(1)} %collective-permute-done.9.refs_2_, ...), custom_call_target="tpu_custom_call", output_to_operand_aliasing={{}: (21, {})} | custom-call | flops 12800000000 | bytes 10000000 | tf_op jit(solution)/shard_map/pallas_call | solution.py:276
  (30 shorter events, 0.1 us)
Async XLA Ops:
  5.2 9.3 %collective-permute-start.1 = (bf16[16,8064]{1,0:T(8,128)(2,1)}, bf16[16,8064]{1,0:T(8,128)(2,1)S(1)}, u32[]{:S(2)}, u32[]{:S(2)}) collective-permute-start(bf16[16,8064]{1,0:T(8,128)(2,1)} %shard_map.55.refs_1_), channel_id=1, source_target_pairs={{2,0},{3,16},{0,32},{1,48},{6,64},{7,80},{4,96},{5,112},{10,8},{11... | collective-permute-start | bytes 774152 | tf_op jit(solution)/shard_map/ppermute | solution.py:326
  9.0 8.9 %collective-permute-start = (bf16[16,8064]{1,0:T(8,128)(2,1)}, bf16[16,8064]{1,0:T(8,128)(2,1)S(1)}, u32[]{:S(2)}, u32[]{:S(2)}) collective-permute-start(bf16[16,8064]{1,0:T(8,128)(2,1)} %shard_map.55.refs_1_), channel_id=1, source_target_pairs={{0,4},{1,5},{2,6},{3,7},{4,0},{5,1},{6,2},{7,3},{8,12},{9,13},{10,... | collective-permute-start | bytes 774152 | tf_op jit(solution)/shard_map/ppermute | solution.py:315
  17.8 10.8 %collective-permute-start.3 = (bf16[16,8064]{1,0:T(8,128)(2,1)}, bf16[16,8064]{1,0:T(8,128)(2,1)S(1)}, u32[]{:S(2)}, u32[]{:S(2)}) collective-permute-start(bf16[16,8064]{1,0:T(8,128)(2,1)} %shard_map.55.refs_1_), channel_id=1, source_target_pairs={{0,3},{1,0},{2,1},{3,2},{4,7},{5,4},{6,5},{7,6},{8,11},{9,8},{10,9... | collective-permute-start | bytes 774152 | tf_op jit(solution)/shard_map/ppermute | solution.py:315
  20.6 8.4 %collective-permute-start.2 = (bf16[16,8064]{1,0:T(8,128)(2,1)}, bf16[16,8064]{1,0:T(8,128)(2,1)S(1)}, u32[]{:S(2)}, u32[]{:S(2)}) collective-permute-start(bf16[16,8064]{1,0:T(8,128)(2,1)} %shard_map.55.refs_1_), channel_id=1, source_target_pairs={{0,1},{1,2},{2,3},{3,0},{4,5},{5,6},{6,7},{7,4},{8,9},{9,10},{10,1... | collective-permute-start | bytes 774152 | tf_op jit(solution)/shard_map/ppermute | solution.py:315
  21.0 8.3 %collective-permute-start.6 = (bf16[16,8064]{1,0:T(8,128)(2,1)S(1)}, bf16[16,8064]{1,0:T(8,128)(2,1)S(1)}, u32[]{:S(2)}, u32[]{:S(2)}) collective-permute-start(bf16[16,8064]{1,0:T(8,128)(2,1)S(1)} %collective-permute-done.1.refs_5_), channel_id=1, source_target_pairs={{0,48},{8,56},{16,0},{24,8},{32,16},{40,24},{48,32},{56,40},{64,11... | collective-permute-start | bytes 774152 | tf_op jit(solution)/shard_map/ppermute | solution.py:318
  24.6 8.1 %collective-permute-start.5 = (bf16[16,8064]{1,0:T(8,128)(2,1)S(1)}, bf16[16,8064]{1,0:T(8,128)(2,1)S(1)}, u32[]{:S(2)}, u32[]{:S(2)}) collective-permute-start(bf16[16,8064]{1,0:T(8,128)(2,1)S(1)} %collective-permute-done.1.refs_5_), channel_id=1, source_target_pairs={{0,64},{8,72},{16,80},{24,88},{32,96},{40,104},{48,112},{56,120},{... | collective-permute-start | bytes 774152 | tf_op jit(solution)/shard_map/ppermute | solution.py:318
  27.7 9.5 %collective-permute-start.4 = (bf16[16,8064]{1,0:T(8,128)(2,1)S(1)}, bf16[16,8064]{1,0:T(8,128)(2,1)S(1)}, u32[]{:S(2)}, u32[]{:S(2)}) collective-permute-start(bf16[16,8064]{1,0:T(8,128)(2,1)S(1)} %collective-permute-done.1.refs_5_), channel_id=1, source_target_pairs={{0,16},{8,24},{16,32},{24,40},{32,48},{40,56},{48,0},{56,8},{64,80... | collective-permute-start | bytes 774152 | tf_op jit(solution)/shard_map/ppermute | solution.py:318
  29.3 31.6 %copy-start.1 = (bf16[16,8064]{1,0:T(8,128)(2,1)}, bf16[16,8064]{1,0:T(8,128)(2,1)S(1)}, u32[]{:S(2)}) copy-start(bf16[16,8064]{1,0:T(8,128)(2,1)S(1)} %collective-permute-done.6.refs_7_) | copy-start | bytes 774148
  37.2 5.3 %collective-permute-start.16 = (bf16[16,8064]{1,0:T(8,128)(2,1)S(1)}, bf16[16,8064]{1,0:T(8,128)(2,1)S(1)}, u32[]{:S(2)}, u32[]{:S(2)}) collective-permute-start(bf16[16,8064]{1,0:T(8,128)(2,1)S(1)} %collective-permute-done.1.refs_5_), channel_id=1, source_target_pairs={{0,8},{8,0},{16,24},{24,16},{32,40},{40,32},{48,56},{56,48},{64,72... | collective-permute-start | bytes 774152 | tf_op jit(solution)/shard_map/ppermute | solution.py:321
  39.3 5.0 %collective-permute-start.15 = (bf16[16,8064]{1,0:T(8,128)(2,1)S(1)}, bf16[16,8064]{1,0:T(8,128)(2,1)S(1)}, u32[]{:S(2)}, u32[]{:S(2)}) collective-permute-start(bf16[16,8064]{1,0:T(8,128)(2,1)S(1)} %collective-permute-done.4.refs_4_), channel_id=1, source_target_pairs={{0,8},{8,0},{16,24},{24,16},{32,40},{40,32},{48,56},{56,48},{64,72... | collective-permute-start | bytes 774152 | tf_op jit(solution)/shard_map/ppermute | solution.py:321
  39.3 8.5 %collective-permute-start.13 = (bf16[16,8064]{1,0:T(8,128)(2,1)S(1)}, bf16[16,8064]{1,0:T(8,128)(2,1)S(1)}, u32[]{:S(2)}, u32[]{:S(2)}) collective-permute-start(bf16[16,8064]{1,0:T(8,128)(2,1)S(1)} %collective-permute-done.4.refs_4_), channel_id=1, source_target_pairs={{0,16},{8,24},{16,32},{24,40},{32,48},{40,56},{48,0},{56,8},{64,80... | collective-permute-start | bytes 774152 | tf_op jit(solution)/shard_map/ppermute | solution.py:318
  39.3 10.4 %collective-permute-start.18 = (bf16[16,8064]{1,0:T(8,128)(2,1)S(1)}, bf16[16,8064]{1,0:T(8,128)(2,1)S(1)}, u32[]{:S(2)}, u32[]{:S(2)}) collective-permute-start(bf16[16,8064]{1,0:T(8,128)(2,1)S(1)} %collective-permute-done.6.refs_7_), channel_id=1, source_target_pairs={{0,8},{8,0},{16,24},{24,16},{32,40},{40,32},{48,56},{56,48},{64,72... | collective-permute-start | bytes 774152 | tf_op jit(solution)/shard_map/ppermute | solution.py:321
  39.8 10.3 %collective-permute-start.14 = (bf16[16,8064]{1,0:T(8,128)(2,1)S(1)}, bf16[16,8064]{1,0:T(8,128)(2,1)S(1)}, u32[]{:S(2)}, u32[]{:S(2)}) collective-permute-start(bf16[16,8064]{1,0:T(8,128)(2,1)S(1)} %collective-permute-done.6.refs_7_), channel_id=1, source_target_pairs={{0,112},{8,120},{16,64},{24,72},{32,80},{40,88},{48,96},{56,104},{... | collective-permute-start | bytes 774152 | tf_op jit(solution)/shard_map/ppermute | solution.py:318
  42.5 18.4 %copy-start.2 = (bf16[16,8064]{1,0:T(8,128)(2,1)}, bf16[16,8064]{1,0:T(8,128)(2,1)S(1)}, u32[]{:S(2)}) copy-start(bf16[16,8064]{1,0:T(8,128)(2,1)S(1)} %collective-permute-done.16.refs_13_) | copy-start | bytes 774148
  42.5 11.2 %collective-permute-start.12 = (bf16[16,8064]{1,0:T(8,128)(2,1)S(1)}, bf16[16,8064]{1,0:T(8,128)(2,1)S(1)}, u32[]{:S(2)}, u32[]{:S(2)}) collective-permute-start(bf16[16,8064]{1,0:T(8,128)(2,1)S(1)} %collective-permute-done.5.refs_6_), channel_id=1, source_target_pairs={{0,48},{8,56},{16,0},{24,8},{32,16},{40,24},{48,32},{56,40},{64,11... | collective-permute-start | bytes 774152 | tf_op jit(solution)/shard_map/ppermute | solution.py:318
  44.2 16.7 %copy-start.3 = (bf16[16,8064]{1,0:T(8,128)(2,1)}, bf16[16,8064]{1,0:T(8,128)(2,1)S(1)}, u32[]{:S(2)}) copy-start(bf16[16,8064]{1,0:T(8,128)(2,1)S(1)} %collective-permute-done.15.refs_12_) | copy-start | bytes 774148
  44.2 10.2 %collective-permute-start.11 = (bf16[16,8064]{1,0:T(8,128)(2,1)S(1)}, bf16[16,8064]{1,0:T(8,128)(2,1)S(1)}, u32[]{:S(2)}, u32[]{:S(2)}) collective-permute-start(bf16[16,8064]{1,0:T(8,128)(2,1)S(1)} %collective-permute-done.5.refs_6_), channel_id=1, source_target_pairs={{0,16},{8,24},{16,32},{24,40},{32,48},{40,56},{48,0},{56,8},{64,80... | collective-permute-start | bytes 774152 | tf_op jit(solution)/shard_map/ppermute | solution.py:318
  47.8 13.2 %copy-start.4 = (bf16[16,8064]{1,0:T(8,128)(2,1)}, bf16[16,8064]{1,0:T(8,128)(2,1)S(1)}, u32[]{:S(2)}) copy-start(bf16[16,8064]{1,0:T(8,128)(2,1)S(1)} %collective-permute-done.13.refs_10_) | copy-start | bytes 774148
  47.8 6.9 %collective-permute-start.17 = (bf16[16,8064]{1,0:T(8,128)(2,1)S(1)}, bf16[16,8064]{1,0:T(8,128)(2,1)S(1)}, u32[]{:S(2)}, u32[]{:S(2)}) collective-permute-start(bf16[16,8064]{1,0:T(8,128)(2,1)S(1)} %collective-permute-done.5.refs_6_), channel_id=1, source_target_pairs={{0,8},{8,0},{16,24},{24,16},{32,40},{40,32},{48,56},{56,48},{64,72... | collective-permute-start | bytes 774152 | tf_op jit(solution)/shard_map/ppermute | solution.py:321
  49.7 11.3 %copy-start.5 = (bf16[16,8064]{1,0:T(8,128)(2,1)}, bf16[16,8064]{1,0:T(8,128)(2,1)S(1)}, u32[]{:S(2)}) copy-start(bf16[16,8064]{1,0:T(8,128)(2,1)S(1)} %collective-permute-done.18.refs_15_) | copy-start | bytes 774148
  49.7 7.7 %collective-permute-start.21 = (bf16[16,8064]{1,0:T(8,128)(2,1)S(1)}, bf16[16,8064]{1,0:T(8,128)(2,1)S(1)}, u32[]{:S(2)}, u32[]{:S(2)}) collective-permute-start(bf16[16,8064]{1,0:T(8,128)(2,1)S(1)} %collective-permute-done.13.refs_10_), channel_id=1, source_target_pairs={{0,8},{8,0},{16,24},{24,16},{32,40},{40,32},{48,56},{56,48},{64,72... | collective-permute-start | bytes 774152 | tf_op jit(solution)/shard_map/ppermute | solution.py:321
  50.1 10.9 %copy-start.6 = (bf16[16,8064]{1,0:T(8,128)(2,1)}, bf16[16,8064]{1,0:T(8,128)(2,1)S(1)}, u32[]{:S(2)}) copy-start(bf16[16,8064]{1,0:T(8,128)(2,1)S(1)} %collective-permute-done.14.refs_11_) | copy-start | bytes 774148
  50.1 7.3 %collective-permute-start.22 = (bf16[16,8064]{1,0:T(8,128)(2,1)S(1)}, bf16[16,8064]{1,0:T(8,128)(2,1)S(1)}, u32[]{:S(2)}, u32[]{:S(2)}) collective-permute-start(bf16[16,8064]{1,0:T(8,128)(2,1)S(1)} %collective-permute-done.14.refs_11_), channel_id=1, source_target_pairs={{0,8},{8,0},{16,24},{24,16},{32,40},{40,32},{48,56},{56,48},{64,72... | collective-permute-start | bytes 774152 | tf_op jit(solution)/shard_map/ppermute | solution.py:321
  53.7 7.3 %copy-start.7 = (bf16[16,8064]{1,0:T(8,128)(2,1)}, bf16[16,8064]{1,0:T(8,128)(2,1)S(1)}, u32[]{:S(2)}) copy-start(bf16[16,8064]{1,0:T(8,128)(2,1)S(1)} %collective-permute-done.12.refs_9_) | copy-start | bytes 774148
  53.7 3.8 %collective-permute-start.20 = (bf16[16,8064]{1,0:T(8,128)(2,1)S(1)}, bf16[16,8064]{1,0:T(8,128)(2,1)S(1)}, u32[]{:S(2)}, u32[]{:S(2)}) collective-permute-start(bf16[16,8064]{1,0:T(8,128)(2,1)S(1)} %collective-permute-done.12.refs_9_), channel_id=1, source_target_pairs={{0,8},{8,0},{16,24},{24,16},{32,40},{40,32},{48,56},{56,48},{64,72... | collective-permute-start | bytes 774152 | tf_op jit(solution)/shard_map/ppermute | solution.py:321
  54.5 6.5 %copy-start.8 = (bf16[16,8064]{1,0:T(8,128)(2,1)}, bf16[16,8064]{1,0:T(8,128)(2,1)S(1)}, u32[]{:S(2)}) copy-start(bf16[16,8064]{1,0:T(8,128)(2,1)S(1)} %collective-permute-done.11.refs_8_) | copy-start | bytes 774148
  54.5 6.4 %collective-permute-start.19 = (bf16[16,8064]{1,0:T(8,128)(2,1)S(1)}, bf16[16,8064]{1,0:T(8,128)(2,1)S(1)}, u32[]{:S(2)}, u32[]{:S(2)}) collective-permute-start(bf16[16,8064]{1,0:T(8,128)(2,1)S(1)} %collective-permute-done.11.refs_8_), channel_id=1, source_target_pairs={{0,8},{8,0},{16,24},{24,16},{32,40},{40,32},{48,56},{56,48},{64,72... | collective-permute-start | bytes 774152 | tf_op jit(solution)/shard_map/ppermute | solution.py:321
  54.7 6.3 %copy-start.9 = (bf16[16,8064]{1,0:T(8,128)(2,1)}, bf16[16,8064]{1,0:T(8,128)(2,1)S(1)}, u32[]{:S(2)}) copy-start(bf16[16,8064]{1,0:T(8,128)(2,1)S(1)} %collective-permute-done.17.refs_14_) | copy-start | bytes 774148
  54.7 26.0 %collective-permute-start.8 = (bf16[16,8064]{1,0:T(8,128)(2,1)S(1)}, bf16[16,8064]{1,0:T(8,128)(2,1)S(1)}, u32[]{:S(2)}, u32[]{:S(2)}) collective-permute-start(bf16[16,8064]{1,0:T(8,128)(2,1)S(1)} %collective-permute-done.refs_2_), channel_id=1, source_target_pairs={{0,3},{1,0},{2,1},{3,2},{4,7},{5,4},{6,5},{7,6},{8,11},{9,8},{10,9... | collective-permute-start | bytes 774152 | tf_op jit(solution)/shard_map/ppermute | solution.py:315
  57.4 3.6 %copy-start.10 = (bf16[16,8064]{1,0:T(8,128)(2,1)}, bf16[16,8064]{1,0:T(8,128)(2,1)S(1)}, u32[]{:S(2)}) copy-start(bf16[16,8064]{1,0:T(8,128)(2,1)S(1)} %collective-permute-done.21.refs_18_) | copy-start | bytes 774148
  57.4 23.3 %collective-permute-start.7 = (bf16[16,8064]{1,0:T(8,128)(2,1)S(1)}, bf16[16,8064]{1,0:T(8,128)(2,1)S(1)}, u32[]{:S(2)}, u32[]{:S(2)}) collective-permute-start(bf16[16,8064]{1,0:T(8,128)(2,1)S(1)} %collective-permute-done.refs_2_), channel_id=1, source_target_pairs={{0,1},{1,2},{2,3},{3,0},{4,5},{5,6},{6,7},{7,4},{8,9},{9,10},{10,1... | collective-permute-start | bytes 774152 | tf_op jit(solution)/shard_map/ppermute | solution.py:315
  57.4 3.6 %copy-start.11 = (bf16[16,8064]{1,0:T(8,128)(2,1)}, bf16[16,8064]{1,0:T(8,128)(2,1)S(1)}, u32[]{:S(2)}) copy-start(bf16[16,8064]{1,0:T(8,128)(2,1)S(1)} %collective-permute-done.22.refs_19_) | copy-start | bytes 774148
  57.4 23.3 %collective-permute-start.9 = (bf16[16,8064]{1,0:T(8,128)(2,1)S(1)}, bf16[16,8064]{1,0:T(8,128)(2,1)S(1)}, u32[]{:S(2)}, u32[]{:S(2)}) collective-permute-start(bf16[16,8064]{1,0:T(8,128)(2,1)S(1)} %collective-permute-done.2.refs_0_), channel_id=1, source_target_pairs={{0,1},{1,2},{2,3},{3,0},{4,5},{5,6},{6,7},{7,4},{8,9},{9,10},{10,1... | collective-permute-start | bytes 774152 | tf_op jit(solution)/shard_map/ppermute | solution.py:315
  57.5 3.5 %copy-start.12 = (bf16[16,8064]{1,0:T(8,128)(2,1)}, bf16[16,8064]{1,0:T(8,128)(2,1)S(1)}, u32[]{:S(2)}) copy-start(bf16[16,8064]{1,0:T(8,128)(2,1)S(1)} %collective-permute-done.20.refs_17_) | copy-start | bytes 774148
  57.5 23.2 %collective-permute-start.10 = (bf16[16,8064]{1,0:T(8,128)(2,1)S(1)}, bf16[16,8064]{1,0:T(8,128)(2,1)S(1)}, u32[]{:S(2)}, u32[]{:S(2)}) collective-permute-start(bf16[16,8064]{1,0:T(8,128)(2,1)S(1)} %collective-permute-done.3.refs_3_), channel_id=1, source_target_pairs={{0,7},{1,4},{2,5},{3,6},{4,3},{5,0},{6,1},{7,2},{8,15},{9,12},{10,... | collective-permute-start | bytes 774152 | tf_op jit(solution)/shard_map/ppermute | solution.py:315
  61.0 0.7 copy-start.13
  61.7 0.9 copy-start

commit v9 on v8

--- a/solution.py
+++ b/solution.py
@@ -290,7 +290,7 @@
             pltpu.SemaphoreType.DMA((2,)),
             pltpu.SemaphoreType.DMA((len(col_blocks) + 1,)),
         ],
-        compiler_params=pltpu.CompilerParams(vmem_limit_bytes=52 * 1024 * 1024),
+        compiler_params=pltpu.CompilerParams(vmem_limit_bytes=50 * 1024 * 1024),
         cost_estimate=pl.CostEstimate(flops=n * 2 * 10**8, bytes_accessed=10**7, transcendentals=0),
     )(*inputs)
 

time: 99.8 us -> 104 us (1.042)
  Pallas kernels: 39.6 us -> 44.2 us
    pallas_call x2, Pallas kernels: 36.2 us -> 40.8 us  [correlate(): pl.pallas_call(functools.partial(correlate_kernel, tuple(rows), tuple(col...]
    unnamed x29 -> x11, local copies, waits for them, and re-layouts: 3.53 us -> 3.5 us
  transfers between devices with their start and end apart: 23 -> 23, of which waited for: 9 -> 9; matrix products, arithmetic and copies ran while one was open for 0% -> 0% of each run, Pallas kernels for 18% -> 20%
where the time goes in v9:
time: 104 us
  Pallas kernels  44.2 us (42%)
  starting transfers between devices  34.8 us (33%)
  waiting for transfers between devices  20.8 us (20%)
  local copies, waits for them, and re-layouts  3.5 us (3%)
    pallas_call x2, Pallas kernels, correlate(): pl.pallas_call(functools.partial(correlate_kernel, tuple(rows), tuple(col...  40.8 us
    ppermute x7, waiting for transfers between devices, over_src(): lax.ppermute(value, 'src', [(i, 2 * step(i // 2, ring, side) + i % 2) for...  14.5 us
    ppermute x7, starting transfers between devices, over_rcv(): lax.ppermute(value, 'rcv', [(i, step(i, ring, side)) for i in range(8)])  12.3 us
    ppermute x7, starting transfers between devices, over_src(): lax.ppermute(value, 'src', [(i, 2 * step(i // 2, ring, side) + i % 2) for...  12.1 us
    ppermute x8, starting transfers between devices, other_core(): return lax.ppermute(value, 'src', [(i, i ^ 1) for i in range(16)])  6.64 us
    ppermute x1, starting transfers between devices, body(): turned = lax.ppermute(white, ('src', 'rcv'), flip)  3.74 us
    ppermute x7, waiting for transfers between devices, over_rcv(): lax.ppermute(value, 'rcv', [(i, step(i, ring, side)) for i in range(8)])  3.72 us
    unnamed x11, local copies, waits for them, and re-layouts  3.5 us
  transfers between devices with their start and end apart: 23, of which 9 were waited for; matrix products, arithmetic and copies ran while one was open for 0% of the time, Pallas kernels for 20%

profile of v9, /device:TPU:1, one launch (start us, length us, event | category | flops | bytes accessed | tf_op | source)
XLA Modules:
  0.0 103.6 jit_solution(4010602277782228529)
XLA Ops:
  0.0 1.8 %copy.7.spectra_ref = bf16[16,2,10,400]{3,2,1,0:T(8,128)(2,1)} copy(bf16[16,2,10,400]{3,1,2,0:T(2,128)(2,1)} %param.5) | data formatting | bytes 512000 | tf_op args[0]
  1.8 3.4 %shard_map.55.refs_1_ = bf16[16,8064]{1,0:T(8,128)(2,1)} custom-call(s32[16]{0:T(128)} %mask_ref.1, bf16[16,2,10,400]{3,2,1,0:T(8,128)(2,1)} %copy.7.spectra_ref, s32[16,10]{1,0:T(8,128)} %offsets_ref.1), custom_call_target="tpu_custom_call" | custom-call | tf_op jit(solution)/shard_map/pallas_call | solution.py:89
  5.2 3.7 %collective-permute-start.1 = (bf16[16,8064]{1,0:T(8,128)(2,1)}, bf16[16,8064]{1,0:T(8,128)(2,1)S(1)}, u32[]{:S(2)}, u32[]{:S(2)}) collective-permute-start(bf16[16,8064]{1,0:T(8,128)(2,1)} %shard_map.55.refs_1_), channel_id=1, source_target_pairs={{2,0},{3,16},{0,32},{1,48},{6,64},{7,80},{4,96},{5,112},{10,8},{11... | collective-permute-start | bytes 774152 | tf_op jit(solution)/shard_map/ppermute | solution.py:326
  9.0 3.0 %collective-permute-start = (bf16[16,8064]{1,0:T(8,128)(2,1)}, bf16[16,8064]{1,0:T(8,128)(2,1)S(1)}, u32[]{:S(2)}, u32[]{:S(2)}) collective-permute-start(bf16[16,8064]{1,0:T(8,128)(2,1)} %shard_map.55.refs_1_), channel_id=1, source_target_pairs={{0,4},{1,5},{2,6},{3,7},{4,0},{5,1},{6,2},{7,3},{8,12},{9,13},{10,... | collective-permute-start | bytes 774152 | tf_op jit(solution)/shard_map/ppermute | solution.py:315
  12.0 2.5 %collective-permute-done.1.refs_5_ = bf16[16,8064]{1,0:T(8,128)(2,1)S(1)} collective-permute-done((bf16[16,8064]{1,0:T(8,128)(2,1)}, bf16[16,8064]{1,0:T(8,128)(2,1)S(1)}, u32[]{:S(2)}, u32[]{:S(2)}) %collective-permute-start.1) | collective-permute-done | bytes 258080 | tf_op jit(solution)/shard_map/ppermute | solution.py:326
  14.5 3.3 %collective-permute-done.refs_2_ = bf16[16,8064]{1,0:T(8,128)(2,1)S(1)} collective-permute-done((bf16[16,8064]{1,0:T(8,128)(2,1)}, bf16[16,8064]{1,0:T(8,128)(2,1)S(1)}, u32[]{:S(2)}, u32[]{:S(2)}) %collective-permute-start) | collective-permute-done | bytes 258080 | tf_op jit(solution)/shard_map/ppermute | solution.py:315
  17.8 2.8 %collective-permute-start.3 = (bf16[16,8064]{1,0:T(8,128)(2,1)}, bf16[16,8064]{1,0:T(8,128)(2,1)S(1)}, u32[]{:S(2)}, u32[]{:S(2)}) collective-permute-start(bf16[16,8064]{1,0:T(8,128)(2,1)} %shard_map.55.refs_1_), channel_id=1, source_target_pairs={{0,3},{1,0},{2,1},{3,2},{4,7},{5,4},{6,5},{7,6},{8,11},{9,8},{10,9... | collective-permute-start | bytes 774152 | tf_op jit(solution)/shard_map/ppermute | solution.py:315
  20.6 0.4 collective-permute-start.2
  21.0 3.6 %collective-permute-start.6 = (bf16[16,8064]{1,0:T(8,128)(2,1)S(1)}, bf16[16,8064]{1,0:T(8,128)(2,1)S(1)}, u32[]{:S(2)}, u32[]{:S(2)}) collective-permute-start(bf16[16,8064]{1,0:T(8,128)(2,1)S(1)} %collective-permute-done.1.refs_5_), channel_id=1, source_target_pairs={{0,48},{8,56},{16,0},{24,8},{32,16},{40,24},{48,32},{56,40},{64,11... | collective-permute-start | bytes 774152 | tf_op jit(solution)/shard_map/ppermute | solution.py:318
  24.6 3.1 %collective-permute-start.5 = (bf16[16,8064]{1,0:T(8,128)(2,1)S(1)}, bf16[16,8064]{1,0:T(8,128)(2,1)S(1)}, u32[]{:S(2)}, u32[]{:S(2)}) collective-permute-start(bf16[16,8064]{1,0:T(8,128)(2,1)S(1)} %collective-permute-done.1.refs_5_), channel_id=1, source_target_pairs={{0,64},{8,72},{16,80},{24,88},{32,96},{40,104},{48,112},{56,120},{... | collective-permute-start | bytes 774152 | tf_op jit(solution)/shard_map/ppermute | solution.py:318
  27.7 0.9 collective-permute-start.4
  28.7 0.0 collective-permute-done.3.refs_3_
  28.7 0.4 collective-permute-done.2.refs_0_
  29.0 0.3 collective-permute-done.6.refs_7_
  29.3 3.4 %collective-permute-done.5.refs_6_ = bf16[16,8064]{1,0:T(8,128)(2,1)S(1)} collective-permute-done((bf16[16,8064]{1,0:T(8,128)(2,1)S(1)}, bf16[16,8064]{1,0:T(8,128)(2,1)S(1)}, u32[]{:S(2)}, u32[]{:S(2)}) %collective-permute-start.5) | collective-permute-done | bytes 258080 | tf_op jit(solution)/shard_map/ppermute | solution.py:318
  32.7 4.5 %collective-permute-done.4.refs_4_ = bf16[16,8064]{1,0:T(8,128)(2,1)S(1)} collective-permute-done((bf16[16,8064]{1,0:T(8,128)(2,1)S(1)}, bf16[16,8064]{1,0:T(8,128)(2,1)S(1)}, u32[]{:S(2)}, u32[]{:S(2)}) %collective-permute-start.4) | collective-permute-done | bytes 258080 | tf_op jit(solution)/shard_map/ppermute | solution.py:318
  37.2 2.1 %collective-permute-start.16 = (bf16[16,8064]{1,0:T(8,128)(2,1)S(1)}, bf16[16,8064]{1,0:T(8,128)(2,1)S(1)}, u32[]{:S(2)}, u32[]{:S(2)}) collective-permute-start(bf16[16,8064]{1,0:T(8,128)(2,1)S(1)} %collective-permute-done.1.refs_5_), channel_id=1, source_target_pairs={{0,8},{8,0},{16,24},{24,16},{32,40},{40,32},{48,56},{56,48},{64,72... | collective-permute-start | bytes 774152 | tf_op jit(solution)/shard_map/ppermute | solution.py:321
  39.3 0.0 collective-permute-start.15
  39.3 0.0 collective-permute-start.13
  39.3 0.5 collective-permute-start.18
  39.8 2.7 %collective-permute-start.14 = (bf16[16,8064]{1,0:T(8,128)(2,1)S(1)}, bf16[16,8064]{1,0:T(8,128)(2,1)S(1)}, u32[]{:S(2)}, u32[]{:S(2)}) collective-permute-start(bf16[16,8064]{1,0:T(8,128)(2,1)S(1)} %collective-permute-done.6.refs_7_), channel_id=1, source_target_pairs={{0,112},{8,120},{16,64},{24,72},{32,80},{40,88},{48,96},{56,104},{... | collective-permute-start | bytes 774152 | tf_op jit(solution)/shard_map/ppermute | solution.py:318
  42.5 0.0 collective-permute-done.16.refs_13_
  42.5 1.7 %collective-permute-start.12 = (bf16[16,8064]{1,0:T(8,128)(2,1)S(1)}, bf16[16,8064]{1,0:T(8,128)(2,1)S(1)}, u32[]{:S(2)}, u32[]{:S(2)}) collective-permute-start(bf16[16,8064]{1,0:T(8,128)(2,1)S(1)} %collective-permute-done.5.refs_6_), channel_id=1, source_target_pairs={{0,48},{8,56},{16,0},{24,8},{32,16},{40,24},{48,32},{56,40},{64,11... | collective-permute-start | bytes 774152 | tf_op jit(solution)/shard_map/ppermute | solution.py:318
  44.2 0.0 collective-permute-done.15.refs_12_
  44.2 0.0 collective-permute-start.11
  44.3 3.5 %collective-permute-done.13.refs_10_ = bf16[16,8064]{1,0:T(8,128)(2,1)S(1)} collective-permute-done((bf16[16,8064]{1,0:T(8,128)(2,1)S(1)}, bf16[16,8064]{1,0:T(8,128)(2,1)S(1)}, u32[]{:S(2)}, u32[]{:S(2)}) %collective-permute-start.13) | collective-permute-done | bytes 258080 | tf_op jit(solution)/shard_map/ppermute | solution.py:318
  47.8 1.9 %collective-permute-start.17 = (bf16[16,8064]{1,0:T(8,128)(2,1)S(1)}, bf16[16,8064]{1,0:T(8,128)(2,1)S(1)}, u32[]{:S(2)}, u32[]{:S(2)}) collective-permute-start(bf16[16,8064]{1,0:T(8,128)(2,1)S(1)} %collective-permute-done.5.refs_6_), channel_id=1, source_target_pairs={{0,8},{8,0},{16,24},{24,16},{32,40},{40,32},{48,56},{56,48},{64,72... | collective-permute-start | bytes 774152 | tf_op jit(solution)/shard_map/ppermute | solution.py:321
  49.7 0.0 collective-permute-done.18.refs_15_
  49.7 0.0 collective-permute-start.21
  49.7 0.4 collective-permute-done.14.refs_11_
  50.1 1.2 %collective-permute-start.22 = (bf16[16,8064]{1,0:T(8,128)(2,1)S(1)}, bf16[16,8064]{1,0:T(8,128)(2,1)S(1)}, u32[]{:S(2)}, u32[]{:S(2)}) collective-permute-start(bf16[16,8064]{1,0:T(8,128)(2,1)S(1)} %collective-permute-done.14.refs_11_), channel_id=1, source_target_pairs={{0,8},{8,0},{16,24},{24,16},{32,40},{40,32},{48,56},{56,48},{64,72... | collective-permute-start | bytes 774152 | tf_op jit(solution)/shard_map/ppermute | solution.py:321
  51.2 2.4 %collective-permute-done.12.refs_9_ = bf16[16,8064]{1,0:T(8,128)(2,1)S(1)} collective-permute-done((bf16[16,8064]{1,0:T(8,128)(2,1)S(1)}, bf16[16,8064]{1,0:T(8,128)(2,1)S(1)}, u32[]{:S(2)}, u32[]{:S(2)}) %collective-permute-start.12) | collective-permute-done | bytes 258080 | tf_op jit(solution)/shard_map/ppermute | solution.py:318
  53.7 0.8 collective-permute-start.20
  54.5 0.0 collective-permute-done.11.refs_8_
  54.5 0.2 collective-permute-start.19
  54.7 0.0 collective-permute-done.17.refs_14_
  54.7 2.7 %collective-permute-start.8 = (bf16[16,8064]{1,0:T(8,128)(2,1)S(1)}, bf16[16,8064]{1,0:T(8,128)(2,1)S(1)}, u32[]{:S(2)}, u32[]{:S(2)}) collective-permute-start(bf16[16,8064]{1,0:T(8,128)(2,1)S(1)} %collective-permute-done.refs_2_), channel_id=1, source_target_pairs={{0,3},{1,0},{2,1},{3,2},{4,7},{5,4},{6,5},{7,6},{8,11},{9,8},{10,9... | collective-permute-start | bytes 774152 | tf_op jit(solution)/shard_map/ppermute | solution.py:315
  57.4 0.0 collective-permute-done.21.refs_18_
  57.4 0.0 collective-permute-start.7
  57.4 0.1 collective-permute-start.9
  57.5 3.4 %collective-permute-start.10 = (bf16[16,8064]{1,0:T(8,128)(2,1)S(1)}, bf16[16,8064]{1,0:T(8,128)(2,1)S(1)}, u32[]{:S(2)}, u32[]{:S(2)}) collective-permute-start(bf16[16,8064]{1,0:T(8,128)(2,1)S(1)} %collective-permute-done.3.refs_3_), channel_id=1, source_target_pairs={{0,7},{1,4},{2,5},{3,6},{4,3},{5,0},{6,1},{7,2},{8,15},{9,12},{10,... | collective-permute-start | bytes 774152 | tf_op jit(solution)/shard_map/ppermute | solution.py:315
  60.9 0.7 copy-done.4
  61.6 0.9 copy-done
  62.6 20.3 %shard_map.56.refs_21_ = bf16[101,128,256]{2,1,0:T(8,128)(2,1)} custom-call(bf16[16,8064]{1,0:T(8,128)(2,1)S(1)} %collective-permute-done.2.refs_0_, bf16[16,8064]{1,0:T(8,128)(2,1)S(1)} %copy-done, bf16[16,8064]{1,0:T(8,128)(2,1)S(1)} %collective-permute-done.refs_2_, bf16[16,8064]{1,0:T(8,128)(2,1)S(1)} %collective-permute-done.3.refs_3_, ...), custom_call_target="tpu_custom_call" | custom-call | flops 12800000000 | bytes 10000000 | tf_op jit(solution)/shard_map/pallas_call | solution.py:276
  82.8 0.0 collective-permute-done.9.refs_2_
  82.8 0.0 collective-permute-done.8.refs_1_
  82.9 0.0 collective-permute-done.7.refs_0_
  82.9 20.6 %shard_map.57 = bf16[101,128,256]{2,1,0:T(8,128)(2,1)} custom-call(bf16[16,8064]{1,0:T(8,128)(2,1)S(1)} %collective-permute-done.7.refs_0_, bf16[16,8064]{1,0:T(8,128)(2,1)S(1)} %collective-permute-done.8.refs_1_, bf16[16,8064]{1,0:T(8,128)(2,1)S(1)} %collective-permute-done.9.refs_2_, ...), custom_call_target="tpu_custom_call", output_to_operand_aliasing={{}: (21, {})} | custom-call | flops 12800000000 | bytes 10000000 | tf_op jit(solution)/shard_map/pallas_call | solution.py:276
  (12 shorter events, 0.0 us)
Async XLA Ops:
  5.2 9.3 %collective-permute-start.1 = (bf16[16,8064]{1,0:T(8,128)(2,1)}, bf16[16,8064]{1,0:T(8,128)(2,1)S(1)}, u32[]{:S(2)}, u32[]{:S(2)}) collective-permute-start(bf16[16,8064]{1,0:T(8,128)(2,1)} %shard_map.55.refs_1_), channel_id=1, source_target_pairs={{2,0},{3,16},{0,32},{1,48},{6,64},{7,80},{4,96},{5,112},{10,8},{11... | collective-permute-start | bytes 774152 | tf_op jit(solution)/shard_map/ppermute | solution.py:326
  9.0 8.9 %collective-permute-start = (bf16[16,8064]{1,0:T(8,128)(2,1)}, bf16[16,8064]{1,0:T(8,128)(2,1)S(1)}, u32[]{:S(2)}, u32[]{:S(2)}) collective-permute-start(bf16[16,8064]{1,0:T(8,128)(2,1)} %shard_map.55.refs_1_), channel_id=1, source_target_pairs={{0,4},{1,5},{2,6},{3,7},{4,0},{5,1},{6,2},{7,3},{8,12},{9,13},{10,... | collective-permute-start | bytes 774152 | tf_op jit(solution)/shard_map/ppermute | solution.py:315
  17.8 10.8 %collective-permute-start.3 = (bf16[16,8064]{1,0:T(8,128)(2,1)}, bf16[16,8064]{1,0:T(8,128)(2,1)S(1)}, u32[]{:S(2)}, u32[]{:S(2)}) collective-permute-start(bf16[16,8064]{1,0:T(8,128)(2,1)} %shard_map.55.refs_1_), channel_id=1, source_target_pairs={{0,3},{1,0},{2,1},{3,2},{4,7},{5,4},{6,5},{7,6},{8,11},{9,8},{10,9... | collective-permute-start | bytes 774152 | tf_op jit(solution)/shard_map/ppermute | solution.py:315
  20.6 8.4 %collective-permute-start.2 = (bf16[16,8064]{1,0:T(8,128)(2,1)}, bf16[16,8064]{1,0:T(8,128)(2,1)S(1)}, u32[]{:S(2)}, u32[]{:S(2)}) collective-permute-start(bf16[16,8064]{1,0:T(8,128)(2,1)} %shard_map.55.refs_1_), channel_id=1, source_target_pairs={{0,1},{1,2},{2,3},{3,0},{4,5},{5,6},{6,7},{7,4},{8,9},{9,10},{10,1... | collective-permute-start | bytes 774152 | tf_op jit(solution)/shard_map/ppermute | solution.py:315
  21.0 8.3 %collective-permute-start.6 = (bf16[16,8064]{1,0:T(8,128)(2,1)S(1)}, bf16[16,8064]{1,0:T(8,128)(2,1)S(1)}, u32[]{:S(2)}, u32[]{:S(2)}) collective-permute-start(bf16[16,8064]{1,0:T(8,128)(2,1)S(1)} %collective-permute-done.1.refs_5_), channel_id=1, source_target_pairs={{0,48},{8,56},{16,0},{24,8},{32,16},{40,24},{48,32},{56,40},{64,11... | collective-permute-start | bytes 774152 | tf_op jit(solution)/shard_map/ppermute | solution.py:318
  24.6 8.1 %collective-permute-start.5 = (bf16[16,8064]{1,0:T(8,128)(2,1)S(1)}, bf16[16,8064]{1,0:T(8,128)(2,1)S(1)}, u32[]{:S(2)}, u32[]{:S(2)}) collective-permute-start(bf16[16,8064]{1,0:T(8,128)(2,1)S(1)} %collective-permute-done.1.refs_5_), channel_id=1, source_target_pairs={{0,64},{8,72},{16,80},{24,88},{32,96},{40,104},{48,112},{56,120},{... | collective-permute-start | bytes 774152 | tf_op jit(solution)/shard_map/ppermute | solution.py:318
  27.7 9.5 %collective-permute-start.4 = (bf16[16,8064]{1,0:T(8,128)(2,1)S(1)}, bf16[16,8064]{1,0:T(8,128)(2,1)S(1)}, u32[]{:S(2)}, u32[]{:S(2)}) collective-permute-start(bf16[16,8064]{1,0:T(8,128)(2,1)S(1)} %collective-permute-done.1.refs_5_), channel_id=1, source_target_pairs={{0,16},{8,24},{16,32},{24,40},{32,48},{40,56},{48,0},{56,8},{64,80... | collective-permute-start | bytes 774152 | tf_op jit(solution)/shard_map/ppermute | solution.py:318
  37.2 5.3 %collective-permute-start.16 = (bf16[16,8064]{1,0:T(8,128)(2,1)S(1)}, bf16[16,8064]{1,0:T(8,128)(2,1)S(1)}, u32[]{:S(2)}, u32[]{:S(2)}) collective-permute-start(bf16[16,8064]{1,0:T(8,128)(2,1)S(1)} %collective-permute-done.1.refs_5_), channel_id=1, source_target_pairs={{0,8},{8,0},{16,24},{24,16},{32,40},{40,32},{48,56},{56,48},{64,72... | collective-permute-start | bytes 774152 | tf_op jit(solution)/shard_map/ppermute | solution.py:321
  39.3 5.0 %collective-permute-start.15 = (bf16[16,8064]{1,0:T(8,128)(2,1)S(1)}, bf16[16,8064]{1,0:T(8,128)(2,1)S(1)}, u32[]{:S(2)}, u32[]{:S(2)}) collective-permute-start(bf16[16,8064]{1,0:T(8,128)(2,1)S(1)} %collective-permute-done.4.refs_4_), channel_id=1, source_target_pairs={{0,8},{8,0},{16,24},{24,16},{32,40},{40,32},{48,56},{56,48},{64,72... | collective-permute-start | bytes 774152 | tf_op jit(solution)/shard_map/ppermute | solution.py:321
  39.3 8.5 %collective-permute-start.13 = (bf16[16,8064]{1,0:T(8,128)(2,1)S(1)}, bf16[16,8064]{1,0:T(8,128)(2,1)S(1)}, u32[]{:S(2)}, u32[]{:S(2)}) collective-permute-start(bf16[16,8064]{1,0:T(8,128)(2,1)S(1)} %collective-permute-done.4.refs_4_), channel_id=1, source_target_pairs={{0,16},{8,24},{16,32},{24,40},{32,48},{40,56},{48,0},{56,8},{64,80... | collective-permute-start | bytes 774152 | tf_op jit(solution)/shard_map/ppermute | solution.py:318
  39.3 10.4 %collective-permute-start.18 = (bf16[16,8064]{1,0:T(8,128)(2,1)S(1)}, bf16[16,8064]{1,0:T(8,128)(2,1)S(1)}, u32[]{:S(2)}, u32[]{:S(2)}) collective-permute-start(bf16[16,8064]{1,0:T(8,128)(2,1)S(1)} %collective-permute-done.6.refs_7_), channel_id=1, source_target_pairs={{0,8},{8,0},{16,24},{24,16},{32,40},{40,32},{48,56},{56,48},{64,72... | collective-permute-start | bytes 774152 | tf_op jit(solution)/shard_map/ppermute | solution.py:321
  39.8 10.3 %collective-permute-start.14 = (bf16[16,8064]{1,0:T(8,128)(2,1)S(1)}, bf16[16,8064]{1,0:T(8,128)(2,1)S(1)}, u32[]{:S(2)}, u32[]{:S(2)}) collective-permute-start(bf16[16,8064]{1,0:T(8,128)(2,1)S(1)} %collective-permute-done.6.refs_7_), channel_id=1, source_target_pairs={{0,112},{8,120},{16,64},{24,72},{32,80},{40,88},{48,96},{56,104},{... | collective-permute-start | bytes 774152 | tf_op jit(solution)/shard_map/ppermute | solution.py:318
  42.5 11.2 %collective-permute-start.12 = (bf16[16,8064]{1,0:T(8,128)(2,1)S(1)}, bf16[16,8064]{1,0:T(8,128)(2,1)S(1)}, u32[]{:S(2)}, u32[]{:S(2)}) collective-permute-start(bf16[16,8064]{1,0:T(8,128)(2,1)S(1)} %collective-permute-done.5.refs_6_), channel_id=1, source_target_pairs={{0,48},{8,56},{16,0},{24,8},{32,16},{40,24},{48,32},{56,40},{64,11... | collective-permute-start | bytes 774152 | tf_op jit(solution)/shard_map/ppermute | solution.py:318
  44.2 10.2 %collective-permute-start.11 = (bf16[16,8064]{1,0:T(8,128)(2,1)S(1)}, bf16[16,8064]{1,0:T(8,128)(2,1)S(1)}, u32[]{:S(2)}, u32[]{:S(2)}) collective-permute-start(bf16[16,8064]{1,0:T(8,128)(2,1)S(1)} %collective-permute-done.5.refs_6_), channel_id=1, source_target_pairs={{0,16},{8,24},{16,32},{24,40},{32,48},{40,56},{48,0},{56,8},{64,80... | collective-permute-start | bytes 774152 | tf_op jit(solution)/shard_map/ppermute | solution.py:318
  47.8 6.9 %collective-permute-start.17 = (bf16[16,8064]{1,0:T(8,128)(2,1)S(1)}, bf16[16,8064]{1,0:T(8,128)(2,1)S(1)}, u32[]{:S(2)}, u32[]{:S(2)}) collective-permute-start(bf16[16,8064]{1,0:T(8,128)(2,1)S(1)} %collective-permute-done.5.refs_6_), channel_id=1, source_target_pairs={{0,8},{8,0},{16,24},{24,16},{32,40},{40,32},{48,56},{56,48},{64,72... | collective-permute-start | bytes 774152 | tf_op jit(solution)/shard_map/ppermute | solution.py:321
  49.7 7.7 %collective-permute-start.21 = (bf16[16,8064]{1,0:T(8,128)(2,1)S(1)}, bf16[16,8064]{1,0:T(8,128)(2,1)S(1)}, u32[]{:S(2)}, u32[]{:S(2)}) collective-permute-start(bf16[16,8064]{1,0:T(8,128)(2,1)S(1)} %collective-permute-done.13.refs_10_), channel_id=1, source_target_pairs={{0,8},{8,0},{16,24},{24,16},{32,40},{40,32},{48,56},{56,48},{64,72... | collective-permute-start | bytes 774152 | tf_op jit(solution)/shard_map/ppermute | solution.py:321
  50.1 7.3 %collective-permute-start.22 = (bf16[16,8064]{1,0:T(8,128)(2,1)S(1)}, bf16[16,8064]{1,0:T(8,128)(2,1)S(1)}, u32[]{:S(2)}, u32[]{:S(2)}) collective-permute-start(bf16[16,8064]{1,0:T(8,128)(2,1)S(1)} %collective-permute-done.14.refs_11_), channel_id=1, source_target_pairs={{0,8},{8,0},{16,24},{24,16},{32,40},{40,32},{48,56},{56,48},{64,72... | collective-permute-start | bytes 774152 | tf_op jit(solution)/shard_map/ppermute | solution.py:321
  53.7 3.8 %collective-permute-start.20 = (bf16[16,8064]{1,0:T(8,128)(2,1)S(1)}, bf16[16,8064]{1,0:T(8,128)(2,1)S(1)}, u32[]{:S(2)}, u32[]{:S(2)}) collective-permute-start(bf16[16,8064]{1,0:T(8,128)(2,1)S(1)} %collective-permute-done.12.refs_9_), channel_id=1, source_target_pairs={{0,8},{8,0},{16,24},{24,16},{32,40},{40,32},{48,56},{56,48},{64,72... | collective-permute-start | bytes 774152 | tf_op jit(solution)/shard_map/ppermute | solution.py:321
  54.5 6.4 %collective-permute-start.19 = (bf16[16,8064]{1,0:T(8,128)(2,1)S(1)}, bf16[16,8064]{1,0:T(8,128)(2,1)S(1)}, u32[]{:S(2)}, u32[]{:S(2)}) collective-permute-start(bf16[16,8064]{1,0:T(8,128)(2,1)S(1)} %collective-permute-done.11.refs_8_), channel_id=1, source_target_pairs={{0,8},{8,0},{16,24},{24,16},{32,40},{40,32},{48,56},{56,48},{64,72... | collective-permute-start | bytes 774152 | tf_op jit(solution)/shard_map/ppermute | solution.py:321
  54.7 28.2 %collective-permute-start.8 = (bf16[16,8064]{1,0:T(8,128)(2,1)S(1)}, bf16[16,8064]{1,0:T(8,128)(2,1)S(1)}, u32[]{:S(2)}, u32[]{:S(2)}) collective-permute-start(bf16[16,8064]{1,0:T(8,128)(2,1)S(1)} %collective-permute-done.refs_2_), channel_id=1, source_target_pairs={{0,3},{1,0},{2,1},{3,2},{4,7},{5,4},{6,5},{7,6},{8,11},{9,8},{10,9... | collective-permute-start | bytes 774152 | tf_op jit(solution)/shard_map/ppermute | solution.py:315
  57.4 3.5 %copy-start.1 = (bf16[16,8064]{1,0:T(8,128)(2,1)}, bf16[16,8064]{1,0:T(8,128)(2,1)S(1)}, u32[]{:S(2)}) copy-start(bf16[16,8064]{1,0:T(8,128)(2,1)S(1)} %collective-permute-done.21.refs_18_) | copy-start | bytes 774148
  57.4 25.5 %collective-permute-start.7 = (bf16[16,8064]{1,0:T(8,128)(2,1)S(1)}, bf16[16,8064]{1,0:T(8,128)(2,1)S(1)}, u32[]{:S(2)}, u32[]{:S(2)}) collective-permute-start(bf16[16,8064]{1,0:T(8,128)(2,1)S(1)} %collective-permute-done.refs_2_), channel_id=1, source_target_pairs={{0,1},{1,2},{2,3},{3,0},{4,5},{5,6},{6,7},{7,4},{8,9},{9,10},{10,1... | collective-permute-start | bytes 774152 | tf_op jit(solution)/shard_map/ppermute | solution.py:315
  57.4 3.5 %copy-start.2 = (bf16[16,8064]{1,0:T(8,128)(2,1)}, bf16[16,8064]{1,0:T(8,128)(2,1)S(1)}, u32[]{:S(2)}) copy-start(bf16[16,8064]{1,0:T(8,128)(2,1)S(1)} %collective-permute-done.22.refs_19_) | copy-start | bytes 774148
  57.4 25.4 %collective-permute-start.9 = (bf16[16,8064]{1,0:T(8,128)(2,1)S(1)}, bf16[16,8064]{1,0:T(8,128)(2,1)S(1)}, u32[]{:S(2)}, u32[]{:S(2)}) collective-permute-start(bf16[16,8064]{1,0:T(8,128)(2,1)S(1)} %collective-permute-done.2.refs_0_), channel_id=1, source_target_pairs={{0,1},{1,2},{2,3},{3,0},{4,5},{5,6},{6,7},{7,4},{8,9},{9,10},{10,1... | collective-permute-start | bytes 774152 | tf_op jit(solution)/shard_map/ppermute | solution.py:315
  57.5 3.4 %copy-start.3 = (bf16[16,8064]{1,0:T(8,128)(2,1)}, bf16[16,8064]{1,0:T(8,128)(2,1)S(1)}, u32[]{:S(2)}) copy-start(bf16[16,8064]{1,0:T(8,128)(2,1)S(1)} %collective-permute-done.20.refs_17_) | copy-start | bytes 774148
  57.5 25.4 %collective-permute-start.10 = (bf16[16,8064]{1,0:T(8,128)(2,1)S(1)}, bf16[16,8064]{1,0:T(8,128)(2,1)S(1)}, u32[]{:S(2)}, u32[]{:S(2)}) collective-permute-start(bf16[16,8064]{1,0:T(8,128)(2,1)S(1)} %collective-permute-done.3.refs_3_), channel_id=1, source_target_pairs={{0,7},{1,4},{2,5},{3,6},{4,3},{5,0},{6,1},{7,2},{8,15},{9,12},{10,... | collective-permute-start | bytes 774152 | tf_op jit(solution)/shard_map/ppermute | solution.py:315
  60.9 0.7 copy-start.4
  61.6 0.9 copy-start
